TPU v7x, 256 devices: a whole 4x4x8 slice. The times are simulated.
256 devices in a mesh: gx: 8 (over z_hi, y), gy: 32 (over x, z_lo, core).
Axes of the slice: x: 4, y: 4, z: 8 (z_hi: 2, z_lo: 4; z = z_hi * 4 + z_lo), core: 2. Of those that a mesh axis runs over, the one named last changes fastest.
Arguments:
- disp: bfloat16 [40, 320, 26, 3], P('gx', 'gy'), may hold values from -6 to 6
- disp_prev: bfloat16 [40, 320, 26, 3], P('gx', 'gy'), may hold values from -6 to 6
- tangent: bfloat16 [40, 320, 4992], P('gx', 'gy'), may hold values from -6 to 6
- tangent_prev: bfloat16 [40, 320, 4992], P('gx', 'gy'), may hold values from -6 to 6
- lame_lambda: bfloat16 [8, 64, 5], P('gx', 'gy'), may hold values from 0.29882812 to 3
- lame_mu: bfloat16 [8, 64, 5], P('gx', 'gy'), may hold values from 0.29882812 to 3
- node_mass: float32 [40, 320, 26], P('gx', 'gy'), may hold values from 0.5 to 2
- force: bfloat16 [40, 320, 26, 3], P('gx', 'gy'), may hold values from -48 to 48
- cell_block: int32 [8, 64, 5], P('gx', 'gy'), may hold values from 0 to 63
- direction_block: int32 [64], replicated, may hold values from 0 to 63
- port_id: int32 [40, 320, 26], P('gx', 'gy'), may hold values from 0 to 64, as said below
- port_mode: bfloat16 [40, 320, 26, 3], P('gx', 'gy'), may hold values from -0.059814453 to 0.059814453
Outputs:
- disp_next: bfloat16 [40, 320, 26, 3], P('gx', 'gy')
- tangent_next: bfloat16 [40, 320, 4992], P('gx', 'gy')
- port_amp: float32 [64, 64], P('gy', 'gx')
Inputs may be any that keep to these rules, and one draw needn't show every extreme that they name: `port_id`: 64 marks a node outside every output section; the output sections are the last 40 node layers along the second dimension, where every node belongs to some port; within each node line along the first dimension the port numbers never fall.
All inputs are finite; a program needn't handle non-finite values.
Results may differ from a plain program's by a relative error of at most 0.0016.
Values may be sent and summed in bfloat16 or wider, within the bound.
No kernel may reach another device: no remote copies, remote signals or barrier semaphores. Data moves between devices by JAX's collectives and lax.ppermute only.
A program may use at most 192 MiB of HBM per device.

v0:
```python
import jax
import jax.numpy as jnp
import numpy as np
from jax import lax
from jax.sharding import PartitionSpec as P

PORTS = 64


GLL_POINTS = np.array(
    [-1.0, -0.765055323929465, -0.285231516480645, 0.285231516480645, 0.765055323929465, 1.0]
)
GLL_WEIGHTS = np.array(
    [
        1.0 / 15.0,
        0.378474956297847,
        0.554858377035486,
        0.554858377035486,
        0.378474956297847,
        1.0 / 15.0,
    ]
)
STEP_SQUARED = 0.03
HIGHEST = lax.Precision.HIGHEST
BACK_FORMS = ("pa,xpybzcn->xaybzcn", "pb,xaypzcn->xaybzcn", "pc,xaybzpn->xaybzcn")


def shifted(block, axis, distance):
    devices = range(lax.axis_size(axis))
    route = [(i - distance, i) for i in devices if i - distance in devices]
    return lax.ppermute(block, axis, route)


def shortened(shard):
    return jax.tree.map(lambda a: a.astype(jnp.bfloat16) if a.dtype == jnp.float32 else a, shard)


def derivative_table():
    identity = np.eye(6)
    differences = GLL_POINTS[:, None] - GLL_POINTS[None, :] + identity
    barycentric = 1.0 / np.prod(differences, axis=1)
    matrix = barycentric[None, :] / barycentric[:, None] / differences
    matrix = matrix * (1.0 - identity)
    matrix = matrix - identity * matrix.sum(axis=1)[:, None]
    return matrix


def point_weights():
    cubed = GLL_WEIGHTS[:, None, None] * GLL_WEIGHTS[None, :, None] * GLL_WEIGHTS[None, None, :]
    return jnp.asarray(cubed.reshape(1, 6, 1, 6, 1, 6, 1), jnp.float32)


def split_axis(values, axis_at):
    values = jnp.moveaxis(values, axis_at, 0)
    elem_count = (values.shape[0] - 1) // 5
    main_part = values[: 5 * elem_count].reshape((elem_count, 5) + values.shape[1:])
    tail_part = values[5::5][:, None]
    joined = jnp.concatenate([main_part, tail_part], axis=1)
    return jnp.moveaxis(joined, (0, 1), (axis_at, axis_at + 1))


def merge_axis(values, axis_at):
    values = jnp.moveaxis(values, (axis_at, axis_at + 1), (0, 1))
    elem_count = values.shape[0]
    rest_shape = values.shape[2:]
    main_part = values[:, :5].reshape((5 * elem_count,) + rest_shape)
    main_part = jnp.concatenate([main_part, jnp.zeros((1,) + rest_shape, values.dtype)], axis=0)
    tail_part = jnp.concatenate(
        [values[:, 5:6], jnp.zeros((elem_count, 4) + rest_shape, values.dtype)], axis=1
    )
    tail_part = tail_part.reshape((5 * elem_count,) + rest_shape)
    tail_part = jnp.concatenate([jnp.zeros((5,) + rest_shape, values.dtype), tail_part], axis=0)[
        : 5 * elem_count + 1
    ]
    return jnp.moveaxis(main_part + tail_part, 0, axis_at)


def to_cells(values):
    return split_axis(split_axis(split_axis(values, 0), 2), 4)


def to_nodes(values):
    return merge_axis(merge_axis(merge_axis(values, 4), 2), 0)


def gradients(cells, deriv):
    return [
        jnp.einsum("pa,xaybzcn->xpybzcn", deriv, cells, precision=HIGHEST),
        jnp.einsum("pb,xaybzcn->xaypzcn", deriv, cells, precision=HIGHEST),
        jnp.einsum("pc,xaybzcn->xaybzpn", deriv, cells, precision=HIGHEST),
    ]


def internal_forces(gradient_list, lam_cells, mu_cells, deriv, weights, block_width):

    def column_block(values, component):
        return values[..., component * block_width : (component + 1) * block_width]

    dilation = (
        column_block(gradient_list[0], 0)
        + column_block(gradient_list[1], 1)
        + column_block(gradient_list[2], 2)
    )
    summed = None
    for direction in range(3):
        pieces = []
        for component in range(3):
            stress = mu_cells * (
                column_block(gradient_list[direction], component)
                + column_block(gradient_list[component], direction)
            )
            if component == direction:
                stress = stress + lam_cells * dilation
            pieces.append(weights * stress)
        contribution = jnp.einsum(
            BACK_FORMS[direction], deriv, jnp.concatenate(pieces, axis=-1), precision=HIGHEST
        )
        summed = contribution if summed is None else summed + contribution
    return summed


def block_forces(primal_nodes, tangent_nodes, lam_cells, mu_cells, select):
    deriv = jnp.asarray(derivative_table(), jnp.float32)
    weights = point_weights()
    lam_wide = lam_cells.astype(jnp.float32)[:, None, :, None, :, None, None]
    mu_wide = mu_cells.astype(jnp.float32)[:, None, :, None, :, None, None]
    primal_grad = gradients(to_cells(primal_nodes).astype(jnp.float32), deriv)
    primal_force = internal_forces(primal_grad, lam_wide, mu_wide, deriv, weights, 1)
    sensitivity = internal_forces(primal_grad, 0.0, 1.0, deriv, weights, 1)
    tangent_grad = gradients(to_cells(tangent_nodes).astype(jnp.float32), deriv)
    directions = select.shape[-1]
    tangent_force = internal_forces(tangent_grad, lam_wide, mu_wide, deriv, weights, directions)
    source = (
        sensitivity[..., :, None] * select.astype(jnp.float32)[:, None, :, None, :, None, None, :]
    )
    tangent_force = tangent_force + source.reshape(tangent_force.shape)
    return (to_nodes(primal_force), to_nodes(tangent_force))


def per_device(
    disp,
    disp_prev,
    tangent,
    tangent_prev,
    lame_lambda,
    lame_mu,
    node_mass,
    force,
    cell_block,
    direction_block,
    port_id,
    port_mode,
):
    directions = direction_block.shape[0]
    node_shape = disp.shape[:3] + (3 * directions,)
    tangent = tangent.reshape(node_shape)
    tangent_prev = tangent_prev.reshape(node_shape)
    select = (cell_block[..., None] == direction_block[None, None, None, :]).astype(jnp.bfloat16)
    rim_ahead = shifted((disp[:1], tangent[:1]), "gx", -1)
    primal_x = jnp.concatenate([disp, rim_ahead[0]], axis=0)
    tangent_x = jnp.concatenate([tangent, rim_ahead[1]], axis=0)
    lam_x, mu_x, select_x = (lame_lambda, lame_mu, select)
    rim_ahead = shifted((primal_x[:, :1], tangent_x[:, :1]), "gy", -1)
    primal_xy = jnp.concatenate([primal_x, rim_ahead[0]], axis=1)
    tangent_xy = jnp.concatenate([tangent_x, rim_ahead[1]], axis=1)
    lam_xy, mu_xy, select_xy = (lam_x, mu_x, select_x)
    primal_force, tangent_force = block_forces(primal_xy, tangent_xy, lam_xy, mu_xy, select_xy)
    returned = (
        shifted(primal_force[:, -1:].astype(jnp.bfloat16), "gy", 1).astype(jnp.float32),
        shifted(tangent_force[:, -1:].astype(jnp.bfloat16), "gy", 1).astype(jnp.float32),
    )
    primal_force = jnp.concatenate(
        [primal_force[:, :1] + returned[0], primal_force[:, 1:-1]], axis=1
    )
    tangent_force = jnp.concatenate(
        [tangent_force[:, :1] + returned[1], tangent_force[:, 1:-1]], axis=1
    )
    returned = shifted((shortened(primal_force[-1:]), shortened(tangent_force[-1:])), "gx", 1)
    primal_force = jnp.concatenate([primal_force[:1] + returned[0], primal_force[1:-1]], axis=0)
    tangent_force = jnp.concatenate([tangent_force[:1] + returned[1], tangent_force[1:-1]], axis=0)
    mass = node_mass[..., None]
    disp_next = (
        2.0 * disp.astype(jnp.float32)
        - disp_prev.astype(jnp.float32)
        + STEP_SQUARED * (force.astype(jnp.float32) - primal_force) / mass
    ).astype(jnp.bfloat16)
    tangent_full = (
        2.0 * tangent.astype(jnp.float32)
        - tangent_prev.astype(jnp.float32)
        - STEP_SQUARED * tangent_force / mass
    )
    modes = port_mode.astype(jnp.float32)
    weighted = modes[..., 0:1] * tangent_full[..., 0:directions]
    weighted = weighted + modes[..., 1:2] * tangent_full[..., directions : 2 * directions]
    weighted = weighted + modes[..., 2:3] * tangent_full[..., 2 * directions : 3 * directions]
    flat_weighted = weighted.reshape(-1, directions)
    onehot = (port_id.reshape(-1)[:, None] == jnp.arange(PORTS, dtype=jnp.int32)[None, :]).astype(
        jnp.float32
    )
    amplitude = jnp.einsum("np,nj->pj", onehot, flat_weighted, precision=HIGHEST)
    total_amp = lax.psum(amplitude, ("gx", "gy"))
    row_count = PORTS // lax.axis_size("gy")
    col_count = directions // lax.axis_size("gx")
    port_amp = lax.dynamic_slice(
        total_amp,
        (lax.axis_index("gy") * row_count, lax.axis_index("gx") * col_count),
        (row_count, col_count),
    )
    tangent_next = tangent_full.astype(jnp.bfloat16).reshape(disp.shape[0], disp.shape[1], -1)
    return (disp_next, tangent_next, port_amp)


def solution(mesh):
    return jax.shard_map(
        per_device,
        mesh=mesh,
        in_specs=(
            P("gx", "gy", None, None),
            P("gx", "gy", None, None),
            P("gx", "gy", None),
            P("gx", "gy", None),
            P("gx", "gy", None),
            P("gx", "gy", None),
            P("gx", "gy", None),
            P("gx", "gy", None, None),
            P("gx", "gy", None),
            P(),
            P("gx", "gy", None),
            P("gx", "gy", None, None),
        ),
        out_specs=(P("gx", "gy", None, None), P("gx", "gy", None), P("gy", "gx")),
        check_vma=False,
    )
```

profile of v0, /device:TPU:1, one launch (start us, length us, event | category | flops | bytes accessed | tf_op | source)
XLA Modules:
  0.0 250.8 jit_solution(1618729902100033152)
XLA Ops:
  12.1 5.1 %collective-permute-start.1 = (bf16[6,1,26,3]{2,0,3,1:T(8,128)(2,1)}, bf16[6,1,26,3]{2,0,3,1:T(8,128)(2,1)}, u32[]{:S(2)}, u32[]{:S(2)}) collective-permute-start(bf16[6,1,26,3]{2,0,3,1:T(8,128)(2,1)} %pad_maximum_fusion.4), channel_id=1, source_target_pairs={{1,0},{2,1},{3,2},{4,3},{5,4},{6,5},{7,6},{8,7},{9,8},{10,9},{11,1... | collective-permute-start | bytes 2816 | tf_op jit(solution)/shard_map/ppermute | solution.py:31
  19.8 1.9 reshape.216
  25.6 1.8 div.24
  29.2 3.7 %slice.271 = bf16[5,1,6,2,6,3]{0,3,5,2,1,4:T(2,128)(2,1)S(1)} slice(bf16[26,1,6,2,6,3]{0,3,5,2,1,4:T(2,128)(2,1)S(1)} %maximum_bitcast_fusion.22), slice={[5:26:5], [0:1:1], [0:6:1], [0:2:1], [0:6:1], [0:3:1]} | slice | bytes 4320 | tf_op jit(solution)/shard_map/slice | solution.py:57
  33.3 1.7 copy.218
  40.2 3.7 %copy.221 = f32[6,2,5,6,3,6]{0,3,4,2,5,1:T(8,128)} copy(f32[6,2,5,6,3,6]{5,3,4,2,1,0:T(8,128)} %fusion.79) | data formatting | bytes 51840 | tf_op jit(solution)/shard_map/pb,xaybzcn->xaypzcn/dot_general | solution.py:89
  43.8 2.2 broadcast_multiply_fusion.2
  46.0 2.3 add_multiply_fusion.4
  48.6 1.7 copy.224
  53.3 2.1 convolution_bitcast_fusion.3
  57.1 1.8 copy.229
  62.0 1.7 copy.251
  67.5 3.3 %collective-permute-start.2 = (bf16[6,1,26,3]{2,3,0,1:T(4,128)(2,1)}, bf16[6,1,26,3]{2,3,0,1:T(4,128)(2,1)}, u32[]{:S(2)}, u32[]{:S(2)}) collective-permute-start(bf16[6,1,26,3]{2,3,0,1:T(4,128)(2,1)} %slice.550), channel_id=1, source_target_pairs={{0,1},{1,2},{2,3},{3,4},{4,5},{5,6},{6,7},{7,8},{8,9},{9,10},{10,1... | collective-permute-start | bytes 2816 | tf_op jit(solution)/shard_map/ppermute | solution.py:31
  70.8 1.8 convolution_bitcast_fusion.1
  73.9 2.8 %copy.255 = f32[6,2,6,5,6,3]{5,1,4,3,2,0:T(2,128)S(1)} copy(f32[6,2,6,5,6,3]{0,4,5,3,2,1:T(8,128)S(1)} %fusion.35) | data formatting | bytes 51840 | tf_op jit(solution)/shard_map/mul | solution.py:134
  76.6 4.0 %mul.210 = f32[6,2,6,5,6,3,64]{6,5,1,4,3,2,0:T(4,128)} broadcast(f32[6,2,6,5,6,3]{5,1,4,3,2,0:T(2,128)S(1)} %copy.255), dimensions={0,1,2,3,4,5} | broadcast | bytes 1684800 | tf_op jit(solution)/shard_map/mul | solution.py:134
  80.7 5.4 %mul.211 = f32[1,6,2,6,5,6,192]{6,2,5,4,3,1,0:T(2,128)S(1)} reshape(f32[6,2,6,5,6,3,64]{6,5,1,4,3,2,0:T(4,128)} %mul.210) | data formatting | bytes 3317760 | tf_op jit(solution)/shard_map/mul | solution.py:134
  86.9 3.5 %collective-permute-start.3 = (bf16[1,10,26,3]{2,3,0,1:T(4,128)(2,1)S(1)}, bf16[1,10,26,3]{2,3,0,1:T(4,128)(2,1)S(1)}, u32[]{:S(2)}, u32[]{:S(2)}) collective-permute-start(bf16[1,10,26,3]{2,3,0,1:T(4,128)(2,1)S(1)} %fusion.72), channel_id=1, source_target_pairs={{0,32},{32,64},{64,96},{96,128},{128,160},{160,192},{192,224},{1,3... | collective-permute-start | bytes 4688 | tf_op jit(solution)/shard_map/ppermute | solution.py:31
  91.2 3.7 %collective-permute-start.5 = (bf16[6,1,26,192]{3,0,2,1:T(8,128)(2,1)S(1)}, bf16[6,1,26,192]{3,0,2,1:T(8,128)(2,1)S(1)}, u32[]{:S(2)}, u32[]{:S(2)}) collective-permute-start(bf16[6,1,26,192]{3,0,2,1:T(8,128)(2,1)S(1)} %pad_maximum_fusion.2), channel_id=1, source_target_pairs={{1,0},{2,1},{3,2},{4,3},{5,4},{6,5},{7,6},{8,7},{9,8},{10,9},{11,1... | collective-permute-start | bytes 179720 | tf_op jit(solution)/shard_map/ppermute | solution.py:31
  94.9 2.3 collective-permute-done.5
  109.2 1.8 add_multiply_fusion.2
  113.3 3.2 %fusion.7 = f32[6,2,6,5,192,6]{4,5,3,2,1,0:T(8,128)S(1)} fusion(f32[6,6,1,1,1,1]{1,0,5,4,3,2:T(8,128)S(1)} %copy-done.14, f32[6,2,6,5,6,192]{5,0,4,3,2,1:T(8,128)S(1)} %get-tuple-element.33), kind=kOutput, calls=%fused_computation.14 | convolution fusion | flops 29859840 | bytes 3317904 | tf_op jit(solution)/shard_map/pc,xaybzpn->xaybzcn/dot_general | solution.py:115
  116.5 3.9 %fusion.9 = f32[6,2,5,6,192,6]{4,5,3,2,1,0:T(8,128)S(1)} fusion(f32[6,6,1,1,1,1]{1,0,5,4,3,2:T(8,128)S(1)} %copy-done.14, f32[6,2,6,5,6,192]{5,0,4,3,2,1:T(8,128)S(1)} %get-tuple-element.32), kind=kOutput, calls=%fused_computation.16 | convolution fusion | flops 29859840 | bytes 3317904 | tf_op jit(solution)/shard_map/pb,xaypzcn->xaybzcn/dot_general | solution.py:115
  120.4 6.3 %fusion.6 = f32[5,6,1,6,2,6,192]{6,3,1,0,5,4,2:T(8,128)S(1)} fusion(f32[1,6,2,6,5,6,192]{6,2,5,4,3,1,0:T(2,128)S(1)} %mul.211, f32[6,2,6,5,192,6]{4,5,3,2,1,0:T(8,128)S(1)} %fusion.7, f32[6,2,5,6,192,6]{4,5,3,2,1,0:T(8,128)S(1)} %fusion.9, f32[6,6,1,1,1,1]{1,0,5,4,3,2:T(8,128)S(1)} %copy-done.14, f32[1,6,2,6,5,6,64]{6,1,5,4,3,2,0:T(8,128)S(1)} %get-tuple-element.20, ...), kind=kOutput, calls=%fused_computation.11 | convolution fusion | flops 32348160 | bytes 8302224 | tf_op jit(solution)/shard_map/pa,xpybzcn->xaybzcn/dot_general | solution.py:115
  131.6 1.9 collective-permute-start.6
  135.8 4.3 %collective-permute-start.7 = (bf16[1,10,26,192]{3,2,1,0:T(8,128)(2,1)}, bf16[1,10,26,192]{3,2,1,0:T(8,128)(2,1)}, u32[]{:S(2)}, u32[]{:S(2)}) collective-permute-start(bf16[1,10,26,192]{3,2,1,0:T(8,128)(2,1)} %fusion.59), channel_id=1, source_target_pairs={{0,32},{32,64},{64,96},{96,128},{128,160},{160,192},{192,224},{1,3... | collective-permute-start | bytes 299528 | tf_op jit(solution)/shard_map/ppermute | solution.py:31
  141.9 2.5 copy.284
  144.4 1.7 fusion.61
  147.4 2.3 fusion.17
  151.7 2.0 fusion.54
  153.8 92.9 %psum.7 = f32[64,64]{1,0:T(8,128)S(1)} all-reduce(f32[64,64]{1,0:T(8,128)S(1)} %fusion.54), channel_id=1, replica_groups=mesh['gx'=8,'gy'=32] {'gx','gy'}, use_global_device_ids=true, to_apply=%region_0.0 | all-reduce | flops 4096 | bytes 32768 | tf_op jit(solution)/shard_map/psum | solution.py:201
  246.7 2.3 fusion.20
  (188 shorter events, 67.2 us)
Async XLA Ops:
  0.6 8.6 %copy-start.28 = (bf16[5,10,26,3]{2,3,1,0:T(4,128)(2,1)S(1)}, bf16[5,10,26,3]{2,3,1,0:T(4,128)(2,1)}, u32[]{:S(2)}) copy-start(bf16[5,10,26,3]{2,3,1,0:T(4,128)(2,1)} %param.25) | copy-start | bytes 23404
  1.6 8.3 %copy-start.33 = (s32[64]{0:T(128)S(1)}, s32[64]{0:T(128)}, u32[]{:S(2)}) copy-start(s32[64]{0:T(128)} %param.23) | copy-start | bytes 772
  1.6 8.4 %copy-start.34 = (bf16[1,2,5]{2,1,0:T(2,128)(2,1)S(1)}, bf16[1,2,5]{2,1,0:T(2,128)(2,1)}, u32[]{:S(2)}) copy-start(bf16[1,2,5]{2,1,0:T(2,128)(2,1)} %param.18) | copy-start | bytes 64
  1.6 8.9 %copy-start.3 = (bf16[5,10,4992]{2,1,0:T(8,128)(2,1)S(1)}, bf16[5,10,4992]{2,1,0:T(8,128)(2,1)}, u32[]{:S(2)}) copy-start(bf16[5,10,4992]{2,1,0:T(8,128)(2,1)} %param.16) | copy-start | bytes 1497604
  2.5 87.9 %collective-permute-start.4 = (bf16[1,10,26,192]{3,0,2,1:T(2,128)(2,1)}, bf16[1,10,26,192]{3,0,2,1:T(2,128)(2,1)}, u32[]{:S(2)}, u32[]{:S(2)}) collective-permute-start(bf16[1,10,26,192]{3,0,2,1:T(2,128)(2,1)} %slice.335), channel_id=1, source_target_pairs={{32,0},{64,32},{96,64},{128,96},{160,128},{192,160},{224,192},{33,... | collective-permute-start | bytes 299528 | tf_op jit(solution)/shard_map/ppermute | solution.py:31
  4.6 6.8 %collective-permute-start = (bf16[1,10,26,3]{2,0,3,1:T(2,128)(2,1)S(1)}, bf16[1,10,26,3]{2,0,3,1:T(2,128)(2,1)S(1)}, u32[]{:S(2)}, u32[]{:S(2)}) collective-permute-start(bf16[1,10,26,3]{2,0,3,1:T(2,128)(2,1)S(1)} %slice.336), channel_id=1, source_target_pairs={{32,0},{64,32},{96,64},{128,96},{160,128},{192,160},{224,192},{33,... | collective-permute-start | bytes 4688 | tf_op jit(solution)/shard_map/ppermute | solution.py:31
  11.4 10.3 %copy-start.1 = (bf16[5,10,26,192]{3,2,1,0:T(8,128)(2,1)}, bf16[5,10,26,192]{3,2,1,0:T(8,128)(2,1)S(1)}, u32[]{:S(2)}) copy-start(bf16[5,10,26,192]{3,2,1,0:T(8,128)(2,1)S(1)} %reshape.189) | copy-start | bytes 1497604
  11.4 5.8 %copy-start.23 = (bf16[1,10,26,3]{2,0,3,1:T(2,128)(2,1)}, bf16[1,10,26,3]{2,0,3,1:T(2,128)(2,1)S(1)}, u32[]{:S(2)}) copy-start(bf16[1,10,26,3]{2,0,3,1:T(2,128)(2,1)S(1)} %collective-permute-done) | copy-start | bytes 4684
  12.1 15.3 %collective-permute-start.1 = (bf16[6,1,26,3]{2,0,3,1:T(8,128)(2,1)}, bf16[6,1,26,3]{2,0,3,1:T(8,128)(2,1)}, u32[]{:S(2)}, u32[]{:S(2)}) collective-permute-start(bf16[6,1,26,3]{2,0,3,1:T(8,128)(2,1)} %pad_maximum_fusion.4), channel_id=1, source_target_pairs={{1,0},{2,1},{3,2},{4,3},{5,4},{6,5},{7,6},{8,7},{9,8},{10,9},{11,1... | collective-permute-start | bytes 2816 | tf_op jit(solution)/shard_map/ppermute | solution.py:31
  29.0 8.5 %copy-start.14 = (f32[6,6,1,1,1,1]{1,0,5,4,3,2:T(8,128)S(1)}, f32[6,6,1,1,1,1]{1,0,5,4,3,2:T(8,128)}, u32[]{:S(2)}) copy-start(f32[6,6,1,1,1,1]{1,0,5,4,3,2:T(8,128)} %constant.97) | copy-start | bytes 436
  38.0 5.9 %copy-start.16 = (f32[6,6,6]{0,2,1:T(8,128)S(1)}, f32[6,6,6]{0,2,1:T(8,128)}, u32[]{:S(2)}) copy-start(f32[6,6,6]{0,2,1:T(8,128)} %constant.96) | copy-start | bytes 2596
  38.0 5.9 %copy-start.30 = (f32[2,5]{1,0:T(2,128)S(1)}, f32[2,5]{1,0:T(2,128)}, u32[]{:S(2)}) copy-start(f32[2,5]{1,0:T(2,128)} %bitcast_convert_fusion.1) | copy-start | bytes 124
  46.0 2.5 %copy-start.6 = (f32[1,6,2,6,5,6,1]{1,5,6,4,3,2,0:T(8,128)}, f32[1,6,2,6,5,6,1]{1,5,6,4,3,2,0:T(8,128)S(1)}, u32[]{:S(2)}) copy-start(f32[1,6,2,6,5,6,1]{1,5,6,4,3,2,0:T(8,128)S(1)} %get-tuple-element.31) | copy-start | bytes 25924
  46.0 2.5 %copy-start.8 = (f32[1,6,2,6,5,6,1]{1,5,6,4,3,2,0:T(8,128)}, f32[1,6,2,6,5,6,1]{1,5,6,4,3,2,0:T(8,128)S(1)}, u32[]{:S(2)}) copy-start(f32[1,6,2,6,5,6,1]{1,5,6,4,3,2,0:T(8,128)S(1)} %get-tuple-element.25) | copy-start | bytes 25924
  46.0 2.6 %copy-start.11 = (f32[1,6,2,6,5,6,1]{1,5,6,4,3,2,0:T(8,128)}, f32[1,6,2,6,5,6,1]{1,5,6,4,3,2,0:T(8,128)S(1)}, u32[]{:S(2)}) copy-start(f32[1,6,2,6,5,6,1]{1,5,6,4,3,2,0:T(8,128)S(1)} %get-tuple-element.29) | copy-start | bytes 25924
  63.7 7.0 %copy-start.5 = (f32[1,6,2,6,5,6,1]{1,5,6,4,3,2,0:T(8,128)S(1)}, f32[1,6,2,6,5,6,1]{1,5,6,4,3,2,0:T(8,128)}, u32[]{:S(2)}) copy-start(f32[1,6,2,6,5,6,1]{1,5,6,4,3,2,0:T(8,128)} %get-tuple-element.30) | copy-start | bytes 25924
  63.7 7.0 %copy-start.7 = (f32[1,6,2,6,5,6,1]{1,5,6,4,3,2,0:T(8,128)S(1)}, f32[1,6,2,6,5,6,1]{1,5,6,4,3,2,0:T(8,128)}, u32[]{:S(2)}) copy-start(f32[1,6,2,6,5,6,1]{1,5,6,4,3,2,0:T(8,128)} %copy-done.6) | copy-start | bytes 25924
  66.7 5.9 %copy-start.12 = (f32[1,6,2,6,5,6,1]{1,5,6,4,3,2,0:T(8,128)S(1)}, f32[1,6,2,6,5,6,1]{1,5,6,4,3,2,0:T(8,128)}, u32[]{:S(2)}) copy-start(f32[1,6,2,6,5,6,1]{1,5,6,4,3,2,0:T(8,128)} %get-tuple-element.39) | copy-start | bytes 25924
  66.8 7.0 %copy-start.15 = (f32[6,11,26,3]{2,3,0,1:T(4,128)}, f32[6,11,26,3]{2,3,0,1:T(4,128)S(1)}, u32[]{:S(2)}) copy-start(f32[6,11,26,3]{2,3,0,1:T(4,128)S(1)} %fusion.62) | copy-start | bytes 61780
  67.5 18.6 %collective-permute-start.2 = (bf16[6,1,26,3]{2,3,0,1:T(4,128)(2,1)}, bf16[6,1,26,3]{2,3,0,1:T(4,128)(2,1)}, u32[]{:S(2)}, u32[]{:S(2)}) collective-permute-start(bf16[6,1,26,3]{2,3,0,1:T(4,128)(2,1)} %slice.550), channel_id=1, source_target_pairs={{0,1},{1,2},{2,3},{3,4},{4,5},{5,6},{6,7},{7,8},{8,9},{9,10},{10,1... | collective-permute-start | bytes 2816 | tf_op jit(solution)/shard_map/ppermute | solution.py:31
  86.9 8.0 %collective-permute-start.3 = (bf16[1,10,26,3]{2,3,0,1:T(4,128)(2,1)S(1)}, bf16[1,10,26,3]{2,3,0,1:T(4,128)(2,1)S(1)}, u32[]{:S(2)}, u32[]{:S(2)}) collective-permute-start(bf16[1,10,26,3]{2,3,0,1:T(4,128)(2,1)S(1)} %fusion.72), channel_id=1, source_target_pairs={{0,32},{32,64},{64,96},{96,128},{128,160},{160,192},{192,224},{1,3... | collective-permute-start | bytes 4688 | tf_op jit(solution)/shard_map/ppermute | solution.py:31
  91.2 6.0 %collective-permute-start.5 = (bf16[6,1,26,192]{3,0,2,1:T(8,128)(2,1)S(1)}, bf16[6,1,26,192]{3,0,2,1:T(8,128)(2,1)S(1)}, u32[]{:S(2)}, u32[]{:S(2)}) collective-permute-start(bf16[6,1,26,192]{3,0,2,1:T(8,128)(2,1)S(1)} %pad_maximum_fusion.2), channel_id=1, source_target_pairs={{1,0},{2,1},{3,2},{4,3},{5,4},{6,5},{7,6},{8,7},{9,8},{10,9},{11,1... | collective-permute-start | bytes 179720 | tf_op jit(solution)/shard_map/ppermute | solution.py:31
  116.4 3.9 %copy-start.25 = (f32[2,5,192]{2,1,0:T(8,128)S(1)}, f32[2,5,192]{2,1,0:T(8,128)}, u32[]{:S(2)}) copy-start(f32[2,5,192]{2,1,0:T(8,128)} %copy.257) | copy-start | bytes 23044
  131.2 2.3 copy-start.18
  131.6 3.5 %collective-permute-start.6 = (bf16[6,1,26,192]{3,2,1,0:T(8,128)(2,1)S(1)}, bf16[6,1,26,192]{3,2,1,0:T(8,128)(2,1)S(1)}, u32[]{:S(2)}, u32[]{:S(2)}) collective-permute-start(bf16[6,1,26,192]{3,2,1,0:T(8,128)(2,1)S(1)} %slice.549), channel_id=1, source_target_pairs={{0,1},{1,2},{2,3},{3,4},{4,5},{5,6},{6,7},{7,8},{8,9},{9,10},{10,1... | collective-permute-start | bytes 179720 | tf_op jit(solution)/shard_map/ppermute | solution.py:31
  135.8 8.6 %collective-permute-start.7 = (bf16[1,10,26,192]{3,2,1,0:T(8,128)(2,1)}, bf16[1,10,26,192]{3,2,1,0:T(8,128)(2,1)}, u32[]{:S(2)}, u32[]{:S(2)}) collective-permute-start(bf16[1,10,26,192]{3,2,1,0:T(8,128)(2,1)} %fusion.59), channel_id=1, source_target_pairs={{0,32},{32,64},{64,96},{96,128},{128,160},{160,192},{192,224},{1,3... | collective-permute-start | bytes 299528 | tf_op jit(solution)/shard_map/ppermute | solution.py:31
  144.4 2.9 %copy-start.17 = (f32[5,10,26]{2,1,0:T(8,128)S(1)}, f32[5,10,26]{2,1,0:T(8,128)}, u32[]{:S(2)}) copy-start(f32[5,10,26]{2,1,0:T(8,128)} %param.20) | copy-start | bytes 15604
  147.4 2.3 copy-start.20
  147.4 2.3 copy-start.21
  147.4 2.3 copy-start.22
  149.8 96.9 %copy-start.4 = (bf16[5,10,4992]{2,1,0:T(8,128)(2,1)S(1)}, bf16[5,10,4992]{2,1,0:T(8,128)(2,1)}, u32[]{:S(2)}) copy-start(bf16[5,10,4992]{2,1,0:T(8,128)(2,1)} %param.16) | copy-start | bytes 1497604
  150.8 95.9 %copy-start.2 = (f32[5,10,4992]{2,1,0:T(8,128)S(1)}, f32[5,10,4992]{2,1,0:T(8,128)}, u32[]{:S(2)}) copy-start(f32[5,10,4992]{2,1,0:T(8,128)} %div.24) | copy-start | bytes 2995204
  (12 other events, 23.1 us)
where the time goes:
time: 256 us; the launch traced here: 251 us
  blocking collectives  92.9 us (36%)
  local copies, waits for them, and re-layouts  65.8 us (26%)
  other arithmetic  31.4 us (12%)
  matrix products  31.4 us (12%)
  starting transfers between devices  24.4 us (10%)
  waiting for transfers between devices  2.98 us (1%)
    psum x1, blocking collectives, per_device(): total_amp = lax.psum(amplitude, ('gx', 'gy'))  92.9 us
    ppermute x8, starting transfers between devices, shifted(): return lax.ppermute(block, axis, route)  24.4 us
    dot_general x9, matrix products, internal_forces(): jnp.einsum(BACK_FORMS[direction], deriv, jnp.concatenate(pieces, axis=-1)...  22.3 us
    mul x6, local copies, waits for them, and re-layouts, block_forces(): sensitivity[..., :, None]  14.2 us
    mul x4, other arithmetic, internal_forces(): pieces.append(weights * stress)  6.94 us
    unnamed x80, local copies, waits for them, and re-layouts  6.11 us
    concatenate x3, local copies, waits for them, and re-layouts, per_device(): jnp.concatenate([tangent_force[:1] + returned[1], tangent_force[1:-1]], a...  5.35 us
  transfers between devices with their start and end apart: 8, of which 2 were waited for; matrix products, arithmetic and copies ran while one was open for 31% of the time, Pallas kernels for 0%

commit v1 on v0

v1 whole, which is shorter than its diff:
```python
import functools

import jax
import jax.numpy as jnp
import ml_dtypes
import numpy as np
from jax import lax
from jax.experimental import pallas as pl
from jax.experimental.pallas import tpu as pltpu
from jax.sharding import PartitionSpec as P

PORTS = 64
GLL_POINTS = np.array(
    [-1.0, -0.765055323929465, -0.285231516480645, 0.285231516480645, 0.765055323929465, 1.0]
)
GLL_WEIGHTS = np.array(
    [
        1.0 / 15.0,
        0.378474956297847,
        0.554858377035486,
        0.554858377035486,
        0.378474956297847,
        1.0 / 15.0,
    ]
)
STEP_SQUARED = 0.03
HIGHEST = lax.Precision.HIGHEST
F32 = jnp.float32
BF16 = jnp.bfloat16

NX, NY, NZ = 5, 10, 26
COLS = 4992
SMALL = 384
WIDE = COLS + SMALL
BACK = COLS + 128
ROWS = 96
PTS = 72
VMEM_LIMIT = 48 * 1024 * 1024


def derivative_table():
    identity = np.eye(6)
    differences = GLL_POINTS[:, None] - GLL_POINTS[None, :] + identity
    barycentric = 1.0 / np.prod(differences, axis=1)
    matrix = barycentric[None, :] / barycentric[:, None] / differences
    matrix = matrix * (1.0 - identity)
    matrix = matrix - identity * matrix.sum(axis=1)[:, None]
    return matrix


def halves(matrix):
    matrix = matrix.astype(np.float32)
    high = matrix.astype(ml_dtypes.bfloat16)
    low = (matrix - high.astype(np.float32)).astype(ml_dtypes.bfloat16)
    return high, low


SYM = {(0, 0): 0, (1, 1): 1, (2, 2): 2, (0, 1): 3, (0, 2): 4, (1, 2): 5}


def sym_of(c, d):
    return SYM[(min(c, d), max(c, d))]


@functools.cache
def tables():
    deriv = derivative_table()
    w = GLL_WEIGHTS
    fx = np.zeros((PTS, ROWS))
    fy = np.zeros((PTS, ROWS))
    fv = np.zeros((PTS, ROWS))
    wxy = np.zeros(PTS)
    for e in range(2):
        for px in range(6):
            for py in range(6):
                r = e * 36 + px * 6 + py
                wxy[r] = w[px] * w[py]
                fv[r, 16 * px + 5 * e + py] = 1.0
                for a in range(6):
                    fx[r, 16 * a + 5 * e + py] += deriv[px, a]
                    fy[r, 16 * px + 5 * e + a] += deriv[py, a]
    forward = np.concatenate([fx, fy, fv], axis=0)
    f_high, f_low = halves(forward)
    forward2 = np.concatenate([f_high, f_low], axis=1)
    backward = np.concatenate([(m * wxy[:, None]).T for m in (fx, fy, fv)], axis=1)
    b_high, b_low = halves(backward)
    backward2 = np.concatenate([b_high, b_low], axis=0)

    coef = np.zeros((2, 39, 128))
    for n in range(3):
        for m in range(3):
            a = np.repeat([deriv[2 * n, 2 * m], deriv[2 * n + 1, 2 * m + 1]], 64)
            b = np.repeat([deriv[2 * n, 2 * m + 1], deriv[2 * n + 1, 2 * m]], 64)
            at = np.repeat([deriv[2 * m, 2 * n], deriv[2 * m + 1, 2 * n + 1]], 64)
            bt = np.repeat([deriv[2 * m + 1, 2 * n], deriv[2 * m, 2 * n + 1]], 64)
            for q, v in enumerate((a, b, at, bt)):
                coef[0, q * 9 + n * 3 + m] = v
                coef[1, q * 9 + n * 3 + m] = np.roll(v, 64)
    for m in range(3):
        v = np.repeat([w[2 * m], w[2 * m + 1]], 64)
        coef[0, 36 + m] = v
        coef[1, 36 + m] = np.roll(v, 64)
    coef = np.repeat(coef.reshape(78, 1, 128), 8, axis=1).astype(np.float32)

    to_sym = np.zeros((3, 128, 512))
    from_sym = np.zeros((256, 384))
    for i in range(5):
        for kp in range(6):
            base = i * 36 + kp * 6
            point_column = (5 * i + kp) * 3
            for c in range(3):
                for d in range(3):
                    s = base + sym_of(c, d)
                    share = 2.0 if c == d else 1.0
                    targets = [(s, share)]
                    if c == d:
                        targets += [(256 + base + q, 1.0) for q in range(3)]
                    for column, factor in targets:
                        if d < 2:
                            to_sym[d, point_column + c, column] += factor
                        else:
                            for k in range(6):
                                to_sym[2, (5 * i + k) * 3 + c, column] += factor * deriv[kp, k]
                    if d < 2:
                        from_sym[s, d * 128 + point_column + c] += w[kp]
                    else:
                        for k in range(6):
                            from_sym[s, 256 + (5 * i + k) * 3 + c] += w[kp] * deriv[kp, k]
    spread = np.zeros((128, 128))
    for piece in range(3):
        for k in range(NZ):
            for c in range(3):
                spread[piece * NZ + k, k * 3 + c] = 1.0
    return dict(
        forward=forward2,
        backward=backward2,
        back32=backward.astype(np.float32),
        coef=coef,
        to_sym=to_sym.reshape(384, 512).astype(np.float32),
        from_sym=from_sym.astype(np.float32),
        spread=spread.astype(ml_dtypes.bfloat16),
    )


def pack_kernel(t_ref, s_ref, x_ref, y_ref, c_ref, wide_ref):
    x_ref[:, :COLS] = t_ref[0]
    x_ref[:, COLS:] = s_ref[0]
    for x in range(NX):
        wide_ref[x : x + 1, :COLS] = t_ref[x, 0:1, :].astype(F32)
        wide_ref[x : x + 1, COLS:] = s_ref[x, 0:1, :].astype(F32)
    y_ref[...] = wide_ref[0:NX, :].astype(BF16)
    c_ref[...] = wide_ref[0:1, :].astype(BF16)


def fdot(a, b):
    return jnp.dot(a, b, preferred_element_type=F32, precision=HIGHEST)


def bdot(a, b):
    return jnp.dot(a, b, preferred_element_type=F32)


def split(value):
    high = value.astype(BF16)
    return high, (value - high.astype(F32)).astype(BF16)


def main_kernel(
    par_ref,
    cell_ref,
    t_ref,
    tp_ref,
    s_ref,
    loc_ref,
    hx_ref,
    hy_ref,
    hc_ref,
    lanes_ref,
    dirs_ref,
    fwd_ref,
    bwd_ref,
    back32_ref,
    coef_ref,
    to_sym_ref,
    from_sym_ref,
    spread_ref,
    part_ref,
    dpart_ref,
    rx_ref,
    ry_ref,
    rc_ref,
    amp_ref,
    wide,
    u2,
    grad,
    stress,
    force,
    sym,
    rowpar,
    edge,
):
    for x in range(NX):
        wide[16 * x + 8 : 16 * x + 16, :] = jnp.zeros((8, WIDE), F32)
        wide[16 * x : 16 * x + NY, :COLS] = t_ref[x].astype(F32)
        wide[16 * x : 16 * x + NY, COLS:] = s_ref[x].astype(F32)
        wide[16 * x + NY : 16 * x + NY + 1, :] = hy_ref[x : x + 1, :].astype(F32)
    wide[88:96, :] = jnp.zeros((8, WIDE), F32)
    wide[80 : 80 + NY, :] = hx_ref[...].astype(F32)
    wide[80 + NY : 81 + NY, :] = hc_ref[...].astype(F32)
    u2[0:ROWS, :] = wide[...].astype(BF16)
    u2[ROWS : 2 * ROWS, :] = u2[0:ROWS, :]

    fwd = fwd_ref[...]
    bwd = bwd_ref[...]
    low_half = lax.broadcasted_iota(jnp.int32, (8, 128), 1) < 64
    low_rows = lax.broadcasted_iota(jnp.int32, (ROWS, 128), 1) < 64
    first_el = lax.broadcasted_iota(jnp.int32, (PTS, 128), 0) < 36
    first_el2 = lax.broadcasted_iota(jnp.int32, (PTS, 256), 0) < 36

    pg = bdot(fwd, u2[:, COLS : COLS + 128])
    both = fdot(pg[0:PTS], to_sym_ref[0:128, :])
    both = both + fdot(pg[PTS : 2 * PTS], to_sym_ref[128:256, :])
    both = both + fdot(pg[2 * PTS : 3 * PTS], to_sym_ref[256:384, :])
    sym[...] = both[:, 0:256]
    lam_l = jnp.where(first_el2, lanes_ref[0:1, :], lanes_ref[1:2, :])
    mu_l = jnp.where(first_el2, lanes_ref[2:3, :], lanes_ref[3:4, :])
    primal_stress = lam_l * both[:, 256:512] + mu_l * both[:, 0:256]
    spread_out = fdot(primal_stress, from_sym_ref[...])
    primal_force = (
        fdot(back32_ref[:, 0:PTS], spread_out[:, 0:128])
        + fdot(back32_ref[:, PTS : 2 * PTS], spread_out[:, 128:256])
        + fdot(back32_ref[:, 2 * PTS : 3 * PTS], spread_out[:, 256:384])
    )

    force[...] = jnp.zeros((ROWS, COLS), F32)

    for i in range(5):
        odd = i % 2
        start = 960 * i - 64 * odd
        count = 9 + odd
        grad[:, 0 : count * 128] = bdot(fwd, u2[:, start : start + count * 128])
        rowpar[0] = jnp.where(first_el, par_ref[0, i], par_ref[0, 5 + i])
        rowpar[1] = jnp.where(first_el, par_ref[1, i], par_ref[1, 5 + i])
        cell = jnp.where(first_el, cell_ref[0, i], cell_ref[0, 5 + i])
        rowpar[2] = jnp.where(cell == dirs_ref[...], 1.0, 0.0)

        def rows_step(rc, carry, i=i, odd=odd):
            row = pl.multiple_of(rc * 8, 8)

            def tile(kind, index):
                at = pl.multiple_of(kind * PTS + rc * 8, 8)
                return grad[pl.ds(at, 8), index * 128 : (index + 1) * 128]

            def coef(index):
                return coef_ref[odd * 39 + index]

            values = []
            for kind in range(3):
                of_c = [[], [], []]
                for m in range(3):
                    if odd:
                        t0, t1, t2, t3 = (tile(kind, 3 * m + q) for q in range(4))
                        of_c[0].append(jnp.where(low_half, t2, t0))
                        of_c[1].append(pltpu.roll(jnp.where(low_half, t1, t2), 64, 1))
                        of_c[2].append(jnp.where(low_half, t3, t1))
                    else:
                        t0, t1, t2 = (tile(kind, 3 * m + q) for q in range(3))
                        of_c[0].append(jnp.where(low_half, t0, t1))
                        of_c[1].append(pltpu.roll(jnp.where(low_half, t2, t0), 64, 1))
                        of_c[2].append(jnp.where(low_half, t1, t2))
                values.append(of_c)
            gz = []
            for c in range(3):
                turned = [pltpu.roll(v, 64, 1) for v in values[2][c]]
                gz.append(
                    [
                        sum(
                            coef(n * 3 + m) * values[2][c][m] + coef(9 + n * 3 + m) * turned[m]
                            for m in range(3)
                        )
                        for n in range(3)
                    ]
                )
            g = [values[0], values[1], gz]
            lam = rowpar[0, pl.ds(row, 8), :]
            mu = rowpar[1, pl.ds(row, 8), :]
            sel = rowpar[2, pl.ds(row, 8), :]
            sym_rows = sym[pl.ds(row, 8), :]
            z_stress = [[None] * 3 for _ in range(3)]

            def put(direction, c, m, value):
                at = pl.multiple_of(direction * PTS + rc * 8, 8)
                stress[pl.ds(at, 8), (c * 3 + m) * 128 : (c * 3 + m + 1) * 128] = value

            for m in range(3):
                wz = coef(36 + m)
                muw = mu * wz
                lamw = lam * wz
                selw = sel * wz
                dil = lamw * (g[0][0][m] + g[1][1][m] + g[2][2][m])
                for c in range(3):
                    for d in range(c, 3):
                        s = i * 36 + sym_of(c, d)
                        first, second = s + (2 * m + odd) * 6, s + (2 * m + 1 - odd) * 6
                        src = jnp.where(
                            low_half,
                            jnp.broadcast_to(sym_rows[:, first : first + 1], (8, 128)),
                            jnp.broadcast_to(sym_rows[:, second : second + 1], (8, 128)),
                        )
                        value = muw * (g[d][c][m] + g[c][d][m]) + selw * src
                        if c == d:
                            value = value + dil
                        for a, b in [(c, d)] if c == d else [(c, d), (d, c)]:
                            if b == 2:
                                z_stress[a][m] = value
                            else:
                                put(b, a, m, value)
            for c in range(3):
                turned = [pltpu.roll(v, 64, 1) for v in z_stress[c]]
                for n in range(3):
                    value = sum(
                        coef(18 + n * 3 + m) * z_stress[c][m] + coef(27 + n * 3 + m) * turned[m]
                        for m in range(3)
                    )
                    put(2, c, n, value)
            return carry

        lax.fori_loop(0, 9, rows_step, 0)
        s_high, s_low = split(stress[...])
        two = bdot(bwd, s_high)
        nodes = two[0:ROWS] + two[ROWS : 2 * ROWS] + bdot(bwd[0:ROWS], s_low)

        def node_tile(c, m, nodes=nodes):
            return nodes[:, (c * 3 + m) * 128 : (c * 3 + m + 1) * 128]

        tile0 = start // 128

        def add(index, value, tile0=tile0):
            at = (tile0 + index) * 128
            force[:, at : at + 128] = force[:, at : at + 128] + value

        zero = jnp.zeros((ROWS, 128), F32)
        last_c2 = zero
        for m in range(3):
            c0, c2 = node_tile(0, m), node_tile(2, m)
            c1 = pltpu.roll(node_tile(1, m), 64, 1)
            if odd:
                add(3 * m, jnp.where(low_rows, last_c2, c0))
                add(3 * m + 1, jnp.where(low_rows, c1, c2))
                add(3 * m + 2, jnp.where(low_rows, c0, c1))
                last_c2 = c2
            else:
                add(3 * m, jnp.where(low_rows, c0, c1))
                add(3 * m + 1, jnp.where(low_rows, c2, c0))
                add(3 * m + 2, jnp.where(low_rows, c1, c2))
        if odd:
            add(9, jnp.where(low_rows, last_c2, zero))

    mass = bdot(u2[0:ROWS, COLS + 256 : COLS + 384], spread_ref[...])
    rate = STEP_SQUARED / jnp.where(mass > 0.0, mass, 1.0)
    primal_step = -rate * primal_force
    for x in range(NX):
        now = wide[16 * x : 16 * x + NY, COLS : COLS + 128]
        dpart_ref[x] = (
            primal_step[16 * x : 16 * x + NY, :]
            + 2.0 * now
            - loc_ref[x].astype(F32)
            + rate[16 * x : 16 * x + NY, :] * loc_ref[NX + x].astype(F32)
        )
    edge[:, COLS:BACK] = jnp.zeros((8, 128), F32)
    rx_ref[:, COLS:] = primal_step[80 : 80 + NY, :].astype(BF16)
    for x in range(NX):
        edge[x : x + 1, COLS:BACK] = primal_step[16 * x + NY : 16 * x + NY + 1, :]
    rc_ref[:, COLS:] = primal_step[80 + NY : 81 + NY, :].astype(BF16)

    ids = jnp.transpose(wide[:, COLS : COLS + 128])
    modes = jnp.transpose(wide[:, COLS + 128 : COLS + 256])
    port = lax.broadcasted_iota(jnp.int32, (PORTS, ROWS), 0).astype(F32)
    total = jnp.zeros((128, 128), F32)
    for tile in range(39):
        k0, k1 = (2 * tile) // 3, (2 * tile + 1) // 3
        at = slice(tile * 128, (tile + 1) * 128)
        r0 = jnp.broadcast_to(rate[:, 3 * k0 : 3 * k0 + 1], (ROWS, 128))
        if k1 != k0:
            r1 = jnp.broadcast_to(rate[:, 3 * k1 : 3 * k1 + 1], (ROWS, 128))
            r0 = jnp.where(low_rows, r0, r1)
        force[:, at] = -r0 * force[:, at]
        for x in range(NX):
            rows = slice(16 * x, 16 * x + NY)
            now = force[rows, at] + 2.0 * wide[rows, at] - tp_ref[x, :, at].astype(F32)
            force[rows, at] = now
            part_ref[x, :, at] = now
        high, low = split(force[:, at])
        picked = []
        for h, k in ((2 * tile, k0), (2 * tile + 1, k1)):
            same = ids[78 + k : 79 + k, :] == port
            picked.append(jnp.where(same, modes[h : h + 1, :], 0.0))
        left = jnp.concatenate(picked, axis=0).astype(BF16)
        total = total + bdot(left, high) + bdot(left, low)
    rx_ref[:, :COLS] = force[80 : 80 + NY, :].astype(BF16)
    for x in range(NX):
        edge[x : x + 1, :COLS] = force[16 * x + NY : 16 * x + NY + 1, :]
    ry_ref[...] = edge[0:NX, :].astype(BF16)
    rc_ref[:, :COLS] = force[80 + NY : 81 + NY, :].astype(BF16)
    amp_ref[...] = total[0:64, 0:64] + pltpu.roll(total[64:128, :], 64, 1)[:, 0:64]


def last_kernel(part_ref, dpart_ref, rx_ref, ry_ref, rc_ref, t_ref, d_ref):
    first = lax.broadcasted_iota(jnp.int32, (NY, COLS), 0) == 0
    first_d = lax.broadcasted_iota(jnp.int32, (NY, 128), 0) == 0
    for x in range(NX):
        row = ry_ref[x : x + 1, :].astype(F32)
        if x == 0:
            row = row + rc_ref[...].astype(F32)
        value = part_ref[x] + jnp.where(first, row[:, :COLS], 0.0)
        dvalue = dpart_ref[x] + jnp.where(first_d, row[:, COLS:], 0.0)
        if x == 0:
            value = value + rx_ref[:, :COLS].astype(F32)
            dvalue = dvalue + rx_ref[:, COLS:].astype(F32)
        t_ref[x] = value.astype(BF16)
        d_ref[x] = dvalue[:, :78].astype(BF16)


def per_device(
    disp,
    disp_prev,
    tangent,
    tangent_prev,
    lame_lambda,
    lame_mu,
    node_mass,
    force,
    cell_block,
    direction_block,
    port_id,
    port_mode,
):
    tab = tables()
    nx_dev, ny_dev = lax.axis_size("gx"), lax.axis_size("gy")
    vmem = pl.BlockSpec(memory_space=pltpu.VMEM)
    smem = pl.BlockSpec(memory_space=pltpu.SMEM)
    params = pltpu.CompilerParams(vmem_limit_bytes=VMEM_LIMIT)

    def step(shift_x, shift_y):
        route = []
        for i in range(nx_dev):
            for j in range(ny_dev):
                a, b = i + shift_x, j + shift_y
                if 0 <= a < nx_dev and 0 <= b < ny_dev:
                    route.append((i * ny_dev + j, a * ny_dev + b))
        return route

    def send(block, shift_x, shift_y):
        return lax.ppermute(block, ("gx", "gy"), step(shift_x, shift_y))

    flat = jnp.concatenate([disp, port_mode, disp_prev, force], axis=0).reshape(20, NY, 78)
    flat = jnp.pad(flat, ((0, 0), (0, 0), (0, 50)))
    m1 = lax.reduce_precision(node_mass, 8, 7)
    m2 = lax.reduce_precision(node_mass - m1, 8, 7)
    m3 = node_mass - m1 - m2
    gap = jnp.zeros((NX, NY, 50), BF16)
    small = jnp.concatenate(
        [
            flat[0:5, :, 0:78],
            port_id.astype(BF16),
            gap[:, :, 0:24],
            flat[5:10],
            m1.astype(BF16),
            m2.astype(BF16),
            m3.astype(BF16),
            gap,
        ],
        axis=-1,
    )
    local = flat[10:20]

    face_x, face_y, corner = pl.pallas_call(
        pack_kernel,
        out_shape=(
            jax.ShapeDtypeStruct((NY, WIDE), BF16),
            jax.ShapeDtypeStruct((NX, WIDE), BF16),
            jax.ShapeDtypeStruct((1, WIDE), BF16),
        ),
        in_specs=[vmem, vmem],
        out_specs=(vmem, vmem, vmem),
        scratch_shapes=[pltpu.VMEM((8, WIDE), F32)],
        compiler_params=params,
    )(tangent, small)
    halo_x = send(face_x, -1, 0)
    halo_y = send(face_y, 0, -1)
    halo_c = send(corner, -1, -1)

    par = jnp.stack([lame_lambda.reshape(10), lame_mu.reshape(10)]).astype(F32)
    cells = cell_block.reshape(1, 10)
    by_lane = jnp.repeat(par.reshape(4, 5), 36, axis=1)
    by_lane = jnp.pad(by_lane, ((0, 0), (0, 76)))
    dirs = jnp.concatenate([direction_block, direction_block]).reshape(1, 128)

    part, dpart, ret_x, ret_y, ret_c, amp = pl.pallas_call(
        main_kernel,
        out_shape=(
            jax.ShapeDtypeStruct((NX, NY, COLS), F32),
            jax.ShapeDtypeStruct((NX, NY, 128), F32),
            jax.ShapeDtypeStruct((NY, BACK), BF16),
            jax.ShapeDtypeStruct((NX, BACK), BF16),
            jax.ShapeDtypeStruct((1, BACK), BF16),
            jax.ShapeDtypeStruct((PORTS, 64), F32),
        ),
        in_specs=[smem, smem] + [vmem] * 16,
        out_specs=(vmem,) * 6,
        scratch_shapes=[
            pltpu.VMEM((ROWS, WIDE), F32),
            pltpu.VMEM((2 * ROWS, WIDE), BF16),
            pltpu.VMEM((3 * PTS, 1280), F32),
            pltpu.VMEM((3 * PTS, 1152), F32),
            pltpu.VMEM((ROWS, COLS), F32),
            pltpu.VMEM((PTS, 256), F32),
            pltpu.VMEM((3, PTS, 128), F32),
            pltpu.VMEM((8, BACK), F32),
        ],
        compiler_params=params,
    )(
        par,
        cells,
        tangent,
        tangent_prev,
        small,
        local,
        halo_x,
        halo_y,
        halo_c,
        by_lane,
        dirs,
        jnp.asarray(tab["forward"]),
        jnp.asarray(tab["backward"]),
        jnp.asarray(tab["back32"]),
        jnp.asarray(tab["coef"]),
        jnp.asarray(tab["to_sym"]),
        jnp.asarray(tab["from_sym"]),
        jnp.asarray(tab["spread"]),
    )

    back_x = send(ret_x, 1, 0)
    back_y = send(ret_y, 0, 1)
    back_c = send(ret_c, 1, 1)

    port_rows, port_cols = PORTS // ny_dev, 64 // nx_dev
    shares = amp.reshape(ny_dev, port_rows, nx_dev, port_cols).transpose(2, 0, 1, 3)
    shares = shares.reshape(nx_dev * ny_dev, port_rows * port_cols)
    shares = lax.all_to_all(shares, ("gx", "gy"), 0, 0)
    port_amp = shares.sum(axis=0).reshape(port_rows, port_cols)

    tangent_next, disp_next = pl.pallas_call(
        last_kernel,
        out_shape=(
            jax.ShapeDtypeStruct((NX, NY, COLS), BF16),
            jax.ShapeDtypeStruct((NX, NY, 78), BF16),
        ),
        in_specs=[vmem] * 5,
        out_specs=(vmem, vmem),
        compiler_params=params,
    )(part, dpart, back_x, back_y, back_c)
    return (disp_next.reshape(NX, NY, NZ, 3), tangent_next, port_amp)


def solution(mesh):
    return jax.shard_map(
        per_device,
        mesh=mesh,
        in_specs=(
            P("gx", "gy", None, None),
            P("gx", "gy", None, None),
            P("gx", "gy", None),
            P("gx", "gy", None),
            P("gx", "gy", None),
            P("gx", "gy", None),
            P("gx", "gy", None),
            P("gx", "gy", None, None),
            P("gx", "gy", None),
            P(),
            P("gx", "gy", None),
            P("gx", "gy", None, None),
        ),
        out_specs=(P("gx", "gy", None, None), P("gx", "gy", None), P("gy", "gx")),
        check_vma=False,
    )
```

time: 256 us -> 94.7 us (0.37); the launches traced: 251 us -> 93.8 us
  blocking collectives: 92.9 us -> 0 us
  local copies, waits for them, and re-layouts: 65.8 us -> 19.2 us
  matrix products: 31.4 us -> 0 us
  other arithmetic: 31.4 us -> 3.68 us
  Pallas kernels: 0 us -> 18.8 us
  starting transfers between devices: 24.4 us -> 38.8 us
  waiting for transfers between devices: 2.98 us -> 12.4 us
    psum x1 -> x0, blocking collectives: 92.9 us -> none  [per_device(): total_amp = lax.psum(amplitude, ('gx', 'gy'))]
    dot_general x16 -> x0, matrix products: 31.4 us -> none  [the longest x9 22.3 us: internal_forces(): jnp.einsum(BACK_FORMS[direction], deriv, jnp.concatenate(pieces, axis=-1)...]
    all_to_all x0 -> x1, starting transfers between devices: none -> 19.2 us  [per_device(): shares = lax.all_to_all(shares, ('gx', 'gy'), 0, 0)]
    pallas_call x0 -> x3, Pallas kernels: none -> 18.8 us  [the longest x1 17.6 us: per_device(): pl.pallas_call(main_kernel, out_shape=(jax.ShapeDtypeStruct((NX, NY, COLS...]
    mul x7 -> x0, local copies, waits for them, and re-layouts: 14.9 us -> none  [the longest x6 14.2 us: block_forces(): sensitivity[..., :, None]]
    slice x25 -> x5, local copies, waits for them, and re-layouts: 11.3 us -> 0.24 us  [the longest x2 0.21 us: per_device(): flat[0:5, :, 0:78]]
    dot_general x5 -> x0, local copies, waits for them, and re-layouts: 9.69 us -> none  [the longest x2 4.99 us: gradients(): jnp.einsum('pb,xaybzcn->xaypzcn', deriv, cells, precision=HIGHEST)]
    mul x6 -> x0, other arithmetic: 8.7 us -> none  [the longest x4 6.94 us: internal_forces(): pieces.append(weights * stress)]
  transfers between devices with their start and end apart: 8 -> 7, of which waited for: 2 -> 2; matrix products, arithmetic and copies ran while one was open for 31% -> 5% of each run, Pallas kernels for 0% -> 0%
where the time goes in v1:
time: 94.7 us; the launch traced here: 93.8 us
  starting transfers between devices  38.8 us (41%)
  local copies, waits for them, and re-layouts  19.2 us (20%)
  Pallas kernels  18.8 us (20%)
  waiting for transfers between devices  12.4 us (13%)
  other arithmetic  3.68 us (4%)
    ppermute x6, starting transfers between devices, send(): return lax.ppermute(block, ('gx', 'gy'), step(shift_x, shift_y))  19.6 us
    all_to_all x1, starting transfers between devices, per_device(): shares = lax.all_to_all(shares, ('gx', 'gy'), 0, 0)  19.2 us
    pallas_call x1, Pallas kernels, per_device(): pl.pallas_call(main_kernel, out_shape=(jax.ShapeDtypeStruct((NX, NY, COLS...  17.6 us
    unnamed x48, local copies, waits for them, and re-layouts  14.4 us
    all_to_all x1, waiting for transfers between devices, per_device(): shares = lax.all_to_all(shares, ('gx', 'gy'), 0, 0)  8.12 us
    ppermute x6, waiting for transfers between devices, send(): return lax.ppermute(block, ('gx', 'gy'), step(shift_x, shift_y))  4.28 us
  transfers between devices with their start and end apart: 7, of which 2 were waited for; matrix products, arithmetic and copies ran while one was open for 5% of the time, Pallas kernels for 0%

profile of v1, /device:TPU:1, one launch (start us, length us, event | category | flops | bytes accessed | tf_op | source)
XLA Modules:
  0.0 93.8 jit_solution(6380946830190770795)
XLA Ops:
  0.6 0.9 convert_element_type.24
  1.5 0.8 fusion
  2.3 1.1 %copy.32 = bf16[5,10,26,3]{1,3,2,0:T(4,128)(2,1)S(1)} copy(bf16[5,10,26,3]{2,3,1,0:T(4,128)(2,1)} %param.19) | data formatting | bytes 15600 | tf_op args[0]
  3.6 1.2 %pad_maximum_fusion = bf16[20,10,26,3]{2,3,1,0:T(4,128)(2,1)S(1)} fusion(bf16[5,10,26,3]{2,3,1,0:T(4,128)(2,1)} %param.26, bf16[5,10,26,3]{2,3,1,0:T(4,128)(2,1)} %param.20, bf16[5,10,26,3]{2,3,1,0:T(4,128)(2,1)} %param.30, bf16[5,10,26,3]{2,3,1,0:T(4,128)(2,1)} %param.19), kind=kLoop, calls=%fused_computation | loop fusion | flops 46800 | bytes 62400 | tf_op jit(solution)/shard_map/concatenate | solution.py:456
  5.9 1.3 %collective-permute-start.2 = (bf16[1,5376]{1,0:T(2,128)(2,1)S(1)}, bf16[1,5376]{1,0:T(2,128)(2,1)S(1)}, u32[]{:S(2)}, u32[]{:S(2)}) collective-permute-start(bf16[1,5376]{1,0:T(2,128)(2,1)S(1)} %get-tuple-element.16), channel_id=1, source_target_pairs={{33,0},{34,1},{35,2},{36,3},{37,4},{38,5},{39,6},{40,7},{41,8},{42... | collective-permute-start | bytes 32264 | tf_op jit(solution)/shard_map/ppermute | solution.py:454
  7.2 5.1 %collective-permute-start.1 = (bf16[5,5376]{1,0:T(8,128)(2,1)S(1)}, bf16[5,5376]{1,0:T(8,128)(2,1)S(1)}, u32[]{:S(2)}, u32[]{:S(2)}) collective-permute-start(bf16[5,5376]{1,0:T(8,128)(2,1)S(1)} %get-tuple-element.15), channel_id=1, source_target_pairs={{1,0},{2,1},{3,2},{4,3},{5,4},{6,5},{7,6},{8,7},{9,8},{10,9},{11,1... | collective-permute-start | bytes 161288 | tf_op jit(solution)/shard_map/ppermute | solution.py:454
  12.3 1.3 %collective-permute-start = (bf16[10,5376]{1,0:T(8,128)(2,1)S(1)}, bf16[10,5376]{1,0:T(8,128)(2,1)S(1)}, u32[]{:S(2)}, u32[]{:S(2)}) collective-permute-start(bf16[10,5376]{1,0:T(8,128)(2,1)S(1)} %get-tuple-element.14), channel_id=1, source_target_pairs={{32,0},{33,1},{34,2},{35,3},{36,4},{37,5},{38,6},{39,7},{40,8},{41... | collective-permute-start | bytes 322568 | tf_op jit(solution)/shard_map/ppermute | solution.py:454
  15.9 4.3 %collective-permute-done.hx_ref = bf16[10,5376]{1,0:T(8,128)(2,1)S(1)} collective-permute-done((bf16[10,5376]{1,0:T(8,128)(2,1)S(1)}, bf16[10,5376]{1,0:T(8,128)(2,1)S(1)}, u32[]{:S(2)}, u32[]{:S(2)}) %collective-permute-start) | collective-permute-done | bytes 107552 | tf_op jit(solution)/shard_map/ppermute | solution.py:454
  20.2 1.1 %copy-done.2 = f32[384,512]{1,0:T(8,128)S(1)} copy-done((f32[384,512]{1,0:T(8,128)S(1)}, f32[384,512]{1,0:T(8,128)}, u32[]{:S(2)}) %copy-start.2) | copy-done | bytes 786456
  21.3 1.0 %copy-done.3 = f32[256,384]{1,0:T(8,128)S(1)} copy-done((f32[256,384]{1,0:T(8,128)S(1)}, f32[256,384]{1,0:T(8,128)}, u32[]{:S(2)}) %copy-start.3) | copy-done | bytes 393240
  22.3 1.0 %copy-done.4 = f32[78,8,128]{2,1,0:T(8,128)S(1)} copy-done((f32[78,8,128]{2,1,0:T(8,128)S(1)}, f32[78,8,128]{2,1,0:T(8,128)}, u32[]{:S(2)}) %copy-start.4) | copy-done | bytes 319512
  23.3 0.9 copy-done.5
  24.2 0.9 copy-done.6
  25.1 0.9 copy-done.7
  26.0 0.8 copy-done.10
  26.7 0.7 copy-done.13
  27.4 0.7 copy-done.15
  28.7 0.7 copy-done.17
  29.4 17.6 %shard_map.203 = (f32[5,10,4992]{2,1,0:T(8,128)S(1)}, f32[5,10,128]{2,1,0:T(8,128)S(1)}, bf16[10,5120]{1,0:T(8,128)(2,1)}, bf16[5,5120]{1,0:T(8,128)(2,1)}, bf16...) custom-call(f32[2,10]{1,0:T(2,128)S(1)} %copy-done.15, s32[1,10]{1,0:T(1,128)S(1)} %copy-done.17, ...), custom_call_target="tpu_custom_call" | custom-call | tf_op jit(solution)/shard_map/pallas_call | solution.py:499
  46.9 0.6 copy-done.8
  47.6 0.6 copy-done.11
  48.8 2.2 %collective-permute-start.3 = (bf16[10,5120]{1,0:T(8,128)(2,1)}, bf16[10,5120]{1,0:T(8,128)(2,1)S(1)}, u32[]{:S(2)}, u32[]{:S(2)}) collective-permute-start(bf16[10,5120]{1,0:T(8,128)(2,1)} %get-tuple-element.19), channel_id=1, source_target_pairs={{0,32},{1,33},{2,34},{3,35},{4,36},{5,37},{6,38},{7,39},{8,40},{9,... | collective-permute-start | bytes 307208 | tf_op jit(solution)/shard_map/ppermute | solution.py:454
  51.0 5.1 %collective-permute-start.4 = (bf16[5,5120]{1,0:T(8,128)(2,1)}, bf16[5,5120]{1,0:T(8,128)(2,1)S(1)}, u32[]{:S(2)}, u32[]{:S(2)}) collective-permute-start(bf16[5,5120]{1,0:T(8,128)(2,1)} %get-tuple-element.20), channel_id=1, source_target_pairs={{0,1},{1,2},{2,3},{3,4},{4,5},{5,6},{6,7},{7,8},{8,9},{9,10},{10,1... | collective-permute-start | bytes 153608 | tf_op jit(solution)/shard_map/ppermute | solution.py:454
  56.0 0.9 reshape.41
  57.2 0.8 copy.38
  57.9 19.2 %all-to-all-start = ((f32[256,1,16]{2,1,0:T(1,128)}), f32[256,1,16]{2,1,0:T(1,128)S(1)}, u32[]{:S(2)}, u32[]{:S(2)}) async-start(f32[256,1,16]{2,1,0:T(1,128)} %copy.38), calls=%async_computation | async-start | bytes 262144 | tf_op jit(solution)/shard_map/all_to_all | solution.py:550
  77.2 4.6 %collective-permute-start.5 = (bf16[1,5120]{1,0:T(2,128)(2,1)}, bf16[1,5120]{1,0:T(2,128)(2,1)S(1)}, u32[]{:S(2)}, u32[]{:S(2)}) collective-permute-start(bf16[1,5120]{1,0:T(2,128)(2,1)} %copy-done.18), channel_id=1, source_target_pairs={{0,33},{1,34},{2,35},{3,36},{4,37},{5,38},{6,39},{7,40},{8,41},{9,... | collective-permute-start | bytes 30728 | tf_op jit(solution)/shard_map/ppermute | solution.py:454
  81.8 8.1 %all-to-all-done = f32[256,1,16]{2,1,0:T(1,128)S(1)} async-done(((f32[256,1,16]{2,1,0:T(1,128)}), f32[256,1,16]{2,1,0:T(1,128)S(1)}, u32[]{:S(2)}, u32[]{:S(2)}) %all-to-all-start) | async-done | bytes 16416 | tf_op jit(solution)/shard_map/all_to_all | solution.py:550
  90.2 0.6 reshape.42
  90.9 0.8 copy-done.9
  91.7 1.1 %shard_map.204 = (bf16[5,10,4992]{2,1,0:T(8,128)(2,1)}, bf16[5,10,78]{2,1,0:T(8,128)(2,1)S(1)}) custom-call(f32[5,10,4992]{2,1,0:T(8,128)S(1)} %get-tuple-element.17.part_ref, f32[5,10,128]{2,1,0:T(8,128)S(1)} %copy-done.9, bf16[10,5120]{1,0:T(8,128)(2,1)S(1)} %collective-permute-done.3.rx_ref, bf16[5,5120]{1,0:T(8,128)(2,1)S(1)} %collective-permute-done.4.ry_ref, ...), custom_call_target="tpu_custom_call" | custom-call | tf_op jit(solution)/shard_map/pallas_call | solution.py:553
  93.0 0.9 copy.39
  (63 shorter events, 5.5 us)
Async XLA Ops:
  0.6 5.1 %copy-start = (bf16[5,10,4992]{2,1,0:T(8,128)(2,1)S(1)}, bf16[5,10,4992]{2,1,0:T(8,128)(2,1)}, u32[]{:S(2)}) copy-start(bf16[5,10,4992]{2,1,0:T(8,128)(2,1)} %t_ref.3) | copy-start | bytes 1497604
  3.4 10.2 %copy-start.20 = (bf16[1,2,5]{2,1,0:T(2,128)(2,1)S(1)}, bf16[1,2,5]{2,1,0:T(2,128)(2,1)}, u32[]{:S(2)}) copy-start(bf16[1,2,5]{2,1,0:T(2,128)(2,1)} %param.23) | copy-start | bytes 64
  3.4 10.3 %copy-start.21 = (bf16[1,2,5]{2,1,0:T(2,128)(2,1)S(1)}, bf16[1,2,5]{2,1,0:T(2,128)(2,1)}, u32[]{:S(2)}) copy-start(bf16[1,2,5]{2,1,0:T(2,128)(2,1)} %param.24) | copy-start | bytes 64
  3.5 10.4 %copy-start.22 = (s32[64]{0:T(128)S(1)}, s32[64]{0:T(128)}, u32[]{:S(2)}) copy-start(s32[64]{0:T(128)} %param.28) | copy-start | bytes 772
  3.5 11.0 %copy-start.19 = (s32[1,2,5]{2,1,0:T(2,128)S(1)}, s32[1,2,5]{2,1,0:T(2,128)}, u32[]{:S(2)}) copy-start(s32[1,2,5]{2,1,0:T(2,128)} %param.27) | copy-start | bytes 124
  3.5 16.7 %copy-start.1 = (bf16[5,10,4992]{2,1,0:T(8,128)(2,1)S(1)}, bf16[5,10,4992]{2,1,0:T(8,128)(2,1)}, u32[]{:S(2)}) copy-start(bf16[5,10,4992]{2,1,0:T(8,128)(2,1)} %tp_ref.1) | copy-start | bytes 1497604
  5.9 9.4 %collective-permute-start.2 = (bf16[1,5376]{1,0:T(2,128)(2,1)S(1)}, bf16[1,5376]{1,0:T(2,128)(2,1)S(1)}, u32[]{:S(2)}, u32[]{:S(2)}) collective-permute-start(bf16[1,5376]{1,0:T(2,128)(2,1)S(1)} %get-tuple-element.16), channel_id=1, source_target_pairs={{33,0},{34,1},{35,2},{36,3},{37,4},{38,5},{39,6},{40,7},{41,8},{42... | collective-permute-start | bytes 32264 | tf_op jit(solution)/shard_map/ppermute | solution.py:454
  7.2 8.7 %collective-permute-start.1 = (bf16[5,5376]{1,0:T(8,128)(2,1)S(1)}, bf16[5,5376]{1,0:T(8,128)(2,1)S(1)}, u32[]{:S(2)}, u32[]{:S(2)}) collective-permute-start(bf16[5,5376]{1,0:T(8,128)(2,1)S(1)} %get-tuple-element.15), channel_id=1, source_target_pairs={{1,0},{2,1},{3,2},{4,3},{5,4},{6,5},{7,6},{8,7},{9,8},{10,9},{11,1... | collective-permute-start | bytes 161288 | tf_op jit(solution)/shard_map/ppermute | solution.py:454
  12.3 7.8 %collective-permute-start = (bf16[10,5376]{1,0:T(8,128)(2,1)S(1)}, bf16[10,5376]{1,0:T(8,128)(2,1)S(1)}, u32[]{:S(2)}, u32[]{:S(2)}) collective-permute-start(bf16[10,5376]{1,0:T(8,128)(2,1)S(1)} %get-tuple-element.14), channel_id=1, source_target_pairs={{32,0},{33,1},{34,2},{35,3},{36,4},{37,5},{38,6},{39,7},{40,8},{41... | collective-permute-start | bytes 322568 | tf_op jit(solution)/shard_map/ppermute | solution.py:454
  13.8 2.0 %copy-start.14 = (f32[2,10]{1,0:T(2,128)}, f32[2,10]{1,0:T(2,128)S(1)}, u32[]{:S(2)}) copy-start(f32[2,10]{1,0:T(2,128)S(1)} %maximum_convert_fusion.par_ref) | copy-start | bytes 244
  15.3 0.6 copy-start.12
  20.2 1.1 %copy-start.2 = (f32[384,512]{1,0:T(8,128)S(1)}, f32[384,512]{1,0:T(8,128)}, u32[]{:S(2)}) copy-start(f32[384,512]{1,0:T(8,128)} %constant.26.clone.to_sym_ref) | copy-start | bytes 2359300
  21.3 1.0 %copy-start.3 = (f32[256,384]{1,0:T(8,128)S(1)}, f32[256,384]{1,0:T(8,128)}, u32[]{:S(2)}) copy-start(f32[256,384]{1,0:T(8,128)} %constant.27.clone.from_sym_ref) | copy-start | bytes 1179652
  22.3 1.0 %copy-start.4 = (f32[78,8,128]{2,1,0:T(8,128)S(1)}, f32[78,8,128]{2,1,0:T(8,128)}, u32[]{:S(2)}) copy-start(f32[78,8,128]{2,1,0:T(8,128)} %constant.25.clone.coef_ref) | copy-start | bytes 958468
  23.3 0.9 copy-start.5
  24.2 0.9 copy-start.6
  25.1 0.9 copy-start.7
  26.0 0.8 copy-start.10
  26.7 0.7 copy-start.13
  27.4 0.7 copy-start.15
  28.1 0.6 copy-start.16
  28.7 0.7 copy-start.17
  46.9 0.6 copy-start.8
  47.6 0.6 copy-start.11
  48.2 0.6 copy-start.18
  48.8 42.1 %collective-permute-start.3 = (bf16[10,5120]{1,0:T(8,128)(2,1)}, bf16[10,5120]{1,0:T(8,128)(2,1)S(1)}, u32[]{:S(2)}, u32[]{:S(2)}) collective-permute-start(bf16[10,5120]{1,0:T(8,128)(2,1)} %get-tuple-element.19), channel_id=1, source_target_pairs={{0,32},{1,33},{2,34},{3,35},{4,36},{5,37},{6,38},{7,39},{8,40},{9,... | collective-permute-start | bytes 307208 | tf_op jit(solution)/shard_map/ppermute | solution.py:454
  51.0 39.9 %collective-permute-start.4 = (bf16[5,5120]{1,0:T(8,128)(2,1)}, bf16[5,5120]{1,0:T(8,128)(2,1)S(1)}, u32[]{:S(2)}, u32[]{:S(2)}) collective-permute-start(bf16[5,5120]{1,0:T(8,128)(2,1)} %get-tuple-element.20), channel_id=1, source_target_pairs={{0,1},{1,2},{2,3},{3,4},{4,5},{5,6},{6,7},{7,8},{8,9},{9,10},{10,1... | collective-permute-start | bytes 153608 | tf_op jit(solution)/shard_map/ppermute | solution.py:454
  57.9 32.0 %all-to-all-start = ((f32[256,1,16]{2,1,0:T(1,128)}), f32[256,1,16]{2,1,0:T(1,128)S(1)}, u32[]{:S(2)}, u32[]{:S(2)}) async-start(f32[256,1,16]{2,1,0:T(1,128)} %copy.38), calls=%async_computation | async-start | bytes 262144 | tf_op jit(solution)/shard_map/all_to_all | solution.py:550
  77.2 13.7 %collective-permute-start.5 = (bf16[1,5120]{1,0:T(2,128)(2,1)}, bf16[1,5120]{1,0:T(2,128)(2,1)S(1)}, u32[]{:S(2)}, u32[]{:S(2)}) collective-permute-start(bf16[1,5120]{1,0:T(2,128)(2,1)} %copy-done.18), channel_id=1, source_target_pairs={{0,33},{1,34},{2,35},{3,36},{4,37},{5,38},{6,39},{7,40},{8,41},{9,... | collective-permute-start | bytes 30728 | tf_op jit(solution)/shard_map/ppermute | solution.py:454
  90.9 0.8 copy-start.9

commit v2 on v1

v2 whole, which is shorter than its diff:
```python
import functools

import jax
import jax.numpy as jnp
import ml_dtypes
import numpy as np
from jax import lax
from jax.experimental import pallas as pl
from jax.experimental.pallas import tpu as pltpu
from jax.sharding import PartitionSpec as P

PORTS = 64
GLL_POINTS = np.array(
    [-1.0, -0.765055323929465, -0.285231516480645, 0.285231516480645, 0.765055323929465, 1.0]
)
GLL_WEIGHTS = np.array(
    [
        1.0 / 15.0,
        0.378474956297847,
        0.554858377035486,
        0.554858377035486,
        0.378474956297847,
        1.0 / 15.0,
    ]
)
STEP_SQUARED = 0.03
HIGHEST = lax.Precision.HIGHEST
F32 = jnp.float32
BF16 = jnp.bfloat16

NX, NY, NZ = 5, 10, 26
COLS = 4992
SMALL = 384
WIDE = COLS + SMALL
BACK = COLS + 128
ROWS = 96
PTS = 72
VMEM_LIMIT = 24 * 1024 * 1024
VMEM_MOST = 60 * 1024 * 1024
UNROLL = 9
LONG_FLOPS = 4_000_000
LONG_BYTES = 8_000_000


def derivative_table():
    identity = np.eye(6)
    differences = GLL_POINTS[:, None] - GLL_POINTS[None, :] + identity
    barycentric = 1.0 / np.prod(differences, axis=1)
    matrix = barycentric[None, :] / barycentric[:, None] / differences
    matrix = matrix * (1.0 - identity)
    matrix = matrix - identity * matrix.sum(axis=1)[:, None]
    return matrix


def halves(matrix):
    matrix = matrix.astype(np.float32)
    high = matrix.astype(ml_dtypes.bfloat16)
    low = (matrix - high.astype(np.float32)).astype(ml_dtypes.bfloat16)
    return high, low


SYM = {(0, 0): 0, (1, 1): 1, (2, 2): 2, (0, 1): 3, (0, 2): 4, (1, 2): 5}


def sym_of(c, d):
    return SYM[(min(c, d), max(c, d))]


@functools.cache
def tables():
    deriv = derivative_table()
    w = GLL_WEIGHTS
    fx = np.zeros((PTS, ROWS))
    fy = np.zeros((PTS, ROWS))
    fv = np.zeros((PTS, ROWS))
    wxy = np.zeros(PTS)
    for e in range(2):
        for px in range(6):
            for py in range(6):
                r = e * 36 + px * 6 + py
                wxy[r] = w[px] * w[py]
                fv[r, 16 * px + 5 * e + py] = 1.0
                for a in range(6):
                    fx[r, 16 * a + 5 * e + py] += deriv[px, a]
                    fy[r, 16 * px + 5 * e + a] += deriv[py, a]
    forward = np.concatenate([fx, fy, fv], axis=0)
    f_high, f_low = halves(forward)
    forward2 = np.concatenate([f_high, f_low], axis=1)
    backward = np.concatenate([(m * wxy[:, None]).T for m in (fx, fy, fv)], axis=1)
    b_high, b_low = halves(backward)
    backward2 = np.concatenate([b_high, b_low], axis=0)

    coef = np.zeros((2, 39, 128))
    for n in range(3):
        for m in range(3):
            a = np.repeat([deriv[2 * n, 2 * m], deriv[2 * n + 1, 2 * m + 1]], 64)
            b = np.repeat([deriv[2 * n, 2 * m + 1], deriv[2 * n + 1, 2 * m]], 64)
            at = np.repeat([deriv[2 * m, 2 * n], deriv[2 * m + 1, 2 * n + 1]], 64)
            bt = np.repeat([deriv[2 * m + 1, 2 * n], deriv[2 * m, 2 * n + 1]], 64)
            for q, v in enumerate((a, b, at, bt)):
                coef[0, q * 9 + n * 3 + m] = v
                coef[1, q * 9 + n * 3 + m] = np.roll(v, 64)
    for m in range(3):
        v = np.repeat([w[2 * m], w[2 * m + 1]], 64)
        coef[0, 36 + m] = v
        coef[1, 36 + m] = np.roll(v, 64)
    coef = np.repeat(coef.reshape(78, 1, 128), 8, axis=1).astype(np.float32)

    to_sym = np.zeros((3, 128, 512))
    from_sym = np.zeros((256, 384))
    merge = np.zeros((128, 128))
    for i in range(5):
        for kp in range(6):
            base = i * 36 + kp * 6
            for c in range(3):
                merge[i * 18 + c * 6 + kp, c * 32 + 5 * i + kp] = 1.0
                for d in range(3):
                    s = base + sym_of(c, d)
                    targets = [(s, 2.0 if c == d else 1.0)]
                    if c == d:
                        targets += [(256 + base + q, 1.0) for q in range(3)]
                    for column, factor in targets:
                        if d < 2:
                            to_sym[d, c * 32 + 5 * i + kp, column] += factor
                        else:
                            for k in range(6):
                                to_sym[2, c * 32 + 5 * i + k, column] += factor * deriv[kp, k]
                    if d < 2:
                        from_sym[s, d * 128 + i * 18 + c * 6 + kp] += w[kp]
                    else:
                        for k in range(6):
                            from_sym[s, 256 + i * 18 + c * 6 + k] += w[kp] * deriv[kp, k]
    spread = np.zeros((128, 128))
    for piece in range(3):
        for k in range(NZ):
            for c in range(3):
                spread[piece * 32 + k, c * 32 + k] = 1.0
    of_first = np.tile(np.arange(PTS) < 36, 3)[None, :]
    back_el = np.concatenate([backward * of_first, backward * ~of_first], axis=0)
    wide = np.zeros((952, 512), np.float32)
    wide[0:384] = to_sym.reshape(384, 512)
    wide[384:640, 0:384] = from_sym
    wide[384:512, 384:512] = merge
    wide[640:832, 0:216] = back_el
    wide[640:952, 256:384] = coef[0:39].reshape(312, 128)
    wide[640:952, 384:512] = coef[39:78].reshape(312, 128)
    short = np.zeros((544, 256), ml_dtypes.bfloat16)
    short[0:216, 0:192] = forward2
    short[224:416, 0:216] = backward2
    short[416:544, 0:128] = spread
    return wide, short


def fdot(a, b):
    return jnp.dot(a, b, preferred_element_type=F32, precision=HIGHEST)


def bdot(a, b):
    return jnp.dot(a, b, preferred_element_type=F32)


def split(value):
    high = value.astype(BF16)
    return high, (value - high.astype(F32)).astype(BF16)


def fetch(pairs, sem):
    copies = [pltpu.make_async_copy(src, dst, sem.at[n]) for n, (src, dst) in enumerate(pairs)]
    for copy in copies:
        copy.start()
    return copies


def pack_kernel(*refs):
    sources, (x_ref, y_ref, c_ref, s_ref), (small, wide), sem = (
        refs[0:5],
        refs[5:9],
        refs[9:11],
        refs[11],
    )
    t_ref, d_ref, m_ref, mass_ref, id_ref = here = refs[12:17]
    copies = fetch(zip(sources, here, strict=True), sem)
    small[...] = jnp.zeros((NX, 16, SMALL), F32)
    for copy in copies[1:]:
        copy.wait()
    for x in range(NX):
        d = d_ref[x].astype(F32)
        m = m_ref[x].astype(F32)
        for c in range(3):
            small[x, 0:NY, 32 * c : 32 * c + NZ] = d[:, c, :]
            small[x, 0:NY, 128 + 32 * c : 128 + 32 * c + NZ] = m[:, c, :]
        small[x, 0:NY, 96 : 96 + NZ] = id_ref[x].astype(F32)
        rest = mass_ref[x]
        for piece in range(3):
            part = rest.astype(BF16).astype(F32)
            small[x, 0:NY, 256 + 32 * piece : 256 + 32 * piece + NZ] = part
            rest = rest - part
        s_ref[x] = small[x, 0:NY, :].astype(BF16)
    copies[0].wait()
    x_ref[:, :COLS] = t_ref[0]
    x_ref[:, COLS:] = small[0, 0:NY, :].astype(BF16)
    for x in range(NX):
        wide[x : x + 1, :COLS] = t_ref[x, 0:1, :].astype(F32)
        wide[x : x + 1, COLS:] = small[x, 0:1, :]
    y_ref[...] = wide[0:NX, :].astype(BF16)
    c_ref[...] = wide[0:1, :].astype(BF16)


def local_kernel(*refs):
    t_ref, tp_ref, d_ref, dp_ref, f_ref, wide_in, short_in = refs[0:7]
    base_ref, own_ref, copy_ref, wide_out, short_out = refs[7:12]
    own_ref[...] = jnp.zeros((2, NX, NY, 128), F32)
    wide_out[...] = wide_in[...]
    short_out[...] = short_in[...]
    for x in range(NX):
        now = t_ref[x]
        copy_ref[x] = now
        base_ref[x] = 2.0 * now.astype(F32) - tp_ref[x].astype(F32)
        d = 2.0 * d_ref[x].astype(F32) - dp_ref[x].astype(F32)
        f = f_ref[x].astype(F32)
        for c in range(3):
            own_ref[0, x, :, 32 * c : 32 * c + NZ] = d[:, c, :]
            own_ref[1, x, :, 32 * c : 32 * c + NZ] = f[:, c, :]


def main_kernel(
    n_x,
    n_y,
    par_ref,
    cell_ref,
    t_ref,
    base_ref,
    own_ref,
    s_ref,
    hx_ref,
    hy_ref,
    hc_ref,
    lanes_ref,
    dirs_ref,
    *rest,
):
    tab, short = rest[0:2]
    part_ref, rx_ref, ry_ref, rc_ref, share_ref = rest[2:7]
    (wide, uc, grad, stress, force, edge, amp) = rest[7:]

    for x in range(NX):
        wide[16 * x + 8 : 16 * x + 16, :] = jnp.zeros((8, WIDE), F32)
        wide[16 * x : 16 * x + NY, :COLS] = t_ref[x].astype(F32)
        wide[16 * x : 16 * x + NY, COLS:] = s_ref[x].astype(F32)
        wide[16 * x + NY : 16 * x + NY + 1, :] = hy_ref[x : x + 1, :].astype(F32)
    wide[88:96, :] = jnp.zeros((8, WIDE), F32)
    wide[80 : 80 + NY, :] = hx_ref[...].astype(F32)
    wide[80 + NY : 81 + NY, :] = hc_ref[...].astype(F32)

    low_rows = lax.broadcasted_iota(jnp.int32, (ROWS, 128), 1) < 64
    first_el = lax.broadcasted_iota(jnp.int32, (PTS, 128), 0) < 36
    first_el2 = lax.broadcasted_iota(jnp.int32, (PTS, 256), 0) < 36

    for i in range(5):
        odd = i % 2
        tile0 = (960 * i - 64 * odd) // 128

        def source(index, tile0=tile0):
            return wide[:, (tile0 + index) * 128 : (tile0 + index + 1) * 128]

        for m in range(3):
            t = [source(3 * m + q) for q in range(3 + odd)]
            if odd:
                by_c = (
                    jnp.where(low_rows, t[2], t[0]),
                    pltpu.roll(jnp.where(low_rows, t[1], t[2]), 64, 1),
                    jnp.where(low_rows, t[3], t[1]),
                )
            else:
                by_c = (
                    jnp.where(low_rows, t[0], t[1]),
                    pltpu.roll(jnp.where(low_rows, t[2], t[0]), 64, 1),
                    jnp.where(low_rows, t[1], t[2]),
                )
            for c in range(3):
                at = i * 1152 + (c * 3 + m) * 128
                value = by_c[c].astype(BF16)
                uc[0:ROWS, at : at + 128] = value
                uc[ROWS : 2 * ROWS, at : at + 128] = value

    fwd = short[0:216, 0:192]
    bwd = short[224:416, :]

    small_nodes = wide[:, COLS : COLS + 128].astype(BF16)
    pg = bdot(fwd, jnp.concatenate([small_nodes, small_nodes], axis=0))
    both = fdot(pg[0:PTS], tab[0:128, :])
    both = both + fdot(pg[PTS : 2 * PTS], tab[128:256, :])
    both = both + fdot(pg[2 * PTS : 3 * PTS], tab[256:384, :])
    lam_l = jnp.where(first_el2, lanes_ref[0:1, :], lanes_ref[1:2, :])
    mu_l = jnp.where(first_el2, lanes_ref[2:3, :], lanes_ref[3:4, :])
    primal_stress = lam_l * both[:, 256:512] + mu_l * both[:, 0:256]
    unit = fdot(both[:, 0:256], tab[384:640, 0:384])
    full = fdot(primal_stress, tab[384:640, 0:384])
    terms = jnp.zeros((2 * ROWS, 256), F32)
    for d in range(3):
        pair = jnp.concatenate([a[:, d * 128 : (d + 1) * 128] for a in (unit, full)], axis=1)
        terms = terms + fdot(tab[640:832, d * PTS : (d + 1) * PTS], pair)
    unit_first, unit_second = terms[0:ROWS, 0:128], terms[ROWS : 2 * ROWS, 0:128]
    primal_force = fdot(terms[0:ROWS, 128:256] + terms[ROWS : 2 * ROWS, 128:256], tab[384:512, 384:512])

    force[...] = jnp.zeros((ROWS, COLS), F32)
    lane = lax.broadcasted_iota(jnp.int32, (ROWS, 128), 1)
    row40 = lax.broadcasted_iota(jnp.int32, (40, 128), 0)
    half40 = lax.broadcasted_iota(jnp.int32, (40, 128), 1) // 64

    for i in range(5):
        odd = i % 2
        grad[...] = bdot(fwd, uc[:, i * 1152 : (i + 1) * 1152])
        lam_rows = jnp.where(first_el, par_ref[0, i], par_ref[0, 5 + i])
        mu_rows = jnp.where(first_el, par_ref[1, i], par_ref[1, 5 + i])
        edge[0:PTS, 0:128] = lam_rows
        edge[0:PTS, 128:256] = mu_rows
        pick = [
            jnp.where(dirs_ref[...] == cell_ref[0, 5 * e + i], 1.0, 0.0) for e in range(2)
        ]
        for c in range(3):
            for m in range(3):
                target = c * 6 + 2 * m + (1 - half40 if odd else half40)
                value = jnp.where(
                    row40 == target,
                    pick[0],
                    jnp.where(row40 == target + 18, pick[1], 0.0),
                )
                stress[216:256, (c * 3 + m) * 128 : (c * 3 + m + 1) * 128] = value

        def rows_step(rc, carry, odd=odd):
            row = pl.multiple_of(rc * 8, 8)

            def tile(kind, c, m):
                at = pl.multiple_of(kind * PTS + rc * 8, 8)
                return grad[pl.ds(at, 8), (c * 3 + m) * 128 : (c * 3 + m + 1) * 128]

            def coef(index):
                at = 256 + 128 * odd
                return tab[640 + 8 * index : 648 + 8 * index, at : at + 128]

            def put(direction, c, m, value):
                at = pl.multiple_of(direction * PTS + rc * 8, 8)
                stress[pl.ds(at, 8), (c * 3 + m) * 128 : (c * 3 + m + 1) * 128] = value

            def along_z(tiles, offset):
                turned = [pltpu.roll(v, 64, 1) for v in tiles]
                return [
                    sum(
                        coef(offset + n * 3 + m) * tiles[m]
                        + coef(offset + 9 + n * 3 + m) * turned[m]
                        for m in range(3)
                    )
                    for n in range(3)
                ]

            gz = [along_z([tile(2, c, m) for m in range(3)], 0) for c in range(3)]
            lam = edge[pl.ds(row, 8), 0:128]
            mu = edge[pl.ds(row, 8), 128:256]
            z_stress = [[None] * 3 for _ in range(3)]
            for m in range(3):
                wz = coef(36 + m)
                muw = mu * wz
                g = [[tile(0, c, m) for c in range(3)], [tile(1, c, m) for c in range(3)]]
                g.append([gz[c][m] for c in range(3)])
                dil = (lam * wz) * (g[0][0] + g[1][1] + g[2][2])
                put(0, 0, m, (muw + muw) * g[0][0] + dil)
                put(1, 1, m, (muw + muw) * g[1][1] + dil)
                z_stress[2][m] = (muw + muw) * g[2][2] + dil
                value = muw * (g[0][1] + g[1][0])
                put(0, 1, m, value)
                put(1, 0, m, value)
                value = muw * (g[0][2] + g[2][0])
                put(0, 2, m, value)
                z_stress[0][m] = value
                value = muw * (g[1][2] + g[2][1])
                put(1, 2, m, value)
                z_stress[1][m] = value
            for c in range(3):
                for n, value in enumerate(along_z(z_stress[c], 18)):
                    put(2, c, n, value)
            return carry

        lax.fori_loop(0, 9, rows_step, 0, unroll=UNROLL)
        s_high = stress[...].astype(BF16)
        s_low = (stress[0:216, :] - s_high[0:216].astype(F32)).astype(BF16)
        unit_here = jnp.where(
            lane < 106,
            pltpu.roll(unit_first, (88 - 18 * i) % 128, 1),
            pltpu.roll(unit_second, (106 - 18 * i) % 128, 1),
        )
        unit_high, unit_low = split(unit_here)
        unit_both = jnp.concatenate([unit_high, unit_low], axis=0)
        lane2 = lax.broadcasted_iota(jnp.int32, (2 * ROWS, 128), 1)
        inside = (lane2 >= 88) & (lane2 < 124)
        left = jnp.concatenate(
            [
                bwd[:, 0:128],
                jnp.where(inside, unit_both.astype(F32), bwd[:, 128:256].astype(F32)).astype(BF16),
            ],
            axis=1,
        )
        two = bdot(left, s_high)
        nodes = two[0:ROWS] + two[ROWS : 2 * ROWS] + bdot(bwd[0:ROWS, 0:216], s_low)

        def node_tile(c, m, nodes=nodes):
            return nodes[:, (c * 3 + m) * 128 : (c * 3 + m + 1) * 128]

        tile0 = (960 * i - 64 * odd) // 128

        def add(index, value, tile0=tile0):
            at = (tile0 + index) * 128
            force[:, at : at + 128] = force[:, at : at + 128] + value

        zero = jnp.zeros((ROWS, 128), F32)
        last_c2 = zero
        for m in range(3):
            c0, c2 = node_tile(0, m), node_tile(2, m)
            c1 = pltpu.roll(node_tile(1, m), 64, 1)
            if odd:
                add(3 * m, jnp.where(low_rows, last_c2, c0))
                add(3 * m + 1, jnp.where(low_rows, c1, c2))
                add(3 * m + 2, jnp.where(low_rows, c0, c1))
                last_c2 = c2
            else:
                add(3 * m, jnp.where(low_rows, c0, c1))
                add(3 * m + 1, jnp.where(low_rows, c2, c0))
                add(3 * m + 2, jnp.where(low_rows, c1, c2))
        if odd:
            add(9, jnp.where(low_rows, last_c2, zero))

    mass = bdot(wide[:, COLS + 256 : COLS + 384].astype(BF16), short[416:544, 0:128])
    rate = STEP_SQUARED / jnp.where(mass > 0.0, mass, 1.0)
    primal_step = -rate * primal_force
    for x in range(NX):
        part_ref[x, :, COLS:] = (
            primal_step[16 * x : 16 * x + NY, :]
            + own_ref[0, x]
            + rate[16 * x : 16 * x + NY, :] * own_ref[1, x]
        )
    rx_ref[:, COLS:] = primal_step[80 : 80 + NY, :].astype(BF16)
    for x in range(NX):
        edge[x : x + 1, COLS:BACK] = primal_step[16 * x + NY : 16 * x + NY + 1, :]
    rc_ref[:, COLS:] = primal_step[80 + NY : 81 + NY, :].astype(BF16)

    ids = jnp.transpose(wide[:, COLS : COLS + 128])[96:128]
    ids = jnp.concatenate([ids, ids], axis=1)
    modes = jnp.transpose(wide[:, COLS + 128 : COLS + 256])
    modes = jnp.concatenate([modes, modes], axis=1)
    port = lax.broadcasted_iota(jnp.int32, (PORTS, 2 * ROWS), 0).astype(F32)
    total = jnp.zeros((128, 128), F32)
    for tile in range(39):
        at = slice(tile * 128, (tile + 1) * 128)
        two_halves = [divmod(2 * tile, 3), divmod(2 * tile + 1, 3)]
        k0, k1 = two_halves[0][0], two_halves[1][0]
        r0 = jnp.broadcast_to(rate[:, k0 : k0 + 1], (ROWS, 128))
        if k1 != k0:
            r1 = jnp.broadcast_to(rate[:, k1 : k1 + 1], (ROWS, 128))
            r0 = jnp.where(low_rows, r0, r1)
        force[:, at] = -r0 * force[:, at]
        for x in range(NX):
            rows = slice(16 * x, 16 * x + NY)
            now = force[rows, at] + base_ref[x, :, at]
            force[rows, at] = now
            part_ref[x, :, at] = now
        high, low = split(force[:, at])
        picked = [
            jnp.where(ids[k : k + 1, :] == port, modes[32 * c + k : 32 * c + k + 1, :], 0.0)
            for k, c in two_halves
        ]
        left = jnp.concatenate(picked, axis=0).astype(BF16)
        total = total + bdot(left, jnp.concatenate([high, low], axis=0))
    rx_ref[:, :COLS] = force[80 : 80 + NY, :].astype(BF16)
    for x in range(NX):
        edge[x : x + 1, :COLS] = force[16 * x + NY : 16 * x + NY + 1, :]
    ry_ref[...] = edge[0:NX, 0:BACK].astype(BF16)
    rc_ref[:, :COLS] = force[80 + NY : 81 + NY, :].astype(BF16)
    amp[:, 0:64] = total[0:64, 0:64] + pltpu.roll(total[64:128, :], 64, 1)[:, 0:64]
    p_rows, p_cols = PORTS // n_y, 64 // n_x
    for q in range(p_rows):
        mine = amp[pl.ds(q, n_y, stride=p_rows), :] if p_rows > 1 else amp[...]
        for a in range(n_x):
            share_ref[a * n_y : (a + 1) * n_y, q * p_cols : (q + 1) * p_cols] = mine[
                :, a * p_cols : (a + 1) * p_cols
            ]


def last_kernel(part_ref, rx_ref, ry_ref, rc_ref, t_ref, d_ref):
    first = lax.broadcasted_iota(jnp.int32, (NY, BACK), 0) == 0
    for x in range(NX):
        row = ry_ref[x : x + 1, :].astype(F32)
        if x == 0:
            row = row + rc_ref[...].astype(F32)
        value = part_ref[x] + jnp.where(first, row, 0.0)
        if x == 0:
            value = value + rx_ref[...].astype(F32)
        t_ref[x] = value[:, :COLS].astype(BF16)
        d_ref[x] = value[:, COLS:]


def final_kernel(port_rows, port_cols, share_ref, d_ref, amp_ref, out_ref, lined):
    row = jnp.sum(share_ref[...], axis=0, keepdims=True)
    for q in range(port_rows):
        amp_ref[q : q + 1, :] = row[:, q * port_cols : (q + 1) * port_cols]
    for x in range(NX):
        for c in range(3):
            lined[x, :, c, :] = d_ref[x, :, 32 * c : 32 * c + NZ]
        out_ref[x] = lined[x].astype(BF16)


def per_device(
    disp,
    disp_prev,
    tangent,
    tangent_prev,
    lame_lambda,
    lame_mu,
    node_mass,
    force,
    cell_block,
    direction_block,
    port_id,
    port_mode,
):
    tab = tables()
    nx_dev, ny_dev = lax.axis_size("gx"), lax.axis_size("gy")
    vmem = pl.BlockSpec(memory_space=pltpu.VMEM)
    smem = pl.BlockSpec(memory_space=pltpu.SMEM)
    hbm = pl.BlockSpec(memory_space=pltpu.HBM)
    params = pltpu.CompilerParams(vmem_limit_bytes=VMEM_LIMIT)

    def step(shift_x, shift_y):
        route = []
        for i in range(nx_dev):
            for j in range(ny_dev):
                a, b = i + shift_x, j + shift_y
                if 0 <= a < nx_dev and 0 <= b < ny_dev:
                    route.append((i * ny_dev + j, a * ny_dev + b))
        return route

    def send(block, shift_x, shift_y):
        return lax.ppermute(block, ("gx", "gy"), step(shift_x, shift_y))

    by_comp = [a.transpose(0, 1, 3, 2) for a in (disp, port_mode, disp_prev, force)]
    face_x, face_y, corner, small = pl.pallas_call(
        pack_kernel,
        out_shape=(
            jax.ShapeDtypeStruct((NY, WIDE), BF16),
            jax.ShapeDtypeStruct((NX, WIDE), BF16),
            jax.ShapeDtypeStruct((1, WIDE), BF16),
            jax.ShapeDtypeStruct((NX, NY, SMALL), BF16),
        ),
        in_specs=[hbm] * 5,
        out_specs=(vmem,) * 4,
        scratch_shapes=[
            pltpu.VMEM((NX, 16, SMALL), F32),
            pltpu.VMEM((8, WIDE), F32),
            pltpu.SemaphoreType.DMA((5,)),
            pltpu.VMEM((NX, NY, COLS), BF16),
            pltpu.VMEM((NX, NY, 3, NZ), BF16),
            pltpu.VMEM((NX, NY, 3, NZ), BF16),
            pltpu.VMEM((NX, NY, NZ), F32),
            pltpu.VMEM((NX, NY, NZ), jnp.int32),
        ],
        compiler_params=pltpu.CompilerParams(vmem_limit_bytes=VMEM_MOST),
    )(tangent, by_comp[0], by_comp[1], node_mass, port_id)
    halo_x = send(face_x, -1, 0)
    halo_y = send(face_y, 0, -1)
    halo_c = send(corner, -1, -1)

    wide_table, short_table = (jnp.asarray(a) for a in tab)
    base, own, near, *near_tables = pl.pallas_call(
        local_kernel,
        out_shape=(
            jax.ShapeDtypeStruct((NX, NY, COLS), F32),
            jax.ShapeDtypeStruct((2, NX, NY, 128), F32),
            jax.ShapeDtypeStruct((NX, NY, COLS), BF16),
            jax.ShapeDtypeStruct(wide_table.shape, F32),
            jax.ShapeDtypeStruct(short_table.shape, BF16),
        ),
        in_specs=[vmem] * 7,
        out_specs=(vmem,) * 5,
        compiler_params=params,
        cost_estimate=pl.CostEstimate(
            flops=LONG_FLOPS, bytes_accessed=LONG_BYTES, transcendentals=0
        ),
    )(tangent, tangent_prev, by_comp[0], by_comp[2], by_comp[3], wide_table, short_table)

    par = jnp.stack([lame_lambda.reshape(10), lame_mu.reshape(10)]).astype(F32)
    cells = cell_block.reshape(1, 10)
    by_lane = jnp.repeat(par.reshape(4, 5), 36, axis=1)
    by_lane = jnp.pad(by_lane, ((0, 0), (0, 76)))
    dirs = jnp.concatenate([direction_block, direction_block]).reshape(1, 128)

    part, ret_x, ret_y, ret_c, shares = pl.pallas_call(
        functools.partial(main_kernel, nx_dev, ny_dev),
        out_shape=(
            jax.ShapeDtypeStruct((NX, NY, BACK), F32),
            jax.ShapeDtypeStruct((NY, BACK), BF16),
            jax.ShapeDtypeStruct((NX, BACK), BF16),
            jax.ShapeDtypeStruct((1, BACK), BF16),
            jax.ShapeDtypeStruct((nx_dev * ny_dev, PORTS * 64 // (nx_dev * ny_dev)), F32),
        ),
        in_specs=[smem, smem]
        + [vmem] * 11,
        out_specs=(vmem,) * 5,
        scratch_shapes=[
            pltpu.VMEM((ROWS, WIDE), F32),
            pltpu.VMEM((2 * ROWS, 5 * 1152), BF16),
            pltpu.VMEM((3 * PTS, 1152), F32),
            pltpu.VMEM((256, 1152), F32),
            pltpu.VMEM((ROWS, COLS), F32),
            pltpu.VMEM((PTS, BACK), F32),
            pltpu.VMEM((PORTS, 64), F32),
        ],
        compiler_params=params,
        cost_estimate=pl.CostEstimate(
            flops=400000000, bytes_accessed=8000000, transcendentals=0
        ),
    )(
        par,
        cells,
        near,
        base,
        own,
        small,
        halo_x,
        halo_y,
        halo_c,
        by_lane,
        dirs,
        *near_tables,
    )

    port_rows, port_cols = PORTS // ny_dev, 64 // nx_dev
    shares = lax.all_to_all(shares, ("gx", "gy"), 0, 0)
    back_c = send(ret_c, 1, 1)
    back_y = send(ret_y, 0, 1)
    back_x = send(ret_x, 1, 0)

    tangent_next, disp_wide = pl.pallas_call(
        last_kernel,
        out_shape=(
            jax.ShapeDtypeStruct((NX, NY, COLS), BF16),
            jax.ShapeDtypeStruct((NX, NY, 128), F32),
        ),
        in_specs=[vmem] * 4,
        out_specs=(vmem, vmem),
        compiler_params=params,
        cost_estimate=pl.CostEstimate(flops=4000000, bytes_accessed=8000000, transcendentals=0),
    )(part, back_x, back_y, back_c)
    port_amp, disp_next = pl.pallas_call(
        functools.partial(final_kernel, port_rows, port_cols),
        out_shape=(
            jax.ShapeDtypeStruct((port_rows, port_cols), F32),
            jax.ShapeDtypeStruct((NX, NY, 3, NZ), BF16),
        ),
        in_specs=[vmem, vmem],
        out_specs=(vmem, vmem),
        scratch_shapes=[pltpu.VMEM((NX, NY, 3, NZ), F32)],
        compiler_params=params,
    )(shares, disp_wide)
    return (disp_next.transpose(0, 1, 3, 2), tangent_next, port_amp)


def solution(mesh):
    return jax.shard_map(
        per_device,
        mesh=mesh,
        in_specs=(
            P("gx", "gy", None, None),
            P("gx", "gy", None, None),
            P("gx", "gy", None),
            P("gx", "gy", None),
            P("gx", "gy", None),
            P("gx", "gy", None),
            P("gx", "gy", None),
            P("gx", "gy", None, None),
            P("gx", "gy", None),
            P(),
            P("gx", "gy", None),
            P("gx", "gy", None, None),
        ),
        out_specs=(P("gx", "gy", None, None), P("gx", "gy", None), P("gy", "gx")),
        check_vma=False,
    )
```

time: 94.7 us -> 74 us (0.78)
  local copies, waits for them, and re-layouts: 19.2 us -> 9.88 us
  waiting for transfers between devices: 12.4 us -> 7.09 us
  Pallas kernels: 18.8 us -> 14.7 us
  other arithmetic: 3.68 us -> 0.82 us
  starting transfers between devices: 38.8 us -> 40 us
    unnamed x48 -> x16, local copies, waits for them, and re-layouts: 14.4 us -> 7.41 us
    pallas_call x1 -> x3, Pallas kernels: 17.6 us -> 11.6 us  [the longest x1 10.2 us: per_device(): pl.pallas_call(functools.partial(main_kernel, nx_dev, ny_dev), out_shape=...]
    ppermute x6, waiting for transfers between devices: 4.28 us -> 0.9 us  [send(): return lax.ppermute(block, ('gx', 'gy'), step(shift_x, shift_y))]
    reshape x5 -> x0, local copies, waits for them, and re-layouts: 1.98 us -> none  [the longest x1 0.88 us: per_device(): amp.reshape(ny_dev, port_rows, nx_dev, port_cols).transpose(2, 0, 1, 3)]
    all_to_all x1, waiting for transfers between devices: 8.12 us -> 6.19 us  [per_device(): shares = lax.all_to_all(shares, ('gx', 'gy'), 0, 0)]
    pallas_call x1, Pallas kernels: 0.13 us -> 2.06 us  [per_device(): pl.pallas_call(pack_kernel, out_shape=(jax.ShapeDtypeStruct((NY, WIDE), B...]
    convert_element_type x2 -> x0, other arithmetic: 1.65 us -> none  [the longest x1 0.86 us: per_device(): port_id.astype(BF16)]
    another operation x2, local copies, waits for them, and re-layouts: 0.17 us -> 1.48 us  [per_device(): par = jnp.stack([lame_lambda.reshape(10), lame_mu.reshape(10)]).astype(F32)]
  transfers between devices with their start and end apart: 7 -> 7, of which waited for: 2 -> 2; matrix products, arithmetic and copies ran while one was open for 5% -> 4% of each run, Pallas kernels for 0% -> 2%
where the time goes in v2:
time: 74 us; the launch traced here: 73.3 us
  starting transfers between devices  40 us (54%)
  Pallas kernels  14.7 us (20%)
  local copies, waits for them, and re-layouts  9.88 us (13%)
  waiting for transfers between devices  7.09 us (10%)
  other arithmetic  0.82 us (1%)
  between operations  0.75 us (1%)
    ppermute x6, starting transfers between devices, send(): return lax.ppermute(block, ('gx', 'gy'), step(shift_x, shift_y))  20.8 us
    all_to_all x1, starting transfers between devices, per_device(): shares = lax.all_to_all(shares, ('gx', 'gy'), 0, 0)  19.2 us
    pallas_call x1, Pallas kernels, per_device(): pl.pallas_call(functools.partial(main_kernel, nx_dev, ny_dev), out_shape=...  10.2 us
    unnamed x16, local copies, waits for them, and re-layouts  7.41 us
    all_to_all x1, waiting for transfers between devices, per_device(): shares = lax.all_to_all(shares, ('gx', 'gy'), 0, 0)  6.19 us
    pallas_call x1, Pallas kernels, per_device(): pl.pallas_call(pack_kernel, out_shape=(jax.ShapeDtypeStruct((NY, WIDE), B...  2.06 us
  transfers between devices with their start and end apart: 7, of which 2 were waited for; matrix products, arithmetic and copies ran while one was open for 4% of the time, Pallas kernels for 2%

profile of v2, /device:TPU:1, one launch (start us, length us, event | category | flops | bytes accessed | tf_op | source)
XLA Modules:
  0.0 73.3 jit_solution(5923824671289541213)
XLA Ops:
  0.6 2.1 %shard_map.158 = (bf16[10,5376]{1,0:T(8,128)(2,1)}, bf16[5,5376]{1,0:T(8,128)(2,1)}, bf16[1,5376]{1,0:T(2,128)(2,1)}, bf16[5,10,384]{2,1,0:T(8,128)(2,1)}) custom-call(bf16[5,10,4992]{2,1,0:T(8,128)(2,1)} %refs_0_.3, bf16[5,10,3,26]{3,2,1,0:T(4,128)(2,1)} %bitcast.12, bf16[5,10,3,26]{3,2,1,0:T(4,128)(2,1)} %bitcast.16, f32[5,10,26]{2,1,0:T(8,128)} %refs_3_.1, ...), custom_call_target="tpu_custom_call" | custom-call | tf_op jit(solution)/shard_map/pallas_call | solution.py:545
  2.7 1.3 %collective-permute-start.2 = (bf16[1,5376]{1,0:T(2,128)(2,1)}, bf16[1,5376]{1,0:T(2,128)(2,1)S(1)}, u32[]{:S(2)}, u32[]{:S(2)}) collective-permute-start(bf16[1,5376]{1,0:T(2,128)(2,1)} %get-tuple-element.27), channel_id=1, source_target_pairs={{33,0},{34,1},{35,2},{36,3},{37,4},{38,5},{39,6},{40,7},{41,8},{42... | collective-permute-start | bytes 32264 | tf_op jit(solution)/shard_map/ppermute | solution.py:542
  4.0 5.1 %collective-permute-start.1 = (bf16[5,5376]{1,0:T(8,128)(2,1)}, bf16[5,5376]{1,0:T(8,128)(2,1)S(1)}, u32[]{:S(2)}, u32[]{:S(2)}) collective-permute-start(bf16[5,5376]{1,0:T(8,128)(2,1)} %get-tuple-element.26), channel_id=1, source_target_pairs={{1,0},{2,1},{3,2},{4,3},{5,4},{6,5},{7,6},{8,7},{9,8},{10,9},{11,1... | collective-permute-start | bytes 161288 | tf_op jit(solution)/shard_map/ppermute | solution.py:542
  9.2 1.3 %collective-permute-start = (bf16[10,5376]{1,0:T(8,128)(2,1)}, bf16[10,5376]{1,0:T(8,128)(2,1)S(1)}, u32[]{:S(2)}, u32[]{:S(2)}) collective-permute-start(bf16[10,5376]{1,0:T(8,128)(2,1)} %get-tuple-element.25), channel_id=1, source_target_pairs={{32,0},{33,1},{34,2},{35,3},{36,4},{37,5},{38,6},{39,7},{40,8},{41... | collective-permute-start | bytes 322568 | tf_op jit(solution)/shard_map/ppermute | solution.py:542
  10.5 0.7 %stack_reshape.6 = bf16[1,10]{1,0:T(2,128)(2,1)S(1)} reshape(bf16[1,2,5]{2,1,0:T(2,128)(2,1)} %param.18) | data formatting | bytes 40 | tf_op jit(solution)/shard_map/stack;reshape | solution.py:589
  11.2 0.7 %stack_reshape.7 = bf16[1,10]{1,0:T(2,128)(2,1)S(1)} reshape(bf16[1,2,5]{2,1,0:T(2,128)(2,1)} %param.19) | data formatting | bytes 40 | tf_op jit(solution)/shard_map/stack;reshape | solution.py:589
  11.9 0.8 %add_bitcast_fusion.dirs_ref = s32[1,128]{1,0:T(1,128)S(1)} fusion(s32[64]{0:T(128)} %param.23), kind=kLoop, calls=%fused_computation.1 | loop fusion | flops 128 | bytes 768 | tf_op jit(solution)/shard_map/reshape | solution.py:593
  12.8 0.8 %reshape.21.cell_ref = s32[1,10]{1,0:T(1,128)S(1)} reshape(s32[1,2,5]{2,1,0:T(2,128)} %param.22) | data formatting | bytes 80 | tf_op jit(solution)/shard_map/reshape | solution.py:590
  13.5 0.1 reshape.24
  13.6 0.1 broadcast_in_dim.3
  13.7 0.1 reshape.22
  13.8 1.1 %copy-done = bf16[5,10,4992]{2,1,0:T(8,128)(2,1)S(1)} copy-done((bf16[5,10,4992]{2,1,0:T(8,128)(2,1)S(1)}, bf16[5,10,4992]{2,1,0:T(8,128)(2,1)}, u32[]{:S(2)}) %copy-start) | copy-done | bytes 499224
  14.9 1.5 %copy-done.1 = f32[952,512]{1,0:T(8,128)S(1)} copy-done((f32[952,512]{1,0:T(8,128)S(1)}, f32[952,512]{1,0:T(8,128)}, u32[]{:S(2)}) %copy-start.1) | copy-done | bytes 1949720
  16.4 1.1 %copy-done.2 = bf16[5,10,4992]{2,1,0:T(8,128)(2,1)S(1)} copy-done((bf16[5,10,4992]{2,1,0:T(8,128)(2,1)S(1)}, bf16[5,10,4992]{2,1,0:T(8,128)(2,1)}, u32[]{:S(2)}) %copy-start.2) | copy-done | bytes 499224
  17.6 1.0 %copy-done.3 = bf16[544,256]{1,0:T(8,128)(2,1)S(1)} copy-done((bf16[544,256]{1,0:T(8,128)(2,1)S(1)}, bf16[544,256]{1,0:T(8,128)(2,1)}, u32[]{:S(2)}) %copy-start.3) | copy-done | bytes 278552
  18.5 0.8 %copy-done.4 = bf16[5,10,26,3]{2,3,1,0:T(4,128)(2,1)S(1)} copy-done((bf16[5,10,26,3]{2,3,1,0:T(4,128)(2,1)S(1)}, bf16[5,10,26,3]{2,3,1,0:T(4,128)(2,1)}, u32[]{:S(2)}) %copy-start.4) | copy-done | bytes 7824
  19.3 0.8 %copy-done.6 = bf16[5,10,26,3]{2,3,1,0:T(4,128)(2,1)S(1)} copy-done((bf16[5,10,26,3]{2,3,1,0:T(4,128)(2,1)S(1)}, bf16[5,10,26,3]{2,3,1,0:T(4,128)(2,1)}, u32[]{:S(2)}) %copy-start.6) | copy-done | bytes 7824
  20.1 0.8 %copy-done.7 = bf16[5,10,26,3]{2,3,1,0:T(4,128)(2,1)S(1)} copy-done((bf16[5,10,26,3]{2,3,1,0:T(4,128)(2,1)S(1)}, bf16[5,10,26,3]{2,3,1,0:T(4,128)(2,1)}, u32[]{:S(2)}) %copy-start.7) | copy-done | bytes 7824
  20.9 0.6 shard_map.157
  21.5 0.0 collective-permute-done.2.hc_ref
  21.5 0.0 collective-permute-done.1.hy_ref
  21.5 0.2 copy-done.5
  21.8 10.2 %shard_map.159 = (f32[5,10,5120]{2,1,0:T(8,128)S(1)}, bf16[10,5120]{1,0:T(8,128)(2,1)S(1)}, bf16[5,5120]{1,0:T(8,128)(2,1)S(1)}, bf16[1,5120]{1,0:T(2,128)(2,1)S(1)}, f32[256,16]{1,0:T(8,128)}) custom-call(f32[2,10]{1,0:T(2,128)S(1)} %maximum_convert_fusion.par_ref, s32[1,10]{1,0:T(1,128)S(1)} %reshape.21.cell_ref, ...), custom_call_target="tpu_custom_call" | custom-call | flops 400000000 | bytes 8000000 | tf_op jit(solution)/shard_map/pallas_call | solution.py:595
  32.0 4.5 %collective-permute-start.3 = (bf16[10,5120]{1,0:T(8,128)(2,1)S(1)}, bf16[10,5120]{1,0:T(8,128)(2,1)S(1)}, u32[]{:S(2)}, u32[]{:S(2)}) collective-permute-start(bf16[10,5120]{1,0:T(8,128)(2,1)S(1)} %get-tuple-element.32), channel_id=1, source_target_pairs={{0,32},{1,33},{2,34},{3,35},{4,36},{5,37},{6,38},{7,39},{8,40},{9,... | collective-permute-start | bytes 307208 | tf_op jit(solution)/shard_map/ppermute | solution.py:542
  36.5 3.9 %collective-permute-start.4 = (bf16[5,5120]{1,0:T(8,128)(2,1)S(1)}, bf16[5,5120]{1,0:T(8,128)(2,1)S(1)}, u32[]{:S(2)}, u32[]{:S(2)}) collective-permute-start(bf16[5,5120]{1,0:T(8,128)(2,1)S(1)} %get-tuple-element.33), channel_id=1, source_target_pairs={{0,1},{1,2},{2,3},{3,4},{4,5},{5,6},{6,7},{7,8},{8,9},{9,10},{10,1... | collective-permute-start | bytes 153608 | tf_op jit(solution)/shard_map/ppermute | solution.py:542
  40.4 19.2 %all-to-all-start = ((f32[256,1,16]{2,1,0:T(1,128)}), f32[256,1,16]{2,1,0:T(1,128)S(1)}, u32[]{:S(2)}, u32[]{:S(2)}) async-start(f32[256,1,16]{2,1,0:T(1,128)} %bitcast.6), calls=%async_computation | async-start | bytes 262144 | tf_op jit(solution)/shard_map/all_to_all | solution.py:636
  59.7 4.6 %collective-permute-start.5 = (bf16[1,5120]{1,0:T(2,128)(2,1)S(1)}, bf16[1,5120]{1,0:T(2,128)(2,1)S(1)}, u32[]{:S(2)}, u32[]{:S(2)}) collective-permute-start(bf16[1,5120]{1,0:T(2,128)(2,1)S(1)} %get-tuple-element.34), channel_id=1, source_target_pairs={{0,33},{1,34},{2,35},{3,36},{4,37},{5,38},{6,39},{7,40},{8,41},{9,... | collective-permute-start | bytes 30728 | tf_op jit(solution)/shard_map/ppermute | solution.py:542
  64.3 0.9 %collective-permute-done.5.rc_ref = bf16[1,5120]{1,0:T(2,128)(2,1)S(1)} collective-permute-done((bf16[1,5120]{1,0:T(2,128)(2,1)S(1)}, bf16[1,5120]{1,0:T(2,128)(2,1)S(1)}, u32[]{:S(2)}, u32[]{:S(2)}) %collective-permute-start.5) | collective-permute-done | bytes 10272 | tf_op jit(solution)/shard_map/ppermute | solution.py:542
  65.2 0.0 collective-permute-done.4.ry_ref
  65.2 1.1 %shard_map.160 = (bf16[5,10,4992]{2,1,0:T(8,128)(2,1)}, f32[5,10,128]{2,1,0:T(8,128)S(1)}) custom-call(f32[5,10,5120]{2,1,0:T(8,128)S(1)} %get-tuple-element.31.part_ref, bf16[10,5120]{1,0:T(8,128)(2,1)S(1)} %collective-permute-done.3.rx_ref, bf16[5,5120]{1,0:T(8,128)(2,1)S(1)} %collective-permute-done.4.ry_ref, ...), custom_call_target="tpu_custom_call" | custom-call | flops 4000000 | bytes 8000000 | tf_op jit(solution)/shard_map/pallas_call | solution.py:641
  66.3 6.2 %all-to-all-done = f32[256,1,16]{2,1,0:T(1,128)S(1)} async-done(((f32[256,1,16]{2,1,0:T(1,128)}), f32[256,1,16]{2,1,0:T(1,128)S(1)}, u32[]{:S(2)}, u32[]{:S(2)}) %all-to-all-start) | async-done | bytes 16416 | tf_op jit(solution)/shard_map/all_to_all | solution.py:636
  72.5 0.8 %shard_map.161 = (f32[2,8]{1,0:T(2,128)}, bf16[5,10,3,26]{3,2,1,0:T(4,128)(2,1)}) custom-call(f32[256,16]{1,0:T(8,128)S(1)} %bitcast.11, f32[5,10,128]{2,1,0:T(8,128)S(1)} %get-tuple-element.35.d_ref), custom_call_target="tpu_custom_call" | custom-call | tf_op jit(solution)/shard_map/pallas_call | solution.py:652
  (12 shorter events, 0.0 us)
Async XLA Ops:
  2.7 18.8 %collective-permute-start.2 = (bf16[1,5376]{1,0:T(2,128)(2,1)}, bf16[1,5376]{1,0:T(2,128)(2,1)S(1)}, u32[]{:S(2)}, u32[]{:S(2)}) collective-permute-start(bf16[1,5376]{1,0:T(2,128)(2,1)} %get-tuple-element.27), channel_id=1, source_target_pairs={{33,0},{34,1},{35,2},{36,3},{37,4},{38,5},{39,6},{40,7},{41,8},{42... | collective-permute-start | bytes 32264 | tf_op jit(solution)/shard_map/ppermute | solution.py:542
  4.0 17.5 %collective-permute-start.1 = (bf16[5,5376]{1,0:T(8,128)(2,1)}, bf16[5,5376]{1,0:T(8,128)(2,1)S(1)}, u32[]{:S(2)}, u32[]{:S(2)}) collective-permute-start(bf16[5,5376]{1,0:T(8,128)(2,1)} %get-tuple-element.26), channel_id=1, source_target_pairs={{1,0},{2,1},{3,2},{4,3},{5,4},{6,5},{7,6},{8,7},{9,8},{10,9},{11,1... | collective-permute-start | bytes 161288 | tf_op jit(solution)/shard_map/ppermute | solution.py:542
  9.2 12.4 %collective-permute-start = (bf16[10,5376]{1,0:T(8,128)(2,1)}, bf16[10,5376]{1,0:T(8,128)(2,1)S(1)}, u32[]{:S(2)}, u32[]{:S(2)}) collective-permute-start(bf16[10,5376]{1,0:T(8,128)(2,1)} %get-tuple-element.25), channel_id=1, source_target_pairs={{32,0},{33,1},{34,2},{35,3},{36,4},{37,5},{38,6},{39,7},{40,8},{41... | collective-permute-start | bytes 322568 | tf_op jit(solution)/shard_map/ppermute | solution.py:542
  13.8 1.1 %copy-start = (bf16[5,10,4992]{2,1,0:T(8,128)(2,1)S(1)}, bf16[5,10,4992]{2,1,0:T(8,128)(2,1)}, u32[]{:S(2)}) copy-start(bf16[5,10,4992]{2,1,0:T(8,128)(2,1)} %refs_0_.3) | copy-start | bytes 1497604
  14.9 1.5 %copy-start.1 = (f32[952,512]{1,0:T(8,128)S(1)}, f32[952,512]{1,0:T(8,128)}, u32[]{:S(2)}) copy-start(f32[952,512]{1,0:T(8,128)} %constant.7.clone.refs_5_) | copy-start | bytes 5849092
  16.4 1.1 %copy-start.2 = (bf16[5,10,4992]{2,1,0:T(8,128)(2,1)S(1)}, bf16[5,10,4992]{2,1,0:T(8,128)(2,1)}, u32[]{:S(2)}) copy-start(bf16[5,10,4992]{2,1,0:T(8,128)(2,1)} %refs_1_.1) | copy-start | bytes 1497604
  17.6 1.0 %copy-start.3 = (bf16[544,256]{1,0:T(8,128)(2,1)S(1)}, bf16[544,256]{1,0:T(8,128)(2,1)}, u32[]{:S(2)}) copy-start(bf16[544,256]{1,0:T(8,128)(2,1)} %constant.8.clone.refs_6_) | copy-start | bytes 835588
  18.5 0.8 %copy-start.4 = (bf16[5,10,26,3]{2,3,1,0:T(4,128)(2,1)S(1)}, bf16[5,10,26,3]{2,3,1,0:T(4,128)(2,1)}, u32[]{:S(2)}) copy-start(bf16[5,10,26,3]{2,3,1,0:T(4,128)(2,1)} %param.14) | copy-start | bytes 23404
  19.3 0.8 %copy-start.6 = (bf16[5,10,26,3]{2,3,1,0:T(4,128)(2,1)S(1)}, bf16[5,10,26,3]{2,3,1,0:T(4,128)(2,1)}, u32[]{:S(2)}) copy-start(bf16[5,10,26,3]{2,3,1,0:T(4,128)(2,1)} %param.15) | copy-start | bytes 23404
  20.1 0.8 %copy-start.7 = (bf16[5,10,26,3]{2,3,1,0:T(4,128)(2,1)S(1)}, bf16[5,10,26,3]{2,3,1,0:T(4,128)(2,1)}, u32[]{:S(2)}) copy-start(bf16[5,10,26,3]{2,3,1,0:T(4,128)(2,1)} %param.21) | copy-start | bytes 23404
  20.9 0.8 %copy-start.5 = (bf16[5,10,384]{2,1,0:T(8,128)(2,1)S(1)}, bf16[5,10,384]{2,1,0:T(8,128)(2,1)}, u32[]{:S(2)}) copy-start(bf16[5,10,384]{2,1,0:T(8,128)(2,1)} %get-tuple-element.24.s_ref) | copy-start | bytes 115204
  32.0 33.2 %collective-permute-start.3 = (bf16[10,5120]{1,0:T(8,128)(2,1)S(1)}, bf16[10,5120]{1,0:T(8,128)(2,1)S(1)}, u32[]{:S(2)}, u32[]{:S(2)}) collective-permute-start(bf16[10,5120]{1,0:T(8,128)(2,1)S(1)} %get-tuple-element.32), channel_id=1, source_target_pairs={{0,32},{1,33},{2,34},{3,35},{4,36},{5,37},{6,38},{7,39},{8,40},{9,... | collective-permute-start | bytes 307208 | tf_op jit(solution)/shard_map/ppermute | solution.py:542
  36.5 28.7 %collective-permute-start.4 = (bf16[5,5120]{1,0:T(8,128)(2,1)S(1)}, bf16[5,5120]{1,0:T(8,128)(2,1)S(1)}, u32[]{:S(2)}, u32[]{:S(2)}) collective-permute-start(bf16[5,5120]{1,0:T(8,128)(2,1)S(1)} %get-tuple-element.33), channel_id=1, source_target_pairs={{0,1},{1,2},{2,3},{3,4},{4,5},{5,6},{6,7},{7,8},{8,9},{9,10},{10,1... | collective-permute-start | bytes 153608 | tf_op jit(solution)/shard_map/ppermute | solution.py:542
  40.4 32.0 %all-to-all-start = ((f32[256,1,16]{2,1,0:T(1,128)}), f32[256,1,16]{2,1,0:T(1,128)S(1)}, u32[]{:S(2)}, u32[]{:S(2)}) async-start(f32[256,1,16]{2,1,0:T(1,128)} %bitcast.6), calls=%async_computation | async-start | bytes 262144 | tf_op jit(solution)/shard_map/all_to_all | solution.py:636
  59.7 5.5 %collective-permute-start.5 = (bf16[1,5120]{1,0:T(2,128)(2,1)S(1)}, bf16[1,5120]{1,0:T(2,128)(2,1)S(1)}, u32[]{:S(2)}, u32[]{:S(2)}) collective-permute-start(bf16[1,5120]{1,0:T(2,128)(2,1)S(1)} %get-tuple-element.34), channel_id=1, source_target_pairs={{0,33},{1,34},{2,35},{3,36},{4,37},{5,38},{6,39},{7,40},{8,41},{9,... | collective-permute-start | bytes 30728 | tf_op jit(solution)/shard_map/ppermute | solution.py:542

commit v3 on v2

--- a/solution.py
+++ b/solution.py
@@ -24,7 +24,6 @@
     ]
 )
 STEP_SQUARED = 0.03
-HIGHEST = lax.Precision.HIGHEST
 F32 = jnp.float32
 BF16 = jnp.bfloat16
 
@@ -38,8 +37,8 @@
 VMEM_LIMIT = 24 * 1024 * 1024
 VMEM_MOST = 60 * 1024 * 1024
 UNROLL = 9
-LONG_FLOPS = 4_000_000
-LONG_BYTES = 8_000_000
+CORNER = 1
+SHARE = 64
 
 
 def derivative_table():
@@ -152,7 +151,8 @@
 
 
 def fdot(a, b):
-    return jnp.dot(a, b, preferred_element_type=F32, precision=HIGHEST)
+    (a_high, a_low), (b_high, b_low) = split(a), split(b)
+    return bdot(a_high, b_high) + (bdot(a_low, b_high) + bdot(a_high, b_low))
 
 
 def bdot(a, b):
@@ -172,23 +172,25 @@
 
 
 def pack_kernel(*refs):
-    sources, (x_ref, y_ref, c_ref, s_ref), (small, wide), sem = (
-        refs[0:5],
-        refs[5:9],
-        refs[9:11],
-        refs[11],
-    )
-    t_ref, d_ref, m_ref, mass_ref, id_ref = here = refs[12:17]
+    sources, (x_ref, y_ref, c_ref, s_ref, own_ref, par_ref) = refs[0:11], refs[11:17]
+    small, wide, sem = refs[17:20]
+    here = refs[20:]
+    t_ref, d_ref, m_ref, mass_ref, id_ref, dp_ref, f_ref, lam_ref, mu_ref, cell_ref, dir_ref = here
     copies = fetch(zip(sources, here, strict=True), sem)
     small[...] = jnp.zeros((NX, 16, SMALL), F32)
+    own_ref[...] = jnp.zeros((2, NX, NY, 128), F32)
     for copy in copies[1:]:
         copy.wait()
     for x in range(NX):
         d = d_ref[x].astype(F32)
         m = m_ref[x].astype(F32)
+        before = 2.0 * d - dp_ref[x].astype(F32)
+        f = f_ref[x].astype(F32)
         for c in range(3):
             small[x, 0:NY, 32 * c : 32 * c + NZ] = d[:, c, :]
             small[x, 0:NY, 128 + 32 * c : 128 + 32 * c + NZ] = m[:, c, :]
+            own_ref[0, x, :, 32 * c : 32 * c + NZ] = before[:, c, :]
+            own_ref[1, x, :, 32 * c : 32 * c + NZ] = f[:, c, :]
         small[x, 0:NY, 96 : 96 + NZ] = id_ref[x].astype(F32)
         rest = mass_ref[x]
         for piece in range(3):
@@ -196,6 +198,22 @@
             small[x, 0:NY, 256 + 32 * piece : 256 + 32 * piece + NZ] = part
             rest = rest - part
         s_ref[x] = small[x, 0:NY, :].astype(BF16)
+    along_z = lax.broadcasted_iota(jnp.int32, (1, 256), 1) // 36
+    for q, ref in enumerate((lam_ref, mu_ref)):
+        values = ref[0].astype(F32)
+        for e in range(2):
+            row = jnp.zeros((1, 256), F32)
+            for i in range(5):
+                row = jnp.where(
+                    along_z == i, jnp.broadcast_to(values[e : e + 1, i : i + 1], (1, 256)), row
+                )
+            par_ref[2 * q + e : 2 * q + e + 1, :] = row
+    dirs = jnp.concatenate([dir_ref[...], dir_ref[...]], axis=1)
+    cells = cell_ref[0]
+    for e in range(2):
+        for i in range(5):
+            same = dirs == jnp.broadcast_to(cells[e : e + 1, i : i + 1], (1, 128))
+            par_ref[8 + 5 * e + i : 9 + 5 * e + i, 0:128] = jnp.where(same, 1.0, 0.0)
     copies[0].wait()
     x_ref[:, :COLS] = t_ref[0]
     x_ref[:, COLS:] = small[0, 0:NY, :].astype(BF16)
@@ -206,28 +224,19 @@
     c_ref[...] = wide[0:1, :].astype(BF16)
 
 
-def local_kernel(*refs):
-    t_ref, tp_ref, d_ref, dp_ref, f_ref, wide_in, short_in = refs[0:7]
-    base_ref, own_ref, copy_ref, wide_out, short_out = refs[7:12]
-    own_ref[...] = jnp.zeros((2, NX, NY, 128), F32)
+def local_kernel(t_ref, tp_ref, wide_in, short_in, base_ref, copy_ref, wide_out, short_out):
     wide_out[...] = wide_in[...]
     short_out[...] = short_in[...]
     for x in range(NX):
         now = t_ref[x]
         copy_ref[x] = now
         base_ref[x] = 2.0 * now.astype(F32) - tp_ref[x].astype(F32)
-        d = 2.0 * d_ref[x].astype(F32) - dp_ref[x].astype(F32)
-        f = f_ref[x].astype(F32)
-        for c in range(3):
-            own_ref[0, x, :, 32 * c : 32 * c + NZ] = d[:, c, :]
-            own_ref[1, x, :, 32 * c : 32 * c + NZ] = f[:, c, :]
 
 
 def main_kernel(
     n_x,
     n_y,
     par_ref,
-    cell_ref,
     t_ref,
     base_ref,
     own_ref,
@@ -235,8 +244,6 @@
     hx_ref,
     hy_ref,
     hc_ref,
-    lanes_ref,
-    dirs_ref,
     *rest,
 ):
     tab, short = rest[0:2]
@@ -291,8 +298,8 @@
     both = fdot(pg[0:PTS], tab[0:128, :])
     both = both + fdot(pg[PTS : 2 * PTS], tab[128:256, :])
     both = both + fdot(pg[2 * PTS : 3 * PTS], tab[256:384, :])
-    lam_l = jnp.where(first_el2, lanes_ref[0:1, :], lanes_ref[1:2, :])
-    mu_l = jnp.where(first_el2, lanes_ref[2:3, :], lanes_ref[3:4, :])
+    lam_l = jnp.where(first_el2, par_ref[0:1, :], par_ref[1:2, :])
+    mu_l = jnp.where(first_el2, par_ref[2:3, :], par_ref[3:4, :])
     primal_stress = lam_l * both[:, 256:512] + mu_l * both[:, 0:256]
     unit = fdot(both[:, 0:256], tab[384:640, 0:384])
     full = fdot(primal_stress, tab[384:640, 0:384])
@@ -311,13 +318,19 @@
     for i in range(5):
         odd = i % 2
         grad[...] = bdot(fwd, uc[:, i * 1152 : (i + 1) * 1152])
-        lam_rows = jnp.where(first_el, par_ref[0, i], par_ref[0, 5 + i])
-        mu_rows = jnp.where(first_el, par_ref[1, i], par_ref[1, 5 + i])
+        lam_rows, mu_rows = (
+            jnp.where(
+                first_el,
+                *(
+                    jnp.broadcast_to(par_ref[r : r + 1, 36 * i : 36 * i + 1], (PTS, 128))
+                    for r in (q, q + 1)
+                ),
+            )
+            for q in (0, 2)
+        )
         edge[0:PTS, 0:128] = lam_rows
         edge[0:PTS, 128:256] = mu_rows
-        pick = [
-            jnp.where(dirs_ref[...] == cell_ref[0, 5 * e + i], 1.0, 0.0) for e in range(2)
-        ]
+        pick = [par_ref[8 + 5 * e + i : 9 + 5 * e + i, 0:128] for e in range(2)]
         for c in range(3):
             for m in range(3):
                 target = c * 6 + 2 * m + (1 - half40 if odd else half40)
@@ -441,7 +454,7 @@
     rx_ref[:, COLS:] = primal_step[80 : 80 + NY, :].astype(BF16)
     for x in range(NX):
         edge[x : x + 1, COLS:BACK] = primal_step[16 * x + NY : 16 * x + NY + 1, :]
-    rc_ref[:, COLS:] = primal_step[80 + NY : 81 + NY, :].astype(BF16)
+    rc_ref[:, COLS:] = jnp.broadcast_to(primal_step[80 + NY : 81 + NY, :], (CORNER, 128)).astype(BF16)
 
     ids = jnp.transpose(wide[:, COLS : COLS + 128])[96:128]
     ids = jnp.concatenate([ids, ids], axis=1)
@@ -474,9 +487,10 @@
     for x in range(NX):
         edge[x : x + 1, :COLS] = force[16 * x + NY : 16 * x + NY + 1, :]
     ry_ref[...] = edge[0:NX, 0:BACK].astype(BF16)
-    rc_ref[:, :COLS] = force[80 + NY : 81 + NY, :].astype(BF16)
+    rc_ref[:, :COLS] = jnp.broadcast_to(force[80 + NY : 81 + NY, :], (CORNER, COLS)).astype(BF16)
     amp[:, 0:64] = total[0:64, 0:64] + pltpu.roll(total[64:128, :], 64, 1)[:, 0:64]
     p_rows, p_cols = PORTS // n_y, 64 // n_x
+    share_ref[...] = jnp.zeros((n_x * n_y, SHARE), F32)
     for q in range(p_rows):
         mine = amp[pl.ds(q, n_y, stride=p_rows), :] if p_rows > 1 else amp[...]
         for a in range(n_x):
@@ -490,7 +504,7 @@
     for x in range(NX):
         row = ry_ref[x : x + 1, :].astype(F32)
         if x == 0:
-            row = row + rc_ref[...].astype(F32)
+            row = row + rc_ref[0:1, :].astype(F32)
         value = part_ref[x] + jnp.where(first, row, 0.0)
         if x == 0:
             value = value + rx_ref[...].astype(F32)
@@ -525,7 +539,6 @@
     tab = tables()
     nx_dev, ny_dev = lax.axis_size("gx"), lax.axis_size("gy")
     vmem = pl.BlockSpec(memory_space=pltpu.VMEM)
-    smem = pl.BlockSpec(memory_space=pltpu.SMEM)
     hbm = pl.BlockSpec(memory_space=pltpu.HBM)
     params = pltpu.CompilerParams(vmem_limit_bytes=VMEM_LIMIT)
 
@@ -542,55 +555,48 @@
         return lax.ppermute(block, ("gx", "gy"), step(shift_x, shift_y))
 
     by_comp = [a.transpose(0, 1, 3, 2) for a in (disp, port_mode, disp_prev, force)]
-    face_x, face_y, corner, small = pl.pallas_call(
+    raw = (tangent, by_comp[0], by_comp[1], node_mass, port_id, by_comp[2], by_comp[3])
+    raw += (lame_lambda, lame_mu, cell_block, direction_block.reshape(1, 64))
+    face_x, face_y, corner, small, own, par = pl.pallas_call(
         pack_kernel,
         out_shape=(
             jax.ShapeDtypeStruct((NY, WIDE), BF16),
             jax.ShapeDtypeStruct((NX, WIDE), BF16),
             jax.ShapeDtypeStruct((1, WIDE), BF16),
             jax.ShapeDtypeStruct((NX, NY, SMALL), BF16),
-        ),
-        in_specs=[hbm] * 5,
-        out_specs=(vmem,) * 4,
+            jax.ShapeDtypeStruct((2, NX, NY, 128), F32),
+            jax.ShapeDtypeStruct((24, 256), F32),
+        ),
+        in_specs=[hbm] * len(raw),
+        out_specs=(vmem,) * 6,
         scratch_shapes=[
             pltpu.VMEM((NX, 16, SMALL), F32),
             pltpu.VMEM((8, WIDE), F32),
-            pltpu.SemaphoreType.DMA((5,)),
-            pltpu.VMEM((NX, NY, COLS), BF16),
-            pltpu.VMEM((NX, NY, 3, NZ), BF16),
-            pltpu.VMEM((NX, NY, 3, NZ), BF16),
-            pltpu.VMEM((NX, NY, NZ), F32),
-            pltpu.VMEM((NX, NY, NZ), jnp.int32),
-        ],
+            pltpu.SemaphoreType.DMA((len(raw),)),
+        ]
+        + [pltpu.VMEM(a.shape, a.dtype) for a in raw],
         compiler_params=pltpu.CompilerParams(vmem_limit_bytes=VMEM_MOST),
-    )(tangent, by_comp[0], by_comp[1], node_mass, port_id)
+    )(*raw)
     halo_x = send(face_x, -1, 0)
     halo_y = send(face_y, 0, -1)
     halo_c = send(corner, -1, -1)
 
     wide_table, short_table = (jnp.asarray(a) for a in tab)
-    base, own, near, *near_tables = pl.pallas_call(
+    base, near, *near_tables = pl.pallas_call(
         local_kernel,
         out_shape=(
             jax.ShapeDtypeStruct((NX, NY, COLS), F32),
-            jax.ShapeDtypeStruct((2, NX, NY, 128), F32),
             jax.ShapeDtypeStruct((NX, NY, COLS), BF16),
             jax.ShapeDtypeStruct(wide_table.shape, F32),
             jax.ShapeDtypeStruct(short_table.shape, BF16),
         ),
-        in_specs=[vmem] * 7,
-        out_specs=(vmem,) * 5,
+        in_specs=[vmem] * 4,
+        out_specs=(vmem,) * 4,
         compiler_params=params,
         cost_estimate=pl.CostEstimate(
-            flops=LONG_FLOPS, bytes_accessed=LONG_BYTES, transcendentals=0
-        ),
-    )(tangent, tangent_prev, by_comp[0], by_comp[2], by_comp[3], wide_table, short_table)
-
-    par = jnp.stack([lame_lambda.reshape(10), lame_mu.reshape(10)]).astype(F32)
-    cells = cell_block.reshape(1, 10)
-    by_lane = jnp.repeat(par.reshape(4, 5), 36, axis=1)
-    by_lane = jnp.pad(by_lane, ((0, 0), (0, 76)))
-    dirs = jnp.concatenate([direction_block, direction_block]).reshape(1, 128)
+            flops=4000000, bytes_accessed=8000000, transcendentals=0
+        ),
+    )(tangent, tangent_prev, wide_table, short_table)
 
     part, ret_x, ret_y, ret_c, shares = pl.pallas_call(
         functools.partial(main_kernel, nx_dev, ny_dev),
@@ -598,11 +604,10 @@
             jax.ShapeDtypeStruct((NX, NY, BACK), F32),
             jax.ShapeDtypeStruct((NY, BACK), BF16),
             jax.ShapeDtypeStruct((NX, BACK), BF16),
-            jax.ShapeDtypeStruct((1, BACK), BF16),
-            jax.ShapeDtypeStruct((nx_dev * ny_dev, PORTS * 64 // (nx_dev * ny_dev)), F32),
-        ),
-        in_specs=[smem, smem]
-        + [vmem] * 11,
+            jax.ShapeDtypeStruct((CORNER, BACK), BF16),
+            jax.ShapeDtypeStruct((nx_dev * ny_dev, SHARE), F32),
+        ),
+        in_specs=[vmem] * 10,
         out_specs=(vmem,) * 5,
         scratch_shapes=[
             pltpu.VMEM((ROWS, WIDE), F32),
@@ -619,7 +624,6 @@
         ),
     )(
         par,
-        cells,
         near,
         base,
         own,
@@ -627,8 +631,6 @@
         halo_x,
         halo_y,
         halo_c,
-        by_lane,
-        dirs,
         *near_tables,
     )
 

time: 74 us -> 63.4 us (0.86)
  the two profiles are of different devices: /device:TPU:1 before, /device:TPU:225 now
where the time goes in v3:
time: 63.4 us; the launch traced here: 63 us
  starting transfers between devices  34.1 us (54%)
  Pallas kernels  13.7 us (22%)
  waiting for transfers between devices  9.69 us (15%)
  local copies, waits for them, and re-layouts  4.77 us (8%)
  between operations  0.74 us (1%)
    ppermute x6, starting transfers between devices, send(): return lax.ppermute(block, ('gx', 'gy'), step(shift_x, shift_y))  22.2 us
    all_to_all x1, starting transfers between devices, per_device(): shares = lax.all_to_all(shares, ('gx', 'gy'), 0, 0)  11.9 us
    ppermute x6, waiting for transfers between devices, send(): return lax.ppermute(block, ('gx', 'gy'), step(shift_x, shift_y))  9.69 us
    pallas_call x1, Pallas kernels, per_device(): pl.pallas_call(functools.partial(main_kernel, nx_dev, ny_dev), out_shape=...  9.07 us
    unnamed x14, local copies, waits for them, and re-layouts  4.77 us
    pallas_call x1, Pallas kernels, per_device(): pl.pallas_call(pack_kernel, out_shape=(jax.ShapeDtypeStruct((NY, WIDE), B...  2.32 us
  transfers between devices with their start and end apart: 7, of which 2 were waited for; matrix products, arithmetic and copies ran while one was open for 0% of the time, Pallas kernels for 2%

profile of v3, /device:TPU:225, one launch (start us, length us, event | category | flops | bytes accessed | tf_op | source)
XLA Modules:
  0.0 63.0 jit_solution(5687423350890174274)
XLA Ops:
  0.6 2.3 %shard_map.157 = (bf16[10,5376]{1,0:T(8,128)(2,1)}, bf16[5,5376]{1,0:T(8,128)(2,1)}, bf16[1,5376]{1,0:T(2,128)(2,1)}, bf16[5,10,384]{2,1,0:T(8,128)(2,1)}, f32[2,5,10,128]{3,2,1,0:T(8,128)}, /*index=5*/f32[24,256]{1,0:T(8,128)}) custom-call(bf16[5,10,4992]{2,1,0:T(8,128)(2,1)} %t_ref.1, bf16[5,10,3,26]{3,2,1,0:T(4,128)(2,1)} %bitcast.11, ...), custom_call_target="tpu_custom_call" | custom-call | tf_op jit(solution)/shard_map/pallas_call | solution.py:560
  3.0 5.5 %collective-permute-start = (bf16[10,5376]{1,0:T(8,128)(2,1)}, bf16[10,5376]{1,0:T(8,128)(2,1)S(1)}, u32[]{:S(2)}, u32[]{:S(2)}) collective-permute-start(bf16[10,5376]{1,0:T(8,128)(2,1)} %get-tuple-element.27), channel_id=1, source_target_pairs={{32,0},{33,1},{34,2},{35,3},{36,4},{37,5},{38,6},{39,7},{40,8},{41... | collective-permute-start | bytes 322568 | tf_op jit(solution)/shard_map/ppermute | solution.py:555
  8.5 2.9 %collective-permute-start.1 = (bf16[5,5376]{1,0:T(8,128)(2,1)}, bf16[5,5376]{1,0:T(8,128)(2,1)S(1)}, u32[]{:S(2)}, u32[]{:S(2)}) collective-permute-start(bf16[5,5376]{1,0:T(8,128)(2,1)} %get-tuple-element.28), channel_id=1, source_target_pairs={{1,0},{2,1},{3,2},{4,3},{5,4},{6,5},{7,6},{8,7},{9,8},{10,9},{11,1... | collective-permute-start | bytes 161288 | tf_op jit(solution)/shard_map/ppermute | solution.py:555
  11.4 2.3 %collective-permute-start.2 = (bf16[1,5376]{1,0:T(2,128)(2,1)}, bf16[1,5376]{1,0:T(2,128)(2,1)S(1)}, u32[]{:S(2)}, u32[]{:S(2)}) collective-permute-start(bf16[1,5376]{1,0:T(2,128)(2,1)} %get-tuple-element.29), channel_id=1, source_target_pairs={{33,0},{34,1},{35,2},{36,3},{37,4},{38,5},{39,6},{40,7},{41,8},{42... | collective-permute-start | bytes 32264 | tf_op jit(solution)/shard_map/ppermute | solution.py:555
  13.6 0.0 copy-start
  13.6 1.1 %copy-done = bf16[5,10,4992]{2,1,0:T(8,128)(2,1)S(1)} copy-done((bf16[5,10,4992]{2,1,0:T(8,128)(2,1)S(1)}, bf16[5,10,4992]{2,1,0:T(8,128)(2,1)}, u32[]{:S(2)}) %copy-start) | copy-done | bytes 499224
  14.8 0.0 copy-start.1
  14.8 1.5 %copy-done.1 = f32[952,512]{1,0:T(8,128)S(1)} copy-done((f32[952,512]{1,0:T(8,128)S(1)}, f32[952,512]{1,0:T(8,128)}, u32[]{:S(2)}) %copy-start.1) | copy-done | bytes 1949720
  16.3 0.0 copy-start.2
  16.3 1.1 %copy-done.2 = bf16[5,10,4992]{2,1,0:T(8,128)(2,1)S(1)} copy-done((bf16[5,10,4992]{2,1,0:T(8,128)(2,1)S(1)}, bf16[5,10,4992]{2,1,0:T(8,128)(2,1)}, u32[]{:S(2)}) %copy-start.2) | copy-done | bytes 499224
  17.5 0.0 copy-start.3
  17.5 1.0 %copy-done.3 = bf16[544,256]{1,0:T(8,128)(2,1)S(1)} copy-done((bf16[544,256]{1,0:T(8,128)(2,1)S(1)}, bf16[544,256]{1,0:T(8,128)(2,1)}, u32[]{:S(2)}) %copy-start.3) | copy-done | bytes 278552
  18.4 0.0 copy-start.4
  18.4 0.0 copy-start.5
  18.4 0.4 shard_map.158
  18.8 1.5 %collective-permute-done.2.hc_ref = bf16[1,5376]{1,0:T(2,128)(2,1)S(1)} collective-permute-done((bf16[1,5376]{1,0:T(2,128)(2,1)}, bf16[1,5376]{1,0:T(2,128)(2,1)S(1)}, u32[]{:S(2)}, u32[]{:S(2)}) %collective-permute-start.2) | collective-permute-done | bytes 10784 | tf_op jit(solution)/shard_map/ppermute | solution.py:555
  20.3 0.0 collective-permute-done.1.hy_ref
  20.3 0.0 collective-permute-done.hx_ref
  20.3 0.0 copy-done.4
  20.3 0.0 copy-done.5
  20.3 0.0 copy-done.6
  20.3 9.1 %shard_map.159 = (f32[5,10,5120]{2,1,0:T(8,128)S(1)}, bf16[10,5120]{1,0:T(8,128)(2,1)S(1)}, bf16[5,5120]{1,0:T(8,128)(2,1)S(1)}, bf16[1,5120]{1,0:T(2,128)(2,1)S(1)}, f32[256,64]{1,0:T(8,128)}) custom-call(f32[24,256]{1,0:T(8,128)S(1)} %copy-done.6, bf16[5,10,4992]{2,1,0:T(8,128)(2,1)S(1)} %get-tuple-element.23.t_ref, ...), custom_call_target="tpu_custom_call" | custom-call | flops 400000000 | bytes 8000000 | tf_op jit(solution)/shard_map/pallas_call | solution.py:601
  29.4 11.9 %all-to-all-start = ((f32[256,1,64]{2,1,0:T(1,128)}), f32[256,1,64]{2,1,0:T(1,128)S(1)}, u32[]{:S(2)}, u32[]{:S(2)}) async-start(f32[256,1,64]{2,1,0:T(1,128)} %bitcast.6), calls=%async_computation | async-start | bytes 262144 | tf_op jit(solution)/shard_map/all_to_all | solution.py:638
  41.2 3.2 %collective-permute-start.3 = (bf16[10,5120]{1,0:T(8,128)(2,1)S(1)}, bf16[10,5120]{1,0:T(8,128)(2,1)S(1)}, u32[]{:S(2)}, u32[]{:S(2)}) collective-permute-start(bf16[10,5120]{1,0:T(8,128)(2,1)S(1)} %get-tuple-element.34), channel_id=1, source_target_pairs={{0,32},{1,33},{2,34},{3,35},{4,36},{5,37},{6,38},{7,39},{8,40},{9,... | collective-permute-start | bytes 307208 | tf_op jit(solution)/shard_map/ppermute | solution.py:555
  44.4 5.5 %collective-permute-start.4 = (bf16[5,5120]{1,0:T(8,128)(2,1)S(1)}, bf16[5,5120]{1,0:T(8,128)(2,1)S(1)}, u32[]{:S(2)}, u32[]{:S(2)}) collective-permute-start(bf16[5,5120]{1,0:T(8,128)(2,1)S(1)} %get-tuple-element.35), channel_id=1, source_target_pairs={{0,1},{1,2},{2,3},{3,4},{4,5},{5,6},{6,7},{7,8},{8,9},{9,10},{10,1... | collective-permute-start | bytes 153608 | tf_op jit(solution)/shard_map/ppermute | solution.py:555
  49.9 2.9 %collective-permute-start.5 = (bf16[1,5120]{1,0:T(2,128)(2,1)S(1)}, bf16[1,5120]{1,0:T(2,128)(2,1)S(1)}, u32[]{:S(2)}, u32[]{:S(2)}) collective-permute-start(bf16[1,5120]{1,0:T(2,128)(2,1)S(1)} %get-tuple-element.36), channel_id=1, source_target_pairs={{0,33},{1,34},{2,35},{3,36},{4,37},{5,38},{6,39},{7,40},{8,41},{9,... | collective-permute-start | bytes 30728 | tf_op jit(solution)/shard_map/ppermute | solution.py:555
  52.8 8.2 %collective-permute-done.5.rc_ref = bf16[1,5120]{1,0:T(2,128)(2,1)S(1)} collective-permute-done((bf16[1,5120]{1,0:T(2,128)(2,1)S(1)}, bf16[1,5120]{1,0:T(2,128)(2,1)S(1)}, u32[]{:S(2)}, u32[]{:S(2)}) %collective-permute-start.5) | collective-permute-done | bytes 10272 | tf_op jit(solution)/shard_map/ppermute | solution.py:555
  61.1 0.0 collective-permute-done.4.ry_ref
  61.1 0.0 collective-permute-done.3.rx_ref
  61.1 1.1 %shard_map.160 = (bf16[5,10,4992]{2,1,0:T(8,128)(2,1)}, f32[5,10,128]{2,1,0:T(8,128)S(1)}) custom-call(f32[5,10,5120]{2,1,0:T(8,128)S(1)} %get-tuple-element.33.part_ref, bf16[10,5120]{1,0:T(8,128)(2,1)S(1)} %collective-permute-done.3.rx_ref, bf16[5,5120]{1,0:T(8,128)(2,1)S(1)} %collective-permute-done.4.ry_ref, ...), custom_call_target="tpu_custom_call" | custom-call | flops 4000000 | bytes 8000000 | tf_op jit(solution)/shard_map/pallas_call | solution.py:643
  62.1 0.0 all-to-all-done
  62.1 0.8 %shard_map.161 = (f32[2,8]{1,0:T(2,128)}, bf16[5,10,3,26]{3,2,1,0:T(4,128)(2,1)}) custom-call(f32[256,64]{1,0:T(8,128)S(1)} %bitcast.10, f32[5,10,128]{2,1,0:T(8,128)S(1)} %get-tuple-element.37.d_ref), custom_call_target="tpu_custom_call" | custom-call | tf_op jit(solution)/shard_map/pallas_call | solution.py:654
  (1 shorter events, 0.0 us)
Async XLA Ops:
  3.0 17.3 %collective-permute-start = (bf16[10,5376]{1,0:T(8,128)(2,1)}, bf16[10,5376]{1,0:T(8,128)(2,1)S(1)}, u32[]{:S(2)}, u32[]{:S(2)}) collective-permute-start(bf16[10,5376]{1,0:T(8,128)(2,1)} %get-tuple-element.27), channel_id=1, source_target_pairs={{32,0},{33,1},{34,2},{35,3},{36,4},{37,5},{38,6},{39,7},{40,8},{41... | collective-permute-start | bytes 322568 | tf_op jit(solution)/shard_map/ppermute | solution.py:555
  8.5 11.8 %collective-permute-start.1 = (bf16[5,5376]{1,0:T(8,128)(2,1)}, bf16[5,5376]{1,0:T(8,128)(2,1)S(1)}, u32[]{:S(2)}, u32[]{:S(2)}) collective-permute-start(bf16[5,5376]{1,0:T(8,128)(2,1)} %get-tuple-element.28), channel_id=1, source_target_pairs={{1,0},{2,1},{3,2},{4,3},{5,4},{6,5},{7,6},{8,7},{9,8},{10,9},{11,1... | collective-permute-start | bytes 161288 | tf_op jit(solution)/shard_map/ppermute | solution.py:555
  11.4 8.9 %collective-permute-start.2 = (bf16[1,5376]{1,0:T(2,128)(2,1)}, bf16[1,5376]{1,0:T(2,128)(2,1)S(1)}, u32[]{:S(2)}, u32[]{:S(2)}) collective-permute-start(bf16[1,5376]{1,0:T(2,128)(2,1)} %get-tuple-element.29), channel_id=1, source_target_pairs={{33,0},{34,1},{35,2},{36,3},{37,4},{38,5},{39,6},{40,7},{41,8},{42... | collective-permute-start | bytes 32264 | tf_op jit(solution)/shard_map/ppermute | solution.py:555
  13.6 1.1 %copy-start = (bf16[5,10,4992]{2,1,0:T(8,128)(2,1)S(1)}, bf16[5,10,4992]{2,1,0:T(8,128)(2,1)}, u32[]{:S(2)}) copy-start(bf16[5,10,4992]{2,1,0:T(8,128)(2,1)} %t_ref.1) | copy-start | bytes 1497604
  14.8 1.5 %copy-start.1 = (f32[952,512]{1,0:T(8,128)S(1)}, f32[952,512]{1,0:T(8,128)}, u32[]{:S(2)}) copy-start(f32[952,512]{1,0:T(8,128)} %constant.4.clone.wide_in) | copy-start | bytes 5849092
  16.3 1.1 %copy-start.2 = (bf16[5,10,4992]{2,1,0:T(8,128)(2,1)S(1)}, bf16[5,10,4992]{2,1,0:T(8,128)(2,1)}, u32[]{:S(2)}) copy-start(bf16[5,10,4992]{2,1,0:T(8,128)(2,1)} %tp_ref.1) | copy-start | bytes 1497604
  17.5 1.0 %copy-start.3 = (bf16[544,256]{1,0:T(8,128)(2,1)S(1)}, bf16[544,256]{1,0:T(8,128)(2,1)}, u32[]{:S(2)}) copy-start(bf16[544,256]{1,0:T(8,128)(2,1)} %constant.5.clone.short_in) | copy-start | bytes 835588
  18.4 1.9 %copy-start.4 = (f32[2,5,10,128]{3,2,1,0:T(8,128)S(1)}, f32[2,5,10,128]{3,2,1,0:T(8,128)}, u32[]{:S(2)}) copy-start(f32[2,5,10,128]{3,2,1,0:T(8,128)} %get-tuple-element.25.own_ref) | copy-start | bytes 153604
  18.4 1.9 %copy-start.5 = (bf16[5,10,384]{2,1,0:T(8,128)(2,1)S(1)}, bf16[5,10,384]{2,1,0:T(8,128)(2,1)}, u32[]{:S(2)}) copy-start(bf16[5,10,384]{2,1,0:T(8,128)(2,1)} %get-tuple-element.26.s_ref) | copy-start | bytes 115204
  18.4 1.9 %copy-start.6 = (f32[24,256]{1,0:T(8,128)S(1)}, f32[24,256]{1,0:T(8,128)}, u32[]{:S(2)}) copy-start(f32[24,256]{1,0:T(8,128)} %get-tuple-element.22.par_ref) | copy-start | bytes 73732
  29.4 32.8 %all-to-all-start = ((f32[256,1,64]{2,1,0:T(1,128)}), f32[256,1,64]{2,1,0:T(1,128)S(1)}, u32[]{:S(2)}, u32[]{:S(2)}) async-start(f32[256,1,64]{2,1,0:T(1,128)} %bitcast.6), calls=%async_computation | async-start | bytes 262144 | tf_op jit(solution)/shard_map/all_to_all | solution.py:638
  41.2 19.8 %collective-permute-start.3 = (bf16[10,5120]{1,0:T(8,128)(2,1)S(1)}, bf16[10,5120]{1,0:T(8,128)(2,1)S(1)}, u32[]{:S(2)}, u32[]{:S(2)}) collective-permute-start(bf16[10,5120]{1,0:T(8,128)(2,1)S(1)} %get-tuple-element.34), channel_id=1, source_target_pairs={{0,32},{1,33},{2,34},{3,35},{4,36},{5,37},{6,38},{7,39},{8,40},{9,... | collective-permute-start | bytes 307208 | tf_op jit(solution)/shard_map/ppermute | solution.py:555
  44.4 16.7 %collective-permute-start.4 = (bf16[5,5120]{1,0:T(8,128)(2,1)S(1)}, bf16[5,5120]{1,0:T(8,128)(2,1)S(1)}, u32[]{:S(2)}, u32[]{:S(2)}) collective-permute-start(bf16[5,5120]{1,0:T(8,128)(2,1)S(1)} %get-tuple-element.35), channel_id=1, source_target_pairs={{0,1},{1,2},{2,3},{3,4},{4,5},{5,6},{6,7},{7,8},{8,9},{9,10},{10,1... | collective-permute-start | bytes 153608 | tf_op jit(solution)/shard_map/ppermute | solution.py:555
  49.9 11.1 %collective-permute-start.5 = (bf16[1,5120]{1,0:T(2,128)(2,1)S(1)}, bf16[1,5120]{1,0:T(2,128)(2,1)S(1)}, u32[]{:S(2)}, u32[]{:S(2)}) collective-permute-start(bf16[1,5120]{1,0:T(2,128)(2,1)S(1)} %get-tuple-element.36), channel_id=1, source_target_pairs={{0,33},{1,34},{2,35},{3,36},{4,37},{5,38},{6,39},{7,40},{8,41},{9,... | collective-permute-start | bytes 30728 | tf_op jit(solution)/shard_map/ppermute | solution.py:555

commit v4 on v3

--- a/solution.py
+++ b/solution.py
@@ -37,8 +37,7 @@
 VMEM_LIMIT = 24 * 1024 * 1024
 VMEM_MOST = 60 * 1024 * 1024
 UNROLL = 9
-CORNER = 1
-SHARE = 64
+SHARE = 32
 
 
 def derivative_table():
@@ -247,8 +246,8 @@
     *rest,
 ):
     tab, short = rest[0:2]
-    part_ref, rx_ref, ry_ref, rc_ref, share_ref = rest[2:7]
-    (wide, uc, grad, stress, force, edge, amp) = rest[7:]
+    part_ref, rx_ref, ry_ref, share_ref = rest[2:6]
+    (wide, uc, grad, stress, force, edge, amp) = rest[6:]
 
     for x in range(NX):
         wide[16 * x + 8 : 16 * x + 16, :] = jnp.zeros((8, WIDE), F32)
@@ -451,10 +450,9 @@
             + own_ref[0, x]
             + rate[16 * x : 16 * x + NY, :] * own_ref[1, x]
         )
-    rx_ref[:, COLS:] = primal_step[80 : 80 + NY, :].astype(BF16)
+    rx_ref[:, COLS:] = primal_step[80 : 81 + NY, :].astype(BF16)
     for x in range(NX):
         edge[x : x + 1, COLS:BACK] = primal_step[16 * x + NY : 16 * x + NY + 1, :]
-    rc_ref[:, COLS:] = jnp.broadcast_to(primal_step[80 + NY : 81 + NY, :], (CORNER, 128)).astype(BF16)
 
     ids = jnp.transpose(wide[:, COLS : COLS + 128])[96:128]
     ids = jnp.concatenate([ids, ids], axis=1)
@@ -483,14 +481,13 @@
         ]
         left = jnp.concatenate(picked, axis=0).astype(BF16)
         total = total + bdot(left, jnp.concatenate([high, low], axis=0))
-    rx_ref[:, :COLS] = force[80 : 80 + NY, :].astype(BF16)
+    rx_ref[:, :COLS] = force[80 : 81 + NY, :].astype(BF16)
     for x in range(NX):
         edge[x : x + 1, :COLS] = force[16 * x + NY : 16 * x + NY + 1, :]
     ry_ref[...] = edge[0:NX, 0:BACK].astype(BF16)
-    rc_ref[:, :COLS] = jnp.broadcast_to(force[80 + NY : 81 + NY, :], (CORNER, COLS)).astype(BF16)
     amp[:, 0:64] = total[0:64, 0:64] + pltpu.roll(total[64:128, :], 64, 1)[:, 0:64]
     p_rows, p_cols = PORTS // n_y, 64 // n_x
-    share_ref[...] = jnp.zeros((n_x * n_y, SHARE), F32)
+    share_ref[...] = jnp.zeros(share_ref.shape, F32)
     for q in range(p_rows):
         mine = amp[pl.ds(q, n_y, stride=p_rows), :] if p_rows > 1 else amp[...]
         for a in range(n_x):
@@ -499,15 +496,21 @@
             ]
 
 
-def last_kernel(part_ref, rx_ref, ry_ref, rc_ref, t_ref, d_ref):
+def relay_kernel(rx_ref, ry_ref, out_ref, rows):
+    rows[0:NX, :] = ry_ref[...].astype(F32)
+    rows[NX : NX + 1, :] = rx_ref[NY : NY + 1, :].astype(F32)
+    out_ref[...] = rows[0 : NX + 1, :].astype(BF16)
+
+
+def last_kernel(part_ref, rx_ref, ry_ref, t_ref, d_ref):
     first = lax.broadcasted_iota(jnp.int32, (NY, BACK), 0) == 0
     for x in range(NX):
         row = ry_ref[x : x + 1, :].astype(F32)
         if x == 0:
-            row = row + rc_ref[0:1, :].astype(F32)
+            row = row + ry_ref[NX : NX + 1, :].astype(F32)
         value = part_ref[x] + jnp.where(first, row, 0.0)
         if x == 0:
-            value = value + rx_ref[...].astype(F32)
+            value = value + rx_ref[0:NY, :].astype(F32)
         t_ref[x] = value[:, :COLS].astype(BF16)
         d_ref[x] = value[:, COLS:]
 
@@ -537,6 +540,7 @@
     port_mode,
 ):
     tab = tables()
+    share_lanes = max(SHARE, PORTS * 64 // (lax.axis_size("gx") * lax.axis_size("gy")))
     nx_dev, ny_dev = lax.axis_size("gx"), lax.axis_size("gy")
     vmem = pl.BlockSpec(memory_space=pltpu.VMEM)
     hbm = pl.BlockSpec(memory_space=pltpu.HBM)
@@ -598,17 +602,16 @@
         ),
     )(tangent, tangent_prev, wide_table, short_table)
 
-    part, ret_x, ret_y, ret_c, shares = pl.pallas_call(
+    part, ret_x, ret_y, shares = pl.pallas_call(
         functools.partial(main_kernel, nx_dev, ny_dev),
         out_shape=(
             jax.ShapeDtypeStruct((NX, NY, BACK), F32),
-            jax.ShapeDtypeStruct((NY, BACK), BF16),
+            jax.ShapeDtypeStruct((NY + 1, BACK), BF16),
             jax.ShapeDtypeStruct((NX, BACK), BF16),
-            jax.ShapeDtypeStruct((CORNER, BACK), BF16),
-            jax.ShapeDtypeStruct((nx_dev * ny_dev, SHARE), F32),
+            jax.ShapeDtypeStruct((nx_dev * ny_dev, share_lanes), F32),
         ),
         in_specs=[vmem] * 10,
-        out_specs=(vmem,) * 5,
+        out_specs=(vmem,) * 4,
         scratch_shapes=[
             pltpu.VMEM((ROWS, WIDE), F32),
             pltpu.VMEM((2 * ROWS, 5 * 1152), BF16),
@@ -636,9 +639,17 @@
 
     port_rows, port_cols = PORTS // ny_dev, 64 // nx_dev
     shares = lax.all_to_all(shares, ("gx", "gy"), 0, 0)
-    back_c = send(ret_c, 1, 1)
-    back_y = send(ret_y, 0, 1)
     back_x = send(ret_x, 1, 0)
+    onward = pl.pallas_call(
+        relay_kernel,
+        out_shape=jax.ShapeDtypeStruct((NX + 1, BACK), BF16),
+        in_specs=[vmem, vmem],
+        out_specs=vmem,
+        scratch_shapes=[pltpu.VMEM((8, BACK), F32)],
+        compiler_params=params,
+        cost_estimate=pl.CostEstimate(flops=100000, bytes_accessed=200000, transcendentals=0),
+    )(back_x, ret_y)
+    back_y = send(onward, 0, 1)
 
     tangent_next, disp_wide = pl.pallas_call(
         last_kernel,
@@ -646,11 +657,11 @@
             jax.ShapeDtypeStruct((NX, NY, COLS), BF16),
             jax.ShapeDtypeStruct((NX, NY, 128), F32),
         ),
-        in_specs=[vmem] * 4,
+        in_specs=[vmem] * 3,
         out_specs=(vmem, vmem),
         compiler_params=params,
         cost_estimate=pl.CostEstimate(flops=4000000, bytes_accessed=8000000, transcendentals=0),
-    )(part, back_x, back_y, back_c)
+    )(part, back_x, back_y)
     port_amp, disp_next = pl.pallas_call(
         functools.partial(final_kernel, port_rows, port_cols),
         out_shape=(

time: 63.4 us -> 61.6 us (0.972)
  the two profiles are of different devices: /device:TPU:225 before, /device:TPU:1 now
where the time goes in v4:
time: 61.6 us; the launch traced here: 61.2 us
  starting transfers between devices  33.5 us (54%)
  Pallas kernels  13.8 us (22%)
  waiting for transfers between devices  7.98 us (13%)
  local copies, waits for them, and re-layouts  5.23 us (8%)
  between operations  0.75 us (1%)
    all_to_all x1, starting transfers between devices, per_device(): shares = lax.all_to_all(shares, ('gx', 'gy'), 0, 0)  17.2 us
    ppermute x5, starting transfers between devices, send(): return lax.ppermute(block, ('gx', 'gy'), step(shift_x, shift_y))  16.3 us
    pallas_call x1, Pallas kernels, per_device(): pl.pallas_call(functools.partial(main_kernel, nx_dev, ny_dev), out_shape=...  9.1 us
    all_to_all x1, waiting for transfers between devices, per_device(): shares = lax.all_to_all(shares, ('gx', 'gy'), 0, 0)  5.87 us
    unnamed x14, local copies, waits for them, and re-layouts  5.23 us
    pallas_call x1, Pallas kernels, per_device(): pl.pallas_call(pack_kernel, out_shape=(jax.ShapeDtypeStruct((NY, WIDE), B...  2.35 us
    ppermute x5, waiting for transfers between devices, send(): return lax.ppermute(block, ('gx', 'gy'), step(shift_x, shift_y))  2.11 us
  transfers between devices with their start and end apart: 6, of which 2 were waited for; matrix products, arithmetic and copies ran while one was open for 0% of the time, Pallas kernels for 2%

profile of v4, /device:TPU:1, one launch (start us, length us, event | category | flops | bytes accessed | tf_op | source)
XLA Modules:
  0.0 61.2 jit_solution(13003185536183878421)
XLA Ops:
  0.6 2.3 %shard_map.157 = (bf16[10,5376]{1,0:T(8,128)(2,1)}, bf16[5,5376]{1,0:T(8,128)(2,1)}, bf16[1,5376]{1,0:T(2,128)(2,1)}, bf16[5,10,384]{2,1,0:T(8,128)(2,1)}, f32[2,5,10,128]{3,2,1,0:T(8,128)}, /*index=5*/f32[24,256]{1,0:T(8,128)}) custom-call(bf16[5,10,4992]{2,1,0:T(8,128)(2,1)} %t_ref.1, bf16[5,10,3,26]{3,2,1,0:T(4,128)(2,1)} %bitcast.11, ...), custom_call_target="tpu_custom_call" | custom-call | tf_op jit(solution)/shard_map/pallas_call | solution.py:564
  3.0 1.3 %collective-permute-start = (bf16[10,5376]{1,0:T(8,128)(2,1)}, bf16[10,5376]{1,0:T(8,128)(2,1)S(1)}, u32[]{:S(2)}, u32[]{:S(2)}) collective-permute-start(bf16[10,5376]{1,0:T(8,128)(2,1)} %get-tuple-element.26), channel_id=1, source_target_pairs={{32,0},{33,1},{34,2},{35,3},{36,4},{37,5},{38,6},{39,7},{40,8},{41... | collective-permute-start | bytes 322568 | tf_op jit(solution)/shard_map/ppermute | solution.py:559
  4.3 5.1 %collective-permute-start.1 = (bf16[5,5376]{1,0:T(8,128)(2,1)}, bf16[5,5376]{1,0:T(8,128)(2,1)S(1)}, u32[]{:S(2)}, u32[]{:S(2)}) collective-permute-start(bf16[5,5376]{1,0:T(8,128)(2,1)} %get-tuple-element.27), channel_id=1, source_target_pairs={{1,0},{2,1},{3,2},{4,3},{5,4},{6,5},{7,6},{8,7},{9,8},{10,9},{11,1... | collective-permute-start | bytes 161288 | tf_op jit(solution)/shard_map/ppermute | solution.py:559
  9.4 1.3 %collective-permute-start.2 = (bf16[1,5376]{1,0:T(2,128)(2,1)}, bf16[1,5376]{1,0:T(2,128)(2,1)S(1)}, u32[]{:S(2)}, u32[]{:S(2)}) collective-permute-start(bf16[1,5376]{1,0:T(2,128)(2,1)} %get-tuple-element.28), channel_id=1, source_target_pairs={{33,0},{34,1},{35,2},{36,3},{37,4},{38,5},{39,6},{40,7},{41,8},{42... | collective-permute-start | bytes 32264 | tf_op jit(solution)/shard_map/ppermute | solution.py:559
  10.7 0.0 copy-start
  10.8 1.1 %copy-done = bf16[5,10,4992]{2,1,0:T(8,128)(2,1)S(1)} copy-done((bf16[5,10,4992]{2,1,0:T(8,128)(2,1)S(1)}, bf16[5,10,4992]{2,1,0:T(8,128)(2,1)}, u32[]{:S(2)}) %copy-start) | copy-done | bytes 499224
  11.9 0.0 copy-start.1
  11.9 1.5 %copy-done.1 = f32[952,512]{1,0:T(8,128)S(1)} copy-done((f32[952,512]{1,0:T(8,128)S(1)}, f32[952,512]{1,0:T(8,128)}, u32[]{:S(2)}) %copy-start.1) | copy-done | bytes 1949720
  13.4 0.0 copy-start.2
  13.4 1.1 %copy-done.2 = bf16[5,10,4992]{2,1,0:T(8,128)(2,1)S(1)} copy-done((bf16[5,10,4992]{2,1,0:T(8,128)(2,1)S(1)}, bf16[5,10,4992]{2,1,0:T(8,128)(2,1)}, u32[]{:S(2)}) %copy-start.2) | copy-done | bytes 499224
  14.6 0.0 copy-start.3
  14.6 1.0 %copy-done.3 = bf16[544,256]{1,0:T(8,128)(2,1)S(1)} copy-done((bf16[544,256]{1,0:T(8,128)(2,1)S(1)}, bf16[544,256]{1,0:T(8,128)(2,1)}, u32[]{:S(2)}) %copy-start.3) | copy-done | bytes 278552
  15.5 0.0 copy-start.4
  15.5 0.0 copy-start.5
  15.5 0.0 copy-start.6
  15.5 0.4 shard_map.158
  15.9 0.0 collective-permute-done.2.hc_ref
  15.9 0.0 collective-permute-done.1.hy_ref
  15.9 0.0 collective-permute-done.hx_ref
  16.0 0.5 copy-done.4
  16.4 0.0 copy-done.5
  16.4 0.0 copy-done.6
  16.4 9.1 %shard_map.159 = (f32[5,10,5120]{2,1,0:T(8,128)S(1)}, bf16[11,5120]{1,0:T(8,128)(2,1)S(1)}, bf16[5,5120]{1,0:T(8,128)(2,1)S(1)}, f32[256,32]{1,0:T(8,128)}) custom-call(f32[24,256]{1,0:T(8,128)S(1)} %copy-done.6, bf16[5,10,4992]{2,1,0:T(8,128)(2,1)S(1)} %get-tuple-element.22.t_ref, f32[5,10,4992]{2,1,0:T(8,128)S(1)} %get-tuple-element.23.base_ref, ...), custom_call_target="tpu_custom_call" | custom-call | flops 400000000 | bytes 8000000 | tf_op jit(solution)/shard_map/pallas_call | solution.py:605
  25.5 4.9 %collective-permute-start.3 = (bf16[11,5120]{1,0:T(8,128)(2,1)S(1)}, bf16[11,5120]{1,0:T(8,128)(2,1)S(1)}, u32[]{:S(2)}, u32[]{:S(2)}) collective-permute-start(bf16[11,5120]{1,0:T(8,128)(2,1)S(1)} %get-tuple-element.33), channel_id=1, source_target_pairs={{0,32},{1,33},{2,34},{3,35},{4,36},{5,37},{6,38},{7,39},{8,40},{9,... | collective-permute-start | bytes 337928 | tf_op jit(solution)/shard_map/ppermute | solution.py:559
  30.4 17.2 %all-to-all-start = ((f32[256,1,32]{2,1,0:T(1,128)}), f32[256,1,32]{2,1,0:T(1,128)S(1)}, u32[]{:S(2)}, u32[]{:S(2)}) async-start(f32[256,1,32]{2,1,0:T(1,128)} %bitcast.6), calls=%async_computation | async-start | bytes 262144 | tf_op jit(solution)/shard_map/all_to_all | solution.py:641
  47.6 0.0 collective-permute-done.3.rx_ref
  47.6 3.7 %collective-permute-start.4 = (bf16[6,5120]{1,0:T(8,128)(2,1)S(1)}, bf16[6,5120]{1,0:T(8,128)(2,1)S(1)}, u32[]{:S(2)}, u32[]{:S(2)}) collective-permute-start(bf16[6,5120]{1,0:T(8,128)(2,1)S(1)} %shard_map.160), channel_id=1, source_target_pairs={{0,1},{1,2},{2,3},{3,4},{4,5},{5,6},{6,7},{7,8},{8,9},{9,10},{10,1... | collective-permute-start | bytes 184328 | tf_op jit(solution)/shard_map/ppermute | solution.py:559
  51.3 2.1 %collective-permute-done.4.ry_ref = bf16[6,5120]{1,0:T(8,128)(2,1)S(1)} collective-permute-done((bf16[6,5120]{1,0:T(8,128)(2,1)S(1)}, bf16[6,5120]{1,0:T(8,128)(2,1)S(1)}, u32[]{:S(2)}, u32[]{:S(2)}) %collective-permute-start.4) | collective-permute-done | bytes 61472 | tf_op jit(solution)/shard_map/ppermute | solution.py:559
  53.4 1.1 %shard_map.161 = (bf16[5,10,4992]{2,1,0:T(8,128)(2,1)}, f32[5,10,128]{2,1,0:T(8,128)S(1)}) custom-call(f32[5,10,5120]{2,1,0:T(8,128)S(1)} %get-tuple-element.32.part_ref, bf16[11,5120]{1,0:T(8,128)(2,1)S(1)} %collective-permute-done.3.rx_ref, bf16[6,5120]{1,0:T(8,128)(2,1)S(1)} %collective-permute-done.4.ry_ref), custom_call_target="tpu_custom_call" | custom-call | flops 4000000 | bytes 8000000 | tf_op jit(solution)/shard_map/pallas_call | solution.py:654
  54.5 5.9 %all-to-all-done = f32[256,1,32]{2,1,0:T(1,128)S(1)} async-done(((f32[256,1,32]{2,1,0:T(1,128)}), f32[256,1,32]{2,1,0:T(1,128)S(1)}, u32[]{:S(2)}, u32[]{:S(2)}) %all-to-all-start) | async-done | bytes 32800 | tf_op jit(solution)/shard_map/all_to_all | solution.py:641
  60.4 0.8 %shard_map.162 = (f32[2,8]{1,0:T(2,128)}, bf16[5,10,3,26]{3,2,1,0:T(4,128)(2,1)}) custom-call(f32[256,32]{1,0:T(8,128)S(1)} %bitcast.10, f32[5,10,128]{2,1,0:T(8,128)S(1)} %get-tuple-element.35.d_ref), custom_call_target="tpu_custom_call" | custom-call | tf_op jit(solution)/shard_map/pallas_call | solution.py:665
  (1 shorter events, 0.0 us)
Async XLA Ops:
  3.0 13.0 %collective-permute-start = (bf16[10,5376]{1,0:T(8,128)(2,1)}, bf16[10,5376]{1,0:T(8,128)(2,1)S(1)}, u32[]{:S(2)}, u32[]{:S(2)}) collective-permute-start(bf16[10,5376]{1,0:T(8,128)(2,1)} %get-tuple-element.26), channel_id=1, source_target_pairs={{32,0},{33,1},{34,2},{35,3},{36,4},{37,5},{38,6},{39,7},{40,8},{41... | collective-permute-start | bytes 322568 | tf_op jit(solution)/shard_map/ppermute | solution.py:559
  4.3 11.6 %collective-permute-start.1 = (bf16[5,5376]{1,0:T(8,128)(2,1)}, bf16[5,5376]{1,0:T(8,128)(2,1)S(1)}, u32[]{:S(2)}, u32[]{:S(2)}) collective-permute-start(bf16[5,5376]{1,0:T(8,128)(2,1)} %get-tuple-element.27), channel_id=1, source_target_pairs={{1,0},{2,1},{3,2},{4,3},{5,4},{6,5},{7,6},{8,7},{9,8},{10,9},{11,1... | collective-permute-start | bytes 161288 | tf_op jit(solution)/shard_map/ppermute | solution.py:559
  9.4 6.5 %collective-permute-start.2 = (bf16[1,5376]{1,0:T(2,128)(2,1)}, bf16[1,5376]{1,0:T(2,128)(2,1)S(1)}, u32[]{:S(2)}, u32[]{:S(2)}) collective-permute-start(bf16[1,5376]{1,0:T(2,128)(2,1)} %get-tuple-element.28), channel_id=1, source_target_pairs={{33,0},{34,1},{35,2},{36,3},{37,4},{38,5},{39,6},{40,7},{41,8},{42... | collective-permute-start | bytes 32264 | tf_op jit(solution)/shard_map/ppermute | solution.py:559
  10.7 1.1 %copy-start = (bf16[5,10,4992]{2,1,0:T(8,128)(2,1)S(1)}, bf16[5,10,4992]{2,1,0:T(8,128)(2,1)}, u32[]{:S(2)}) copy-start(bf16[5,10,4992]{2,1,0:T(8,128)(2,1)} %t_ref.1) | copy-start | bytes 1497604
  11.9 1.5 %copy-start.1 = (f32[952,512]{1,0:T(8,128)S(1)}, f32[952,512]{1,0:T(8,128)}, u32[]{:S(2)}) copy-start(f32[952,512]{1,0:T(8,128)} %constant.4.clone.wide_in) | copy-start | bytes 5849092
  13.4 1.1 %copy-start.2 = (bf16[5,10,4992]{2,1,0:T(8,128)(2,1)S(1)}, bf16[5,10,4992]{2,1,0:T(8,128)(2,1)}, u32[]{:S(2)}) copy-start(bf16[5,10,4992]{2,1,0:T(8,128)(2,1)} %tp_ref.1) | copy-start | bytes 1497604
  14.6 1.0 %copy-start.3 = (bf16[544,256]{1,0:T(8,128)(2,1)S(1)}, bf16[544,256]{1,0:T(8,128)(2,1)}, u32[]{:S(2)}) copy-start(bf16[544,256]{1,0:T(8,128)(2,1)} %constant.5.clone.short_in) | copy-start | bytes 835588
  15.5 0.9 %copy-start.4 = (f32[2,5,10,128]{3,2,1,0:T(8,128)S(1)}, f32[2,5,10,128]{3,2,1,0:T(8,128)}, u32[]{:S(2)}) copy-start(f32[2,5,10,128]{3,2,1,0:T(8,128)} %get-tuple-element.24.own_ref) | copy-start | bytes 153604
  15.5 0.9 %copy-start.5 = (bf16[5,10,384]{2,1,0:T(8,128)(2,1)S(1)}, bf16[5,10,384]{2,1,0:T(8,128)(2,1)}, u32[]{:S(2)}) copy-start(bf16[5,10,384]{2,1,0:T(8,128)(2,1)} %get-tuple-element.25.s_ref) | copy-start | bytes 115204
  15.5 0.9 %copy-start.6 = (f32[24,256]{1,0:T(8,128)S(1)}, f32[24,256]{1,0:T(8,128)}, u32[]{:S(2)}) copy-start(f32[24,256]{1,0:T(8,128)} %get-tuple-element.21.par_ref) | copy-start | bytes 73732
  25.5 22.1 %collective-permute-start.3 = (bf16[11,5120]{1,0:T(8,128)(2,1)S(1)}, bf16[11,5120]{1,0:T(8,128)(2,1)S(1)}, u32[]{:S(2)}, u32[]{:S(2)}) collective-permute-start(bf16[11,5120]{1,0:T(8,128)(2,1)S(1)} %get-tuple-element.33), channel_id=1, source_target_pairs={{0,32},{1,33},{2,34},{3,35},{4,36},{5,37},{6,38},{7,39},{8,40},{9,... | collective-permute-start | bytes 337928 | tf_op jit(solution)/shard_map/ppermute | solution.py:559
  30.4 29.9 %all-to-all-start = ((f32[256,1,32]{2,1,0:T(1,128)}), f32[256,1,32]{2,1,0:T(1,128)S(1)}, u32[]{:S(2)}, u32[]{:S(2)}) async-start(f32[256,1,32]{2,1,0:T(1,128)} %bitcast.6), calls=%async_computation | async-start | bytes 262144 | tf_op jit(solution)/shard_map/all_to_all | solution.py:641
  47.6 5.8 %collective-permute-start.4 = (bf16[6,5120]{1,0:T(8,128)(2,1)S(1)}, bf16[6,5120]{1,0:T(8,128)(2,1)S(1)}, u32[]{:S(2)}, u32[]{:S(2)}) collective-permute-start(bf16[6,5120]{1,0:T(8,128)(2,1)S(1)} %shard_map.160), channel_id=1, source_target_pairs={{0,1},{1,2},{2,3},{3,4},{4,5},{5,6},{6,7},{7,8},{8,9},{9,10},{10,1... | collective-permute-start | bytes 184328 | tf_op jit(solution)/shard_map/ppermute | solution.py:559

commit v5 on v4

--- a/solution.py
+++ b/solution.py
@@ -223,13 +223,9 @@
     c_ref[...] = wide[0:1, :].astype(BF16)
 
 
-def local_kernel(t_ref, tp_ref, wide_in, short_in, base_ref, copy_ref, wide_out, short_out):
+def local_kernel(wide_in, short_in, wide_out, short_out):
     wide_out[...] = wide_in[...]
     short_out[...] = short_in[...]
-    for x in range(NX):
-        now = t_ref[x]
-        copy_ref[x] = now
-        base_ref[x] = 2.0 * now.astype(F32) - tp_ref[x].astype(F32)
 
 
 def main_kernel(
@@ -237,7 +233,7 @@
     n_y,
     par_ref,
     t_ref,
-    base_ref,
+    tp_ref,
     own_ref,
     s_ref,
     hx_ref,
@@ -310,13 +306,13 @@
     primal_force = fdot(terms[0:ROWS, 128:256] + terms[ROWS : 2 * ROWS, 128:256], tab[384:512, 384:512])
 
     force[...] = jnp.zeros((ROWS, COLS), F32)
+    grad[...] = bdot(fwd, uc[...])
     lane = lax.broadcasted_iota(jnp.int32, (ROWS, 128), 1)
     row40 = lax.broadcasted_iota(jnp.int32, (40, 128), 0)
     half40 = lax.broadcasted_iota(jnp.int32, (40, 128), 1) // 64
 
     for i in range(5):
         odd = i % 2
-        grad[...] = bdot(fwd, uc[:, i * 1152 : (i + 1) * 1152])
         lam_rows, mu_rows = (
             jnp.where(
                 first_el,
@@ -338,14 +334,15 @@
                     pick[0],
                     jnp.where(row40 == target + 18, pick[1], 0.0),
                 )
-                stress[216:256, (c * 3 + m) * 128 : (c * 3 + m + 1) * 128] = value
-
-        def rows_step(rc, carry, odd=odd):
+                stress[i, 216:256, (c * 3 + m) * 128 : (c * 3 + m + 1) * 128] = value
+
+        def rows_step(rc, carry, odd=odd, i=i):
             row = pl.multiple_of(rc * 8, 8)
 
             def tile(kind, c, m):
                 at = pl.multiple_of(kind * PTS + rc * 8, 8)
-                return grad[pl.ds(at, 8), (c * 3 + m) * 128 : (c * 3 + m + 1) * 128]
+                lanes = i * 1152 + (c * 3 + m) * 128
+                return grad[pl.ds(at, 8), lanes : lanes + 128]
 
             def coef(index):
                 at = 256 + 128 * odd
@@ -353,7 +350,7 @@
 
             def put(direction, c, m, value):
                 at = pl.multiple_of(direction * PTS + rc * 8, 8)
-                stress[pl.ds(at, 8), (c * 3 + m) * 128 : (c * 3 + m + 1) * 128] = value
+                stress[i, pl.ds(at, 8), (c * 3 + m) * 128 : (c * 3 + m + 1) * 128] = value
 
             def along_z(tiles, offset):
                 turned = [pltpu.roll(v, 64, 1) for v in tiles]
@@ -394,8 +391,8 @@
             return carry
 
         lax.fori_loop(0, 9, rows_step, 0, unroll=UNROLL)
-        s_high = stress[...].astype(BF16)
-        s_low = (stress[0:216, :] - s_high[0:216].astype(F32)).astype(BF16)
+        s_high = stress[i].astype(BF16)
+        s_low = (stress[i, 0:216, :] - s_high[0:216].astype(F32)).astype(BF16)
         unit_here = jnp.where(
             lane < 106,
             pltpu.roll(unit_first, (88 - 18 * i) % 128, 1),
@@ -471,7 +468,7 @@
         force[:, at] = -r0 * force[:, at]
         for x in range(NX):
             rows = slice(16 * x, 16 * x + NY)
-            now = force[rows, at] + base_ref[x, :, at]
+            now = force[rows, at] + 2.0 * wide[rows, at] - tp_ref[x, :, at].astype(F32)
             force[rows, at] = now
             part_ref[x, :, at] = now
         high, low = split(force[:, at])
@@ -586,21 +583,19 @@
     halo_c = send(corner, -1, -1)
 
     wide_table, short_table = (jnp.asarray(a) for a in tab)
-    base, near, *near_tables = pl.pallas_call(
+    near_tables = pl.pallas_call(
         local_kernel,
         out_shape=(
-            jax.ShapeDtypeStruct((NX, NY, COLS), F32),
-            jax.ShapeDtypeStruct((NX, NY, COLS), BF16),
             jax.ShapeDtypeStruct(wide_table.shape, F32),
             jax.ShapeDtypeStruct(short_table.shape, BF16),
         ),
-        in_specs=[vmem] * 4,
-        out_specs=(vmem,) * 4,
+        in_specs=[vmem] * 2,
+        out_specs=(vmem,) * 2,
         compiler_params=params,
         cost_estimate=pl.CostEstimate(
             flops=4000000, bytes_accessed=8000000, transcendentals=0
         ),
-    )(tangent, tangent_prev, wide_table, short_table)
+    )(wide_table, short_table)
 
     part, ret_x, ret_y, shares = pl.pallas_call(
         functools.partial(main_kernel, nx_dev, ny_dev),
@@ -615,8 +610,8 @@
         scratch_shapes=[
             pltpu.VMEM((ROWS, WIDE), F32),
             pltpu.VMEM((2 * ROWS, 5 * 1152), BF16),
-            pltpu.VMEM((3 * PTS, 1152), F32),
-            pltpu.VMEM((256, 1152), F32),
+            pltpu.VMEM((3 * PTS, 5 * 1152), F32),
+            pltpu.VMEM((5, 256, 1152), F32),
             pltpu.VMEM((ROWS, COLS), F32),
             pltpu.VMEM((PTS, BACK), F32),
             pltpu.VMEM((PORTS, 64), F32),
@@ -627,8 +622,8 @@
         ),
     )(
         par,
-        near,
-        base,
+        tangent,
+        tangent_prev,
         own,
         small,
         halo_x,

time: 61.6 us -> 60.8 us (0.987)
  local copies, waits for them, and re-layouts: 5.23 us -> 2.51 us
  waiting for transfers between devices: 7.98 us -> 10.2 us
  Pallas kernels: 13.8 us -> 12.8 us
  starting transfers between devices: 33.5 us -> 34.2 us
    unnamed x14, local copies, waits for them, and re-layouts: 5.23 us -> 2.51 us
    ppermute x5, waiting for transfers between devices: 2.11 us -> 4.36 us  [send(): return lax.ppermute(block, ('gx', 'gy'), step(shift_x, shift_y))]
    all_to_all x1, starting transfers between devices: 17.2 us -> 18.5 us  [per_device(): shares = lax.all_to_all(shares, ('gx', 'gy'), 0, 0)]
    pallas_call x1, Pallas kernels: 9.1 us -> 8.31 us  [per_device(): pl.pallas_call(functools.partial(main_kernel, nx_dev, ny_dev), out_shape=...]
    ppermute x5, starting transfers between devices: 16.3 us -> 15.7 us  [send(): return lax.ppermute(block, ('gx', 'gy'), step(shift_x, shift_y))]
  transfers between devices with their start and end apart: 6 -> 6, of which waited for: 2 -> 3; matrix products, arithmetic and copies ran while one was open for 0% -> 0% of each run, Pallas kernels for 2% -> 2%
where the time goes in v5:
time: 60.8 us; the launch traced here: 60.5 us
  starting transfers between devices  34.2 us (56%)
  Pallas kernels  12.8 us (21%)
  waiting for transfers between devices  10.2 us (17%)
  local copies, waits for them, and re-layouts  2.51 us (4%)
  between operations  0.77 us (1%)
    all_to_all x1, starting transfers between devices, per_device(): shares = lax.all_to_all(shares, ('gx', 'gy'), 0, 0)  18.5 us
    ppermute x5, starting transfers between devices, send(): return lax.ppermute(block, ('gx', 'gy'), step(shift_x, shift_y))  15.7 us
    pallas_call x1, Pallas kernels, per_device(): pl.pallas_call(functools.partial(main_kernel, nx_dev, ny_dev), out_shape=...  8.31 us
    all_to_all x1, waiting for transfers between devices, per_device(): shares = lax.all_to_all(shares, ('gx', 'gy'), 0, 0)  5.86 us
    ppermute x5, waiting for transfers between devices, send(): return lax.ppermute(block, ('gx', 'gy'), step(shift_x, shift_y))  4.36 us
    unnamed x14, local copies, waits for them, and re-layouts  2.51 us
    pallas_call x1, Pallas kernels, per_device(): pl.pallas_call(pack_kernel, out_shape=(jax.ShapeDtypeStruct((NY, WIDE), B...  2.39 us
  transfers between devices with their start and end apart: 6, of which 3 were waited for; matrix products, arithmetic and copies ran while one was open for 0% of the time, Pallas kernels for 2%

profile of v5, /device:TPU:1, one launch (start us, length us, event | category | flops | bytes accessed | tf_op | source)
XLA Modules:
  0.0 60.5 jit_solution(3850355015564703869)
XLA Ops:
  0.6 0.0 copy-start
  0.6 2.4 %shard_map.157 = (bf16[10,5376]{1,0:T(8,128)(2,1)}, bf16[5,5376]{1,0:T(8,128)(2,1)}, bf16[1,5376]{1,0:T(2,128)(2,1)}, bf16[5,10,384]{2,1,0:T(8,128)(2,1)}, f32[2,5,10,128]{3,2,1,0:T(8,128)}, /*index=5*/f32[24,256]{1,0:T(8,128)}) custom-call(bf16[5,10,4992]{2,1,0:T(8,128)(2,1)} %t_ref.1, bf16[5,10,3,26]{3,2,1,0:T(4,128)(2,1)} %bitcast.11, ...), custom_call_target="tpu_custom_call" | custom-call | tf_op jit(solution)/shard_map/pallas_call | solution.py:561
  3.0 1.3 %collective-permute-start = (bf16[10,5376]{1,0:T(8,128)(2,1)}, bf16[10,5376]{1,0:T(8,128)(2,1)S(1)}, u32[]{:S(2)}, u32[]{:S(2)}) collective-permute-start(bf16[10,5376]{1,0:T(8,128)(2,1)} %get-tuple-element.22), channel_id=1, source_target_pairs={{32,0},{33,1},{34,2},{35,3},{36,4},{37,5},{38,6},{39,7},{40,8},{41... | collective-permute-start | bytes 322568 | tf_op jit(solution)/shard_map/ppermute | solution.py:556
  4.3 5.1 %collective-permute-start.1 = (bf16[5,5376]{1,0:T(8,128)(2,1)}, bf16[5,5376]{1,0:T(8,128)(2,1)S(1)}, u32[]{:S(2)}, u32[]{:S(2)}) collective-permute-start(bf16[5,5376]{1,0:T(8,128)(2,1)} %get-tuple-element.23), channel_id=1, source_target_pairs={{1,0},{2,1},{3,2},{4,3},{5,4},{6,5},{7,6},{8,7},{9,8},{10,9},{11,1... | collective-permute-start | bytes 161288 | tf_op jit(solution)/shard_map/ppermute | solution.py:556
  9.5 1.3 %collective-permute-start.2 = (bf16[1,5376]{1,0:T(2,128)(2,1)}, bf16[1,5376]{1,0:T(2,128)(2,1)S(1)}, u32[]{:S(2)}, u32[]{:S(2)}) collective-permute-start(bf16[1,5376]{1,0:T(2,128)(2,1)} %get-tuple-element.24), channel_id=1, source_target_pairs={{33,0},{34,1},{35,2},{36,3},{37,4},{38,5},{39,6},{40,7},{41,8},{42... | collective-permute-start | bytes 32264 | tf_op jit(solution)/shard_map/ppermute | solution.py:556
  10.8 0.0 copy-start.1
  10.8 1.5 %copy-done.1 = f32[952,512]{1,0:T(8,128)S(1)} copy-done((f32[952,512]{1,0:T(8,128)S(1)}, f32[952,512]{1,0:T(8,128)}, u32[]{:S(2)}) %copy-start.1) | copy-done | bytes 1949720
  12.3 0.0 copy-start.3
  12.3 1.0 %copy-done.3 = bf16[544,256]{1,0:T(8,128)(2,1)S(1)} copy-done((bf16[544,256]{1,0:T(8,128)(2,1)S(1)}, bf16[544,256]{1,0:T(8,128)(2,1)}, u32[]{:S(2)}) %copy-start.3) | copy-done | bytes 278552
  13.3 0.0 copy-start.2
  13.3 0.0 copy-start.4
  13.3 0.0 copy-start.5
  13.3 0.0 copy-start.6
  13.3 0.1 shard_map.158
  13.5 2.3 %collective-permute-done.2.hc_ref = bf16[1,5376]{1,0:T(2,128)(2,1)S(1)} collective-permute-done((bf16[1,5376]{1,0:T(2,128)(2,1)}, bf16[1,5376]{1,0:T(2,128)(2,1)S(1)}, u32[]{:S(2)}, u32[]{:S(2)}) %collective-permute-start.2) | collective-permute-done | bytes 10784 | tf_op jit(solution)/shard_map/ppermute | solution.py:556
  15.7 0.0 collective-permute-done.1.hy_ref
  15.7 0.0 collective-permute-done.hx_ref
  15.7 0.0 copy-done
  15.7 0.0 copy-done.2
  15.7 0.0 copy-done.4
  15.8 0.0 copy-done.5
  15.8 0.0 copy-done.6
  15.8 8.3 %shard_map.159 = (f32[5,10,5120]{2,1,0:T(8,128)S(1)}, bf16[11,5120]{1,0:T(8,128)(2,1)S(1)}, bf16[5,5120]{1,0:T(8,128)(2,1)S(1)}, f32[256,32]{1,0:T(8,128)}) custom-call(f32[24,256]{1,0:T(8,128)S(1)} %copy-done.6, bf16[5,10,4992]{2,1,0:T(8,128)(2,1)S(1)} %copy-done, bf16[5,10,4992]{2,1,0:T(8,128)(2,1)S(1)} %copy-done.2, f32[2,5,10,128]{3,2,1,0:T(8,128)S(1)} %copy-done.4, ...), custom_call_target="tpu_custom_call" | custom-call | flops 400000000 | bytes 8000000 | tf_op jit(solution)/shard_map/pallas_call | solution.py:600
  24.1 4.3 %collective-permute-start.3 = (bf16[11,5120]{1,0:T(8,128)(2,1)S(1)}, bf16[11,5120]{1,0:T(8,128)(2,1)S(1)}, u32[]{:S(2)}, u32[]{:S(2)}) collective-permute-start(bf16[11,5120]{1,0:T(8,128)(2,1)S(1)} %get-tuple-element.29), channel_id=1, source_target_pairs={{0,32},{1,33},{2,34},{3,35},{4,36},{5,37},{6,38},{7,39},{8,40},{9,... | collective-permute-start | bytes 337928 | tf_op jit(solution)/shard_map/ppermute | solution.py:556
  28.3 18.5 %all-to-all-start = ((f32[256,1,32]{2,1,0:T(1,128)}), f32[256,1,32]{2,1,0:T(1,128)S(1)}, u32[]{:S(2)}, u32[]{:S(2)}) async-start(f32[256,1,32]{2,1,0:T(1,128)} %bitcast.6), calls=%async_computation | async-start | bytes 262144 | tf_op jit(solution)/shard_map/all_to_all | solution.py:636
  46.9 0.0 collective-permute-done.3.rx_ref
  46.9 3.7 %collective-permute-start.4 = (bf16[6,5120]{1,0:T(8,128)(2,1)S(1)}, bf16[6,5120]{1,0:T(8,128)(2,1)S(1)}, u32[]{:S(2)}, u32[]{:S(2)}) collective-permute-start(bf16[6,5120]{1,0:T(8,128)(2,1)S(1)} %shard_map.160), channel_id=1, source_target_pairs={{0,1},{1,2},{2,3},{3,4},{4,5},{5,6},{6,7},{7,8},{8,9},{9,10},{10,1... | collective-permute-start | bytes 184328 | tf_op jit(solution)/shard_map/ppermute | solution.py:556
  50.6 2.1 %collective-permute-done.4.ry_ref = bf16[6,5120]{1,0:T(8,128)(2,1)S(1)} collective-permute-done((bf16[6,5120]{1,0:T(8,128)(2,1)S(1)}, bf16[6,5120]{1,0:T(8,128)(2,1)S(1)}, u32[]{:S(2)}, u32[]{:S(2)}) %collective-permute-start.4) | collective-permute-done | bytes 61472 | tf_op jit(solution)/shard_map/ppermute | solution.py:556
  52.7 1.1 %shard_map.161 = (bf16[5,10,4992]{2,1,0:T(8,128)(2,1)}, f32[5,10,128]{2,1,0:T(8,128)S(1)}) custom-call(f32[5,10,5120]{2,1,0:T(8,128)S(1)} %get-tuple-element.28.part_ref, bf16[11,5120]{1,0:T(8,128)(2,1)S(1)} %collective-permute-done.3.rx_ref, bf16[6,5120]{1,0:T(8,128)(2,1)S(1)} %collective-permute-done.4.ry_ref), custom_call_target="tpu_custom_call" | custom-call | flops 4000000 | bytes 8000000 | tf_op jit(solution)/shard_map/pallas_call | solution.py:649
  53.8 5.9 %all-to-all-done = f32[256,1,32]{2,1,0:T(1,128)S(1)} async-done(((f32[256,1,32]{2,1,0:T(1,128)}), f32[256,1,32]{2,1,0:T(1,128)S(1)}, u32[]{:S(2)}, u32[]{:S(2)}) %all-to-all-start) | async-done | bytes 32800 | tf_op jit(solution)/shard_map/all_to_all | solution.py:636
  59.6 0.8 %shard_map.162 = (f32[2,8]{1,0:T(2,128)}, bf16[5,10,3,26]{3,2,1,0:T(4,128)(2,1)}) custom-call(f32[256,32]{1,0:T(8,128)S(1)} %bitcast.10, f32[5,10,128]{2,1,0:T(8,128)S(1)} %get-tuple-element.31.d_ref), custom_call_target="tpu_custom_call" | custom-call | tf_op jit(solution)/shard_map/pallas_call | solution.py:660
  (1 shorter events, 0.0 us)
Async XLA Ops:
  0.6 15.1 %copy-start = (bf16[5,10,4992]{2,1,0:T(8,128)(2,1)S(1)}, bf16[5,10,4992]{2,1,0:T(8,128)(2,1)}, u32[]{:S(2)}) copy-start(bf16[5,10,4992]{2,1,0:T(8,128)(2,1)} %t_ref.1) | copy-start | bytes 1497604
  3.0 12.7 %collective-permute-start = (bf16[10,5376]{1,0:T(8,128)(2,1)}, bf16[10,5376]{1,0:T(8,128)(2,1)S(1)}, u32[]{:S(2)}, u32[]{:S(2)}) collective-permute-start(bf16[10,5376]{1,0:T(8,128)(2,1)} %get-tuple-element.22), channel_id=1, source_target_pairs={{32,0},{33,1},{34,2},{35,3},{36,4},{37,5},{38,6},{39,7},{40,8},{41... | collective-permute-start | bytes 322568 | tf_op jit(solution)/shard_map/ppermute | solution.py:556
  4.3 11.4 %collective-permute-start.1 = (bf16[5,5376]{1,0:T(8,128)(2,1)}, bf16[5,5376]{1,0:T(8,128)(2,1)S(1)}, u32[]{:S(2)}, u32[]{:S(2)}) collective-permute-start(bf16[5,5376]{1,0:T(8,128)(2,1)} %get-tuple-element.23), channel_id=1, source_target_pairs={{1,0},{2,1},{3,2},{4,3},{5,4},{6,5},{7,6},{8,7},{9,8},{10,9},{11,1... | collective-permute-start | bytes 161288 | tf_op jit(solution)/shard_map/ppermute | solution.py:556
  9.5 6.2 %collective-permute-start.2 = (bf16[1,5376]{1,0:T(2,128)(2,1)}, bf16[1,5376]{1,0:T(2,128)(2,1)S(1)}, u32[]{:S(2)}, u32[]{:S(2)}) collective-permute-start(bf16[1,5376]{1,0:T(2,128)(2,1)} %get-tuple-element.24), channel_id=1, source_target_pairs={{33,0},{34,1},{35,2},{36,3},{37,4},{38,5},{39,6},{40,7},{41,8},{42... | collective-permute-start | bytes 32264 | tf_op jit(solution)/shard_map/ppermute | solution.py:556
  10.8 1.5 %copy-start.1 = (f32[952,512]{1,0:T(8,128)S(1)}, f32[952,512]{1,0:T(8,128)}, u32[]{:S(2)}) copy-start(f32[952,512]{1,0:T(8,128)} %constant.4.clone.wide_in) | copy-start | bytes 5849092
  12.3 1.0 %copy-start.3 = (bf16[544,256]{1,0:T(8,128)(2,1)S(1)}, bf16[544,256]{1,0:T(8,128)(2,1)}, u32[]{:S(2)}) copy-start(bf16[544,256]{1,0:T(8,128)(2,1)} %constant.5.clone.short_in) | copy-start | bytes 835588
  13.3 2.4 %copy-start.2 = (bf16[5,10,4992]{2,1,0:T(8,128)(2,1)S(1)}, bf16[5,10,4992]{2,1,0:T(8,128)(2,1)}, u32[]{:S(2)}) copy-start(bf16[5,10,4992]{2,1,0:T(8,128)(2,1)} %tp_ref.1) | copy-start | bytes 1497604
  13.3 2.4 %copy-start.4 = (f32[2,5,10,128]{3,2,1,0:T(8,128)S(1)}, f32[2,5,10,128]{3,2,1,0:T(8,128)}, u32[]{:S(2)}) copy-start(f32[2,5,10,128]{3,2,1,0:T(8,128)} %get-tuple-element.20.own_ref) | copy-start | bytes 153604
  13.3 2.5 %copy-start.5 = (bf16[5,10,384]{2,1,0:T(8,128)(2,1)S(1)}, bf16[5,10,384]{2,1,0:T(8,128)(2,1)}, u32[]{:S(2)}) copy-start(bf16[5,10,384]{2,1,0:T(8,128)(2,1)} %get-tuple-element.21.s_ref) | copy-start | bytes 115204
  13.3 2.5 %copy-start.6 = (f32[24,256]{1,0:T(8,128)S(1)}, f32[24,256]{1,0:T(8,128)}, u32[]{:S(2)}) copy-start(f32[24,256]{1,0:T(8,128)} %get-tuple-element.19.par_ref) | copy-start | bytes 73732
  24.1 22.8 %collective-permute-start.3 = (bf16[11,5120]{1,0:T(8,128)(2,1)S(1)}, bf16[11,5120]{1,0:T(8,128)(2,1)S(1)}, u32[]{:S(2)}, u32[]{:S(2)}) collective-permute-start(bf16[11,5120]{1,0:T(8,128)(2,1)S(1)} %get-tuple-element.29), channel_id=1, source_target_pairs={{0,32},{1,33},{2,34},{3,35},{4,36},{5,37},{6,38},{7,39},{8,40},{9,... | collective-permute-start | bytes 337928 | tf_op jit(solution)/shard_map/ppermute | solution.py:556
  28.3 31.3 %all-to-all-start = ((f32[256,1,32]{2,1,0:T(1,128)}), f32[256,1,32]{2,1,0:T(1,128)S(1)}, u32[]{:S(2)}, u32[]{:S(2)}) async-start(f32[256,1,32]{2,1,0:T(1,128)} %bitcast.6), calls=%async_computation | async-start | bytes 262144 | tf_op jit(solution)/shard_map/all_to_all | solution.py:636
  46.9 5.8 %collective-permute-start.4 = (bf16[6,5120]{1,0:T(8,128)(2,1)S(1)}, bf16[6,5120]{1,0:T(8,128)(2,1)S(1)}, u32[]{:S(2)}, u32[]{:S(2)}) collective-permute-start(bf16[6,5120]{1,0:T(8,128)(2,1)S(1)} %shard_map.160), channel_id=1, source_target_pairs={{0,1},{1,2},{2,3},{3,4},{4,5},{5,6},{6,7},{7,8},{8,9},{9,10},{10,1... | collective-permute-start | bytes 184328 | tf_op jit(solution)/shard_map/ppermute | solution.py:556

commit v6 on v5

--- a/solution.py
+++ b/solution.py
@@ -135,18 +135,17 @@
                 spread[piece * 32 + k, c * 32 + k] = 1.0
     of_first = np.tile(np.arange(PTS) < 36, 3)[None, :]
     back_el = np.concatenate([backward * of_first, backward * ~of_first], axis=0)
-    wide = np.zeros((952, 512), np.float32)
+    wide = np.zeros((1168, 512), np.float32)
     wide[0:384] = to_sym.reshape(384, 512)
     wide[384:640, 0:384] = from_sym
     wide[384:512, 384:512] = merge
     wide[640:832, 0:216] = back_el
     wide[640:952, 256:384] = coef[0:39].reshape(312, 128)
     wide[640:952, 384:512] = coef[39:78].reshape(312, 128)
-    short = np.zeros((544, 256), ml_dtypes.bfloat16)
-    short[0:216, 0:192] = forward2
-    short[224:416, 0:216] = backward2
-    short[416:544, 0:128] = spread
-    return wide, short
+    wide[952:1168, 0:192] = forward2.astype(np.float32)
+    wide[952:1144, 256:472] = backward2.astype(np.float32)
+    wide[512:640, 384:512] = spread
+    return wide
 
 
 def fdot(a, b):
@@ -223,9 +222,8 @@
     c_ref[...] = wide[0:1, :].astype(BF16)
 
 
-def local_kernel(wide_in, short_in, wide_out, short_out):
+def local_kernel(wide_in, wide_out):
     wide_out[...] = wide_in[...]
-    short_out[...] = short_in[...]
 
 
 def main_kernel(
@@ -241,9 +239,9 @@
     hc_ref,
     *rest,
 ):
-    tab, short = rest[0:2]
-    part_ref, rx_ref, ry_ref, share_ref = rest[2:6]
-    (wide, uc, grad, stress, force, edge, amp) = rest[6:]
+    tab = rest[0]
+    part_ref, rx_ref, ry_ref, share_ref = rest[1:5]
+    (wide, uc, grad, stress, force, edge, amp) = rest[5:]
 
     for x in range(NX):
         wide[16 * x + 8 : 16 * x + 16, :] = jnp.zeros((8, WIDE), F32)
@@ -285,8 +283,8 @@
                 uc[0:ROWS, at : at + 128] = value
                 uc[ROWS : 2 * ROWS, at : at + 128] = value
 
-    fwd = short[0:216, 0:192]
-    bwd = short[224:416, :]
+    fwd = tab[952:1168, 0:192].astype(BF16)
+    bwd = tab[952:1144, 256:512].astype(BF16)
 
     small_nodes = wide[:, COLS : COLS + 128].astype(BF16)
     pg = bdot(fwd, jnp.concatenate([small_nodes, small_nodes], axis=0))
@@ -438,7 +436,7 @@
         if odd:
             add(9, jnp.where(low_rows, last_c2, zero))
 
-    mass = bdot(wide[:, COLS + 256 : COLS + 384].astype(BF16), short[416:544, 0:128])
+    mass = bdot(wide[:, COLS + 256 : COLS + 384].astype(BF16), tab[512:640, 384:512].astype(BF16))
     rate = STEP_SQUARED / jnp.where(mass > 0.0, mass, 1.0)
     primal_step = -rate * primal_force
     for x in range(NX):
@@ -582,20 +580,17 @@
     halo_y = send(face_y, 0, -1)
     halo_c = send(corner, -1, -1)
 
-    wide_table, short_table = (jnp.asarray(a) for a in tab)
-    near_tables = pl.pallas_call(
+    wide_table = jnp.asarray(tab)
+    near_table = pl.pallas_call(
         local_kernel,
-        out_shape=(
-            jax.ShapeDtypeStruct(wide_table.shape, F32),
-            jax.ShapeDtypeStruct(short_table.shape, BF16),
-        ),
-        in_specs=[vmem] * 2,
-        out_specs=(vmem,) * 2,
+        out_shape=jax.ShapeDtypeStruct(wide_table.shape, F32),
+        in_specs=[vmem],
+        out_specs=vmem,
         compiler_params=params,
         cost_estimate=pl.CostEstimate(
             flops=4000000, bytes_accessed=8000000, transcendentals=0
         ),
-    )(wide_table, short_table)
+    )(wide_table)
 
     part, ret_x, ret_y, shares = pl.pallas_call(
         functools.partial(main_kernel, nx_dev, ny_dev),
@@ -605,7 +600,7 @@
             jax.ShapeDtypeStruct((NX, BACK), BF16),
             jax.ShapeDtypeStruct((nx_dev * ny_dev, share_lanes), F32),
         ),
-        in_specs=[vmem] * 10,
+        in_specs=[vmem] * 9,
         out_specs=(vmem,) * 4,
         scratch_shapes=[
             pltpu.VMEM((ROWS, WIDE), F32),
@@ -629,7 +624,7 @@
         halo_x,
         halo_y,
         halo_c,
-        *near_tables,
+        near_table,
     )
 
     port_rows, port_cols = PORTS // ny_dev, 64 // nx_dev

time: 60.8 us -> 60.9 us (level)
  waiting for transfers between devices: 10.2 us -> 11.1 us
  local copies, waits for them, and re-layouts: 2.51 us -> 1.69 us
    ppermute x5, waiting for transfers between devices: 4.36 us -> 5.21 us  [send(): return lax.ppermute(block, ('gx', 'gy'), step(shift_x, shift_y))]
    unnamed x14 -> x12, local copies, waits for them, and re-layouts: 2.51 us -> 1.69 us
where the time goes in v6:
time: 60.9 us; the launch traced here: 60.5 us
  starting transfers between devices  34.3 us (56%)
  Pallas kernels  12.7 us (21%)
  waiting for transfers between devices  11.1 us (18%)
  local copies, waits for them, and re-layouts  1.69 us (3%)
  between operations  0.77 us (1%)
    all_to_all x1, starting transfers between devices, per_device(): shares = lax.all_to_all(shares, ('gx', 'gy'), 0, 0)  18.5 us
    ppermute x5, starting transfers between devices, send(): return lax.ppermute(block, ('gx', 'gy'), step(shift_x, shift_y))  15.8 us
    pallas_call x1, Pallas kernels, per_device(): pl.pallas_call(functools.partial(main_kernel, nx_dev, ny_dev), out_shape=...  8.31 us
    all_to_all x1, waiting for transfers between devices, per_device(): shares = lax.all_to_all(shares, ('gx', 'gy'), 0, 0)  5.85 us
    ppermute x5, waiting for transfers between devices, send(): return lax.ppermute(block, ('gx', 'gy'), step(shift_x, shift_y))  5.21 us
    pallas_call x1, Pallas kernels, per_device(): pl.pallas_call(pack_kernel, out_shape=(jax.ShapeDtypeStruct((NY, WIDE), B...  2.31 us
    unnamed x12, local copies, waits for them, and re-layouts  1.69 us
  transfers between devices with their start and end apart: 6, of which 3 were waited for; matrix products, arithmetic and copies ran while one was open for 0% of the time, Pallas kernels for 2%

profile of v6, /device:TPU:1, one launch (start us, length us, event | category | flops | bytes accessed | tf_op | source)
XLA Modules:
  0.0 60.5 jit_solution(16793507894333830472)
XLA Ops:
  0.6 2.3 %shard_map.148 = (bf16[10,5376]{1,0:T(8,128)(2,1)}, bf16[5,5376]{1,0:T(8,128)(2,1)}, bf16[1,5376]{1,0:T(2,128)(2,1)}, bf16[5,10,384]{2,1,0:T(8,128)(2,1)}, f32[2,5,10,128]{3,2,1,0:T(8,128)}, /*index=5*/f32[24,256]{1,0:T(8,128)}) custom-call(bf16[5,10,4992]{2,1,0:T(8,128)(2,1)} %t_ref.1, bf16[5,10,3,26]{3,2,1,0:T(4,128)(2,1)} %bitcast.11, ...), custom_call_target="tpu_custom_call" | custom-call | tf_op jit(solution)/shard_map/pallas_call | solution.py:559
  3.0 1.3 %collective-permute-start = (bf16[10,5376]{1,0:T(8,128)(2,1)}, bf16[10,5376]{1,0:T(8,128)(2,1)S(1)}, u32[]{:S(2)}, u32[]{:S(2)}) collective-permute-start(bf16[10,5376]{1,0:T(8,128)(2,1)} %get-tuple-element.20), channel_id=1, source_target_pairs={{32,0},{33,1},{34,2},{35,3},{36,4},{37,5},{38,6},{39,7},{40,8},{41... | collective-permute-start | bytes 322568 | tf_op jit(solution)/shard_map/ppermute | solution.py:554
  4.3 5.1 %collective-permute-start.1 = (bf16[5,5376]{1,0:T(8,128)(2,1)}, bf16[5,5376]{1,0:T(8,128)(2,1)S(1)}, u32[]{:S(2)}, u32[]{:S(2)}) collective-permute-start(bf16[5,5376]{1,0:T(8,128)(2,1)} %get-tuple-element.21), channel_id=1, source_target_pairs={{1,0},{2,1},{3,2},{4,3},{5,4},{6,5},{7,6},{8,7},{9,8},{10,9},{11,1... | collective-permute-start | bytes 161288 | tf_op jit(solution)/shard_map/ppermute | solution.py:554
  9.4 0.0 copy-start
  9.4 1.4 %collective-permute-start.2 = (bf16[1,5376]{1,0:T(2,128)(2,1)}, bf16[1,5376]{1,0:T(2,128)(2,1)S(1)}, u32[]{:S(2)}, u32[]{:S(2)}) collective-permute-start(bf16[1,5376]{1,0:T(2,128)(2,1)} %get-tuple-element.22), channel_id=1, source_target_pairs={{33,0},{34,1},{35,2},{36,3},{37,4},{38,5},{39,6},{40,7},{41,8},{42... | collective-permute-start | bytes 32264 | tf_op jit(solution)/shard_map/ppermute | solution.py:554
  10.9 0.0 copy-start.1
  10.9 1.7 %copy-done.1 = f32[1168,512]{1,0:T(8,128)S(1)} copy-done((f32[1168,512]{1,0:T(8,128)S(1)}, f32[1168,512]{1,0:T(8,128)}, u32[]{:S(2)}) %copy-start.1) | copy-done | bytes 2392088
  12.5 0.0 copy-start.2
  12.5 0.0 copy-start.3
  12.5 0.0 copy-start.4
  12.5 0.0 copy-start.5
  12.5 0.2 shard_map.149.rest_0_
  12.7 3.1 %collective-permute-done.2.hc_ref = bf16[1,5376]{1,0:T(2,128)(2,1)S(1)} collective-permute-done((bf16[1,5376]{1,0:T(2,128)(2,1)}, bf16[1,5376]{1,0:T(2,128)(2,1)S(1)}, u32[]{:S(2)}, u32[]{:S(2)}) %collective-permute-start.2) | collective-permute-done | bytes 10784 | tf_op jit(solution)/shard_map/ppermute | solution.py:554
  15.8 0.0 collective-permute-done.1.hy_ref
  15.8 0.0 collective-permute-done.hx_ref
  15.8 0.0 copy-done
  15.8 0.0 copy-done.2
  15.8 0.0 copy-done.3
  15.8 0.0 copy-done.4
  15.8 0.0 copy-done.5
  15.8 8.3 %shard_map.150 = (f32[5,10,5120]{2,1,0:T(8,128)S(1)}, bf16[11,5120]{1,0:T(8,128)(2,1)S(1)}, bf16[5,5120]{1,0:T(8,128)(2,1)S(1)}, f32[256,32]{1,0:T(8,128)}) custom-call(f32[24,256]{1,0:T(8,128)S(1)} %copy-done.5, bf16[5,10,4992]{2,1,0:T(8,128)(2,1)S(1)} %copy-done, bf16[5,10,4992]{2,1,0:T(8,128)(2,1)S(1)} %copy-done.2, f32[2,5,10,128]{3,2,1,0:T(8,128)S(1)} %copy-done.3, ...), custom_call_target="tpu_custom_call" | custom-call | flops 400000000 | bytes 8000000 | tf_op jit(solution)/shard_map/pallas_call | solution.py:595
  24.1 4.3 %collective-permute-start.3 = (bf16[11,5120]{1,0:T(8,128)(2,1)S(1)}, bf16[11,5120]{1,0:T(8,128)(2,1)S(1)}, u32[]{:S(2)}, u32[]{:S(2)}) collective-permute-start(bf16[11,5120]{1,0:T(8,128)(2,1)S(1)} %get-tuple-element.25), channel_id=1, source_target_pairs={{0,32},{1,33},{2,34},{3,35},{4,36},{5,37},{6,38},{7,39},{8,40},{9,... | collective-permute-start | bytes 337928 | tf_op jit(solution)/shard_map/ppermute | solution.py:554
  28.4 18.5 %all-to-all-start = ((f32[256,1,32]{2,1,0:T(1,128)}), f32[256,1,32]{2,1,0:T(1,128)S(1)}, u32[]{:S(2)}, u32[]{:S(2)}) async-start(f32[256,1,32]{2,1,0:T(1,128)} %bitcast.6), calls=%async_computation | async-start | bytes 262144 | tf_op jit(solution)/shard_map/all_to_all | solution.py:631
  46.9 0.0 collective-permute-done.3.rx_ref
  47.0 3.7 %collective-permute-start.4 = (bf16[6,5120]{1,0:T(8,128)(2,1)S(1)}, bf16[6,5120]{1,0:T(8,128)(2,1)S(1)}, u32[]{:S(2)}, u32[]{:S(2)}) collective-permute-start(bf16[6,5120]{1,0:T(8,128)(2,1)S(1)} %shard_map.151), channel_id=1, source_target_pairs={{0,1},{1,2},{2,3},{3,4},{4,5},{5,6},{6,7},{7,8},{8,9},{9,10},{10,1... | collective-permute-start | bytes 184328 | tf_op jit(solution)/shard_map/ppermute | solution.py:554
  50.7 2.1 %collective-permute-done.4.ry_ref = bf16[6,5120]{1,0:T(8,128)(2,1)S(1)} collective-permute-done((bf16[6,5120]{1,0:T(8,128)(2,1)S(1)}, bf16[6,5120]{1,0:T(8,128)(2,1)S(1)}, u32[]{:S(2)}, u32[]{:S(2)}) %collective-permute-start.4) | collective-permute-done | bytes 61472 | tf_op jit(solution)/shard_map/ppermute | solution.py:554
  52.8 1.1 %shard_map.152 = (bf16[5,10,4992]{2,1,0:T(8,128)(2,1)}, f32[5,10,128]{2,1,0:T(8,128)S(1)}) custom-call(f32[5,10,5120]{2,1,0:T(8,128)S(1)} %get-tuple-element.24.part_ref, bf16[11,5120]{1,0:T(8,128)(2,1)S(1)} %collective-permute-done.3.rx_ref, bf16[6,5120]{1,0:T(8,128)(2,1)S(1)} %collective-permute-done.4.ry_ref), custom_call_target="tpu_custom_call" | custom-call | flops 4000000 | bytes 8000000 | tf_op jit(solution)/shard_map/pallas_call | solution.py:644
  53.9 5.8 %all-to-all-done = f32[256,1,32]{2,1,0:T(1,128)S(1)} async-done(((f32[256,1,32]{2,1,0:T(1,128)}), f32[256,1,32]{2,1,0:T(1,128)S(1)}, u32[]{:S(2)}, u32[]{:S(2)}) %all-to-all-start) | async-done | bytes 32800 | tf_op jit(solution)/shard_map/all_to_all | solution.py:631
  59.7 0.8 %shard_map.153 = (f32[2,8]{1,0:T(2,128)}, bf16[5,10,3,26]{3,2,1,0:T(4,128)(2,1)}) custom-call(f32[256,32]{1,0:T(8,128)S(1)} %bitcast.10, f32[5,10,128]{2,1,0:T(8,128)S(1)} %get-tuple-element.27.d_ref), custom_call_target="tpu_custom_call" | custom-call | tf_op jit(solution)/shard_map/pallas_call | solution.py:655
  (1 shorter events, 0.0 us)
Async XLA Ops:
  3.0 12.8 %collective-permute-start = (bf16[10,5376]{1,0:T(8,128)(2,1)}, bf16[10,5376]{1,0:T(8,128)(2,1)S(1)}, u32[]{:S(2)}, u32[]{:S(2)}) collective-permute-start(bf16[10,5376]{1,0:T(8,128)(2,1)} %get-tuple-element.20), channel_id=1, source_target_pairs={{32,0},{33,1},{34,2},{35,3},{36,4},{37,5},{38,6},{39,7},{40,8},{41... | collective-permute-start | bytes 322568 | tf_op jit(solution)/shard_map/ppermute | solution.py:554
  4.3 11.5 %collective-permute-start.1 = (bf16[5,5376]{1,0:T(8,128)(2,1)}, bf16[5,5376]{1,0:T(8,128)(2,1)S(1)}, u32[]{:S(2)}, u32[]{:S(2)}) collective-permute-start(bf16[5,5376]{1,0:T(8,128)(2,1)} %get-tuple-element.21), channel_id=1, source_target_pairs={{1,0},{2,1},{3,2},{4,3},{5,4},{6,5},{7,6},{8,7},{9,8},{10,9},{11,1... | collective-permute-start | bytes 161288 | tf_op jit(solution)/shard_map/ppermute | solution.py:554
  9.4 6.4 %copy-start = (bf16[5,10,4992]{2,1,0:T(8,128)(2,1)S(1)}, bf16[5,10,4992]{2,1,0:T(8,128)(2,1)}, u32[]{:S(2)}) copy-start(bf16[5,10,4992]{2,1,0:T(8,128)(2,1)} %t_ref.1) | copy-start | bytes 1497604
  9.4 6.4 %collective-permute-start.2 = (bf16[1,5376]{1,0:T(2,128)(2,1)}, bf16[1,5376]{1,0:T(2,128)(2,1)S(1)}, u32[]{:S(2)}, u32[]{:S(2)}) collective-permute-start(bf16[1,5376]{1,0:T(2,128)(2,1)} %get-tuple-element.22), channel_id=1, source_target_pairs={{33,0},{34,1},{35,2},{36,3},{37,4},{38,5},{39,6},{40,7},{41,8},{42... | collective-permute-start | bytes 32264 | tf_op jit(solution)/shard_map/ppermute | solution.py:554
  10.9 1.7 %copy-start.1 = (f32[1168,512]{1,0:T(8,128)S(1)}, f32[1168,512]{1,0:T(8,128)}, u32[]{:S(2)}) copy-start(f32[1168,512]{1,0:T(8,128)} %constant.2.clone.wide_in) | copy-start | bytes 7176196
  12.5 3.3 %copy-start.2 = (bf16[5,10,4992]{2,1,0:T(8,128)(2,1)S(1)}, bf16[5,10,4992]{2,1,0:T(8,128)(2,1)}, u32[]{:S(2)}) copy-start(bf16[5,10,4992]{2,1,0:T(8,128)(2,1)} %tp_ref.1) | copy-start | bytes 1497604
  12.5 3.3 %copy-start.3 = (f32[2,5,10,128]{3,2,1,0:T(8,128)S(1)}, f32[2,5,10,128]{3,2,1,0:T(8,128)}, u32[]{:S(2)}) copy-start(f32[2,5,10,128]{3,2,1,0:T(8,128)} %get-tuple-element.18.own_ref) | copy-start | bytes 153604
  12.5 3.3 %copy-start.4 = (bf16[5,10,384]{2,1,0:T(8,128)(2,1)S(1)}, bf16[5,10,384]{2,1,0:T(8,128)(2,1)}, u32[]{:S(2)}) copy-start(bf16[5,10,384]{2,1,0:T(8,128)(2,1)} %get-tuple-element.19.s_ref) | copy-start | bytes 115204
  12.5 3.3 %copy-start.5 = (f32[24,256]{1,0:T(8,128)S(1)}, f32[24,256]{1,0:T(8,128)}, u32[]{:S(2)}) copy-start(f32[24,256]{1,0:T(8,128)} %get-tuple-element.17.par_ref) | copy-start | bytes 73732
  24.1 22.8 %collective-permute-start.3 = (bf16[11,5120]{1,0:T(8,128)(2,1)S(1)}, bf16[11,5120]{1,0:T(8,128)(2,1)S(1)}, u32[]{:S(2)}, u32[]{:S(2)}) collective-permute-start(bf16[11,5120]{1,0:T(8,128)(2,1)S(1)} %get-tuple-element.25), channel_id=1, source_target_pairs={{0,32},{1,33},{2,34},{3,35},{4,36},{5,37},{6,38},{7,39},{8,40},{9,... | collective-permute-start | bytes 337928 | tf_op jit(solution)/shard_map/ppermute | solution.py:554
  28.4 31.3 %all-to-all-start = ((f32[256,1,32]{2,1,0:T(1,128)}), f32[256,1,32]{2,1,0:T(1,128)S(1)}, u32[]{:S(2)}, u32[]{:S(2)}) async-start(f32[256,1,32]{2,1,0:T(1,128)} %bitcast.6), calls=%async_computation | async-start | bytes 262144 | tf_op jit(solution)/shard_map/all_to_all | solution.py:631
  47.0 5.8 %collective-permute-start.4 = (bf16[6,5120]{1,0:T(8,128)(2,1)S(1)}, bf16[6,5120]{1,0:T(8,128)(2,1)S(1)}, u32[]{:S(2)}, u32[]{:S(2)}) collective-permute-start(bf16[6,5120]{1,0:T(8,128)(2,1)S(1)} %shard_map.151), channel_id=1, source_target_pairs={{0,1},{1,2},{2,3},{3,4},{4,5},{5,6},{6,7},{7,8},{8,9},{9,10},{10,1... | collective-permute-start | bytes 184328 | tf_op jit(solution)/shard_map/ppermute | solution.py:554
